TPU v7x, 128 devices: a whole 4x4x4 slice. The times are simulated.
128 devices in a mesh: tile: 4 (over x), tm: 16 (over y, z), mode: 2 (over core).
Axes of the slice: x: 4, y: 4, z: 4, core: 2. Of those that a mesh axis runs over, the one named last changes fastest.
Arguments:
- object_field: float32 [2, 1056, 4096], P(None, 'tile', 'tm'), may hold values from -4 to 4
- probe_modes: float32 [4, 2, 256, 256], P('mode'), may hold values from -3 to 3
- amplitudes: float32 [128, 256, 256], P(('tile', 'tm')), may hold values from 0.3 to 2.5
- anchors: int32 [128, 1], P(('tile', 'tm')), may hold values from 0 to 14, as said below
- row_offset: int32 [128], P(('tile', 'tm')), may hold values from 0 to 8
- col_offset: int32 [128], P(('tile', 'tm')), may hold values from 0 to 255
- live_counts: int32 [64], P(('tile', 'tm')), may hold values from 1 to 2, as said below
Outputs:
- object_out: float32 [2, 1056, 4096], P(None, 'tile', 'tm')
- probe_out: float32 [4, 2, 256, 256], P('mode')
Inputs may be any that keep to these rules, and one draw needn't show every extreme that they name: The first position of group d has anchor min((d % 16 + 16 // 2) % 16, 14); the other positions' anchors may be any tile of the band up to 14. `live_counts`: some group has all 2 positions live.
All inputs are finite; a program needn't handle non-finite values.
Results may differ from a plain program's by a relative error of at most 0.0033.
Values may be sent and summed in bfloat16 or wider, within the bound.
No kernel may reach another device: no remote copies, remote signals or barrier semaphores. Data moves between devices by JAX's collectives and lax.ppermute only.
A program may use at most 128 MiB of HBM per device.

v0:
```python
import functools

import jax
import jax.numpy as jnp
import ml_dtypes
import numpy as np
from jax import lax
from jax.experimental import pallas as pl
from jax.experimental.pallas import tpu as pltpu
from jax.sharding import PartitionSpec as P

PS = 256
HALF = 128
PARTS = 1
BH = 264
N_TM = 16
UNROLL = 8
CH = 16
HALO = 24
FLOOR_VALUE = 0.5
OBJECT_REG = 1.0
PROBE_REG = 1.0
F32 = jnp.float32
BF16 = jnp.bfloat16
SWAP = [(0, 1), (1, 0)]

VM = pl.BlockSpec(memory_space=pltpu.VMEM)
SM = pl.BlockSpec(memory_space=pltpu.SMEM)


def real_form(matrix):
    return np.block([[matrix.real, -matrix.imag], [matrix.imag, matrix.real]]).astype(np.float32)


def halves(table):
    high = table.astype(ml_dtypes.bfloat16)
    return high, (table - high.astype(np.float32)).astype(ml_dtypes.bfloat16)


def dft_tables():
    n = np.arange(HALF)
    left, right = [], []
    for k in (2 * n, 2 * n + 1):
        table = real_form(np.exp(-2j * np.pi * ((k[:, None] * n[None, :]) % PS) / PS) / np.sqrt(PS))
        for form in (table, np.ascontiguousarray(table.T)):
            high, low = halves(form)
            left.append(np.concatenate([high, low][:PARTS], axis=1))
            right.append(np.concatenate([high, low][:PARTS], axis=0))
    return left + right


def order_table():
    picked = np.concatenate([np.arange(0, PS, 2), np.arange(1, PS, 2)])
    table = np.zeros((PS, PS), np.float32)
    table[np.arange(PS), picked] = 1.0
    return table.astype(ml_dtypes.bfloat16)


def call(kernel, out_shape, in_specs, scratch=(), flops=0, nbytes=1 << 20, vmem=12):
    many = isinstance(out_shape, (tuple, list))
    return pl.pallas_call(
        kernel,
        out_shape=out_shape,
        in_specs=in_specs,
        out_specs=[VM] * len(out_shape) if many else VM,
        scratch_shapes=list(scratch),
        compiler_params=pltpu.CompilerParams(vmem_limit_bytes=vmem << 20),
        cost_estimate=pl.CostEstimate(flops=flops, bytes_accessed=nbytes, transcendentals=0),
    )


def arr(shape, dtype):
    return jax.ShapeDtypeStruct(shape, dtype)


def lanes(rows):
    return lax.broadcasted_iota(jnp.int32, (rows, PS), 1)


def split(value):
    high = value.astype(BF16)
    return high, (value - high.astype(F32)).astype(BF16)


def dot(a, b):
    return lax.dot_general(a, b, (((1,), (0,)), ((), ())), preferred_element_type=F32)


def prep_kernel(anchors, row_offset, col_offset, live_counts, obj, high, field, ints, sems):
    copies = [pltpu.make_async_copy(obj.at[lax.axis_index("mode")], field, sems.at[0])]
    for k, ref in enumerate((anchors, col_offset, row_offset, live_counts)):
        copies.append(pltpu.make_async_copy(ref, ints[k], sems.at[k + 1]))
    for copy in copies:
        copy.start()
    for copy in copies[1:]:
        copy.wait()
    lane = lanes(8)
    meta = jnp.zeros((8, PS), F32)
    for p in range(2):
        alive = jnp.where(p < ints[3][0], 1, 0)
        for k, value in enumerate((ints[0][p], ints[1][p], ints[2][p], alive)):
            meta = jnp.where(lane == 4 * p + k, value.astype(F32), meta)
    copies[0].wait()
    for i in range(N_TM):
        chunk = field[CH * i : CH * i + HALO, :]
        high[i] = jnp.concatenate([chunk, meta], axis=0).astype(BF16)


def order_kernel(table, amp, out):
    def lines(value, product):
        high, low = split(value)
        return product(high) + product(low)

    rows = lines(amp[lax.axis_index("mode")], lambda x: dot(table[...], x))
    out[...] = lines(rows, lambda x: lax.dot_general(x, table[...], (((1,), (1,)), ((), ())), preferred_element_type=F32))


def cut_windows(meta, load, store, denom):
    def visit(t, total):
        for p in range(2):
            at, col, row, alive = (meta[t, 4 * p + k] for k in range(4))
            both = jnp.where(lanes(HALO) >= col, load(at), load(at + 1))
            both = pltpu.roll(both, lax.rem(HALO - row, HALO), 0)[0:CH].astype(BF16)
            store(t, p, both)
            both = pltpu.roll(both.astype(F32), lax.rem(PS - col, PS), 1)
            total = total + both * both * alive.astype(F32)
        return total

    denom[...] = lax.fori_loop(0, N_TM, visit, jnp.zeros((CH, PS), F32), unroll=4)


def window_kernel(meta, high, out, denom):
    def store(t, p, piece):
        out[2 * t + p] = piece

    cut_windows(meta, lambda at: high[at].astype(F32)[0:HALO], store, denom)


def shift_rows(block, row):
    return pltpu.roll(block, lax.rem(HALO + row, 32), 0)[0:HALO]


def weight_kernel(meta, power, out):
    out[...] = jnp.full_like(out, OBJECT_REG)
    first = pl.multiple_of(lax.axis_index("tm") * CH, CH)

    def visit(t, carry):
        block = power[pl.ds(first, 32), :]
        for p in range(2):
            at, col, row, alive = (meta[t, 4 * p + k] for k in range(4))
            mask = lanes(HALO) >= col
            cover = pltpu.roll(shift_rows(block, row), col, 1) * alive.astype(F32)
            out[at] += jnp.where(mask, cover, 0.0)
            out[at + 1] += jnp.where(mask, 0.0, cover)
        return carry

    lax.fori_loop(0, N_TM, visit, 0, unroll=UNROLL)

    def invert(t, carry):
        out[t] = 1.0 / out[t]
        return carry

    lax.fori_loop(0, N_TM, invert, 0, unroll=UNROLL)


def accumulate(meta, parts, num):
    num[...] = jnp.zeros_like(num)

    def visit(t, carry):
        both = parts[t, 64:112, :].astype(F32)
        for p in range(2):
            at, col = meta[t, 4 * p], meta[t, 4 * p + 1]
            mask = lanes(HALO) >= col
            piece = both[HALO * p : HALO * p + HALO]
            num[at] += jnp.where(mask, piece, 0.0)
            num[at + 1] += jnp.where(mask, 0.0, piece)
        return carry

    lax.fori_loop(0, N_TM, visit, 0, unroll=UNROLL)


def update_kernel(meta, parts, scale, high, out, denom, upd, fresh):
    accumulate(meta, parts, upd)

    def visit(t, carry):
        step = upd[t] * scale[t]
        upd[t] = step
        fresh[t] = high[t].astype(F32)[0:HALO] + step
        return carry

    lax.fori_loop(0, N_TM, visit, 0, unroll=UNROLL)

    def store(t, p, piece):
        out[t, CH * p : CH * p + CH, :] = piece

    cut_windows(meta, lambda at: fresh[at], store, denom)


def last_update_kernel(meta, parts, scale, upd, out, num):
    accumulate(meta, parts, num)

    def visit(t, carry):
        total = upd[t] + num[t] * scale[t]
        out[t] = jnp.concatenate([total, jnp.zeros((8, PS), F32)], axis=0).astype(BF16)
        return carry

    lax.fori_loop(0, N_TM, visit, 0, unroll=UNROLL)


def probe_sum_kernel(parts, denom, out):
    total = lax.fori_loop(0, N_TM, lambda t, acc: acc + parts[t, 0:64, :].astype(F32), jnp.zeros((64, PS), F32))
    out[0:64, :] = total.astype(BF16)
    out[64:80, :] = denom[...]


def probe_update_kernel(own, one, two, three, objs, out):
    total = (own[...].astype(F32) + two[...].astype(F32)) + (one[...].astype(F32) + three[...].astype(F32))
    scale = 1.0 / (total[64:80] + PROBE_REG)
    step = (total[0:64] * jnp.concatenate([scale] * 4, axis=0)).astype(BF16)

    def visit(t, carry):
        out[t, 0:32, :] = objs[t]
        out[t, 32:96, :] = step
        return carry

    lax.fori_loop(0, N_TM, visit, 0, unroll=UNROLL)


def pack_kernel(keep, recv, denom, out, denom_out):
    first = lax.axis_index("mode") == 0

    def visit(t, carry):
        mine, theirs = keep[t].astype(F32), recv[t].astype(F32)
        out[t, 0:64, :] = (mine[0:64] + theirs[0:64]).astype(BF16)
        num_mine, num_theirs = mine[64 : 64 + HALO], theirs[64 : 64 + HALO]
        out[t, 64:112, :] = jnp.concatenate(
            [jnp.where(first, num_mine, num_theirs), jnp.where(first, num_theirs, num_mine)], axis=0
        ).astype(BF16)
        return carry

    lax.fori_loop(0, N_TM, visit, 0, unroll=UNROLL)
    theirs = [recv[t, 64:96, :].astype(F32)[HALO:32] for t in range(2)]
    denom_out[...] = (denom[...] + jnp.concatenate(theirs, axis=0)).astype(BF16)


def put_left(ref, row, cols, value):
    for k in range(PARTS):
        ref[pl.ds(pl.multiple_of(row + k * PS, CH), CH), cols] = value.astype(BF16)


def put_right(ref, rows, lane, value):
    for k in range(PARTS):
        ref[rows, lane + k * PS : lane + k * PS + HALF] = value.astype(BF16)


def position_kernel(
    with_update, meta,
    l_even, l_even_t, l_odd, l_odd_t, r_even, r_even_t, r_odd, r_odd_t, p_own, p_oth, h_own, h_oth, amp, denom,
    keep, send, power, obj, probe, x_even, x_odd, y_even, y_odd, half_even, half_odd, far_even, far_odd, shifted,
):
    core = lax.axis_index("mode")
    first = core == 0
    col, row, alive = (meta[lax.axis_index("tm"), 4 * core + k] for k in (1, 2, 3))
    alive = alive.astype(F32)
    back_col = lax.rem(PS - col, PS)

    def rows_of(i, base=0):
        return pl.ds(pl.multiple_of(i * CH + base, CH), CH)

    def mode_cols(m):
        return slice(m * PS, (m + 1) * PS)

    power[0:8, :] = jnp.zeros((8, PS), F32)
    power[264:272, :] = jnp.zeros((8, PS), F32)

    def stage(i, carry):
        rows = rows_of(i)
        if with_update:
            mine = jnp.where(first, h_own[i, 0:CH, :].astype(F32), h_own[i, CH : 2 * CH, :].astype(F32))
            theirs = jnp.where(first, h_oth[i, 0:CH, :].astype(F32), h_oth[i, CH : 2 * CH, :].astype(F32))
            window = (jnp.where(first, mine, theirs), jnp.where(first, theirs, mine))
        else:
            window = [h_own[2 * i + k].astype(F32) for k in range(2)]
        for k in range(2):
            obj[k, rows, :] = pltpu.roll(window[k], back_col, 1)
        total = jnp.zeros((CH, PS), F32)
        for m in range(4):
            src, chunk = (p_own, h_own) if m < 2 else (p_oth, h_oth)
            for k in range(2):
                value = src[m % 2, k, rows, :]
                if with_update:
                    at = 32 + CH * (2 * (m % 2) + k)
                    value = value + chunk[i, at : at + CH, :].astype(F32)
                probe[m, k, rows, :] = value
                total = total + value * value
        power[pl.ds(pl.multiple_of(i * CH + 8, 8), CH), :] = total
        return carry

    lax.fori_loop(0, N_TM, stage, 0, unroll=UNROLL)

    def wave(m, rows):
        pr, pi = probe[m, 0, rows, :], probe[m, 1, rows, :]
        o_r, o_i = obj[0, rows, :], obj[1, rows, :]
        return pr * o_r - pi * o_i, pr * o_i + pi * o_r

    def forward_rows(i, carry):
        for m in range(4):
            upper, lower = wave(m, rows_of(i)), wave(m, rows_of(i, HALF))
            for k in range(2):
                a, b = upper[k], lower[k]
                put_left(x_even, i * CH + k * HALF, mode_cols(m), a + b)
                put_left(x_odd, i * CH + k * HALF, mode_cols(m), a - b)
        return carry

    lax.fori_loop(0, HALF // CH, forward_rows, 0, unroll=UNROLL)
    half_even[...] = dot(l_even[...], x_even[...])
    half_odd[...] = dot(l_odd[...], x_odd[...])

    def forward_cols(i, carry):
        for m in range(4):
            for b, half in enumerate((half_even, half_odd)):
                for k in range(2):
                    value = half[rows_of(i, k * HALF), mode_cols(m)]
                    rows = rows_of(i, m * PS + b * HALF)
                    put_right(y_even, rows, k * HALF, value[:, 0:HALF] + value[:, HALF:PS])
                    put_right(y_odd, rows, k * HALF, value[:, 0:HALF] - value[:, HALF:PS])
        return carry

    lax.fori_loop(0, HALF // CH, forward_cols, 0, unroll=UNROLL)
    far_even[...] = dot(y_even[...], r_even_t[...])
    far_odd[...] = dot(y_odd[...], r_odd_t[...])

    def rescale(i, carry):
        for b, (far, y) in enumerate(((far_even, y_even), (far_odd, y_odd))):
            values = [far[rows_of(i, m * PS), :] for m in range(4)]
            squares = [v[:, 0:HALF] * v[:, 0:HALF] + v[:, HALF:PS] * v[:, HALF:PS] for v in values]
            total = (squares[0] + squares[1]).astype(BF16).astype(F32) + (squares[2] + squares[3]).astype(
                BF16
            ).astype(F32)
            factor = amp[rows_of(i), b * HALF : (b + 1) * HALF] * lax.rsqrt(jnp.maximum(total, FLOOR_VALUE)) - 1.0
            for m in range(4):
                for k in range(2):
                    put_right(y, rows_of(i, m * PS), k * HALF, values[m][:, k * HALF : (k + 1) * HALF] * factor)
        return carry

    lax.fori_loop(0, N_TM, rescale, 0, unroll=UNROLL)
    far_even[...] = dot(y_even[...], r_even[...])
    far_odd[...] = dot(y_odd[...], r_odd[...])

    def backward_cols(i, carry):
        for m in range(4):
            for b, x in enumerate((x_even, x_odd)):
                rows = rows_of(i, m * PS + b * HALF)
                even, odd = far_even[rows, :], far_odd[rows, :]
                total, diff = even + odd, even - odd
                for k in range(2):
                    part = slice(k * HALF, (k + 1) * HALF)
                    put_left(x, i * CH + k * HALF, slice(m * PS, m * PS + HALF), total[:, part])
                    put_left(x, i * CH + k * HALF, slice(m * PS + HALF, (m + 1) * PS), diff[:, part])
        return carry

    lax.fori_loop(0, HALF // CH, backward_cols, 0, unroll=UNROLL)
    half_even[...] = dot(l_even_t[...], x_even[...])
    half_odd[...] = dot(l_odd_t[...], x_odd[...])

    def outputs(i, carry):
        for s in range(2):
            rows = rows_of(i, s * HALF)
            n_re, n_im = jnp.zeros((CH, PS), F32), jnp.zeros((CH, PS), F32)
            for g, target in enumerate((keep, send)):
                g_re, g_im = jnp.zeros((CH, PS), F32), jnp.zeros((CH, PS), F32)
                for mm in range(2):
                    m = 2 * g + mm
                    pr, pi, o_r, o_i = probe[m, 0, rows, :], probe[m, 1, rows, :], obj[0, rows, :], obj[1, rows, :]
                    res = []
                    for k in range(2):
                        at = rows_of(i, k * HALF)
                        even, odd = half_even[at, mode_cols(m)], half_odd[at, mode_cols(m)]
                        res.append(even + odd if s == 0 else even - odd)
                    dr, di = res[0] * alive, res[1] * alive
                    chunk = i + s * (HALF // CH)
                    target[chunk, 2 * mm * CH : (2 * mm + 1) * CH, :] = (o_r * dr + o_i * di).astype(BF16)
                    target[chunk, (2 * mm + 1) * CH : (2 * mm + 2) * CH, :] = (o_r * di - o_i * dr).astype(BF16)
                    g_re = g_re + (pr * dr + pi * di)
                    g_im = g_im + (pr * di - pi * dr)
                n_re = n_re + g_re.astype(BF16).astype(F32)
                n_im = n_im + g_im.astype(BF16).astype(F32)
            at = pl.ds(pl.multiple_of(i * CH + s * HALF + 8, 8), CH)
            shifted[0, at, :] = pltpu.roll(n_re, col, 1)
            shifted[1, at, :] = pltpu.roll(n_im, col, 1)
        return carry

    shifted[:, 0:8, :] = jnp.zeros((2, 8, PS), F32)
    shifted[:, 264:272, :] = jnp.zeros((2, 8, PS), F32)
    lax.fori_loop(0, HALF // CH, outputs, 0, unroll=UNROLL)

    def emit(i, carry):
        rows = pl.ds(pl.multiple_of(i * CH, CH), 32)
        pad = jnp.where(i == 0, denom[0:8, :], jnp.where(i == 1, denom[8:16, :], 0.0))
        re, im = (
            jnp.concatenate([shift_rows(shifted[k, rows, :], row), pad], axis=0) for k in range(2)
        )
        keep[i, 64:96, :] = jnp.where(first, re, im).astype(BF16)
        send[i, 64:96, :] = jnp.where(first, im, re).astype(BF16)
        return carry

    lax.fori_loop(0, N_TM, emit, 0, unroll=UNROLL)


def position(with_update, *args):
    part = arr((N_TM, 96, PS), BF16)
    left, right = pltpu.VMEM((PARTS * PS, 4 * PS), BF16), pltpu.VMEM((4 * PS, PARTS * PS), BF16)
    return call(
        functools.partial(position_kernel, with_update),
        (part, part, arr((272, PS), F32)),
        [SM] + [VM] * 14,
        scratch=[
            pltpu.VMEM((2, PS, PS), F32),
            pltpu.VMEM((4, 2, PS, PS), F32),
            left,
            left,
            right,
            right,
            pltpu.VMEM((PS, 4 * PS), F32),
            pltpu.VMEM((PS, 4 * PS), F32),
            pltpu.VMEM((4 * PS, PS), F32),
            pltpu.VMEM((4 * PS, PS), F32),
            pltpu.VMEM((2, 272, PS), F32),
        ],
        flops=32 * PARTS * 2 * 256 * 256 * 256,
        nbytes=10 << 20,
        vmem=24,
    )(*args)


def final_probe_kernel(p_own, h_one, h_two, out):
    def visit(i, carry):
        rows = pl.ds(pl.multiple_of(i * CH, CH), CH)
        for m in range(2):
            for k in range(2):
                at = 32 + CH * (2 * m + k)
                before = p_own[m, k, rows, :] + h_one[i, at : at + CH, :].astype(F32)
                out[m, k, rows, :] = before + h_two[i, at : at + CH, :].astype(F32)
        return carry

    lax.fori_loop(0, N_TM, visit, 0, unroll=UNROLL)


def final_object_kernel(obj, h_own, h_oth, out):
    core = lax.axis_index("mode")

    def visit(i, carry):
        rows = pl.ds(pl.multiple_of(i * CH, CH), CH)
        out[core, rows, :] = obj[core, rows, :] + h_own[i, 0:CH, :].astype(F32)
        out[1 - core, rows, :] = obj[1 - core, rows, :] + h_oth[i, 0:CH, :].astype(F32)
        return carry

    lax.fori_loop(0, N_TM, visit, 0, unroll=UNROLL)
    last = N_TM - 1
    out[core, 256:264, :] = obj[core, 256:264, :] + h_own[last, 16:32, :].astype(F32)[0:8]
    out[1 - core, 256:264, :] = obj[1 - core, 256:264, :] + h_oth[last, 16:32, :].astype(F32)[0:8]


def body(object_field, probe_modes, amplitudes, anchors, row_offset, col_offset, live_counts):
    tables = [jnp.asarray(t) for t in dft_tables()]

    def exchange(x):
        return lax.all_to_all(x, "tm", 0, 0)

    def swap(x):
        return lax.ppermute(x, "mode", SWAP)

    def over_tiles(x):
        n = lax.axis_size("tile")
        return [lax.ppermute(x, "tile", [(i, (i + k) % n) for i in range(n)]) for k in (1, 2, 3)]

    slot = arr((N_TM, 32, PS), BF16)
    denom_shape = arr((CH, PS), F32)
    chunk = (N_TM, HALO, PS)
    high = call(
        prep_kernel,
        slot,
        [pl.BlockSpec(memory_space=pltpu.HBM)] * 5,
        scratch=[
            pltpu.VMEM((BH, PS), F32),
            [pltpu.SMEM((n,), jnp.int32) for n in (2, 2, 2, 1)],
            pltpu.SemaphoreType.DMA((5,)),
        ],
        vmem=60,
    )(anchors.reshape(-1), row_offset, col_offset, live_counts, object_field)
    probe_other = swap(probe_modes)
    high = exchange(high)
    amp = call(order_kernel, arr((PS, PS), F32), [VM, VM])(jnp.asarray(order_table()), amplitudes)
    high, amp = lax.optimization_barrier((high, amp))
    meta = high[:, HALO, 0:8].astype(jnp.int32)
    windows, denom = call(window_kernel, (arr((2 * N_TM, CH, PS), BF16), denom_shape), [SM, VM])(meta, high)
    h_own = h_oth = lax.all_to_all(windows, ("tm", "mode"), 0, 0)

    for iteration in range(2):
        if iteration > 0:
            h_oth = swap(h_own)
        keep, send, power = position(
            iteration > 0, meta, *tables, probe_modes, probe_other, h_own, h_oth, amp, denom
        )
        recv = swap(send)
        scale = call(weight_kernel, arr(chunk, F32), [SM, VM])(meta, power)
        recv, scale = lax.optimization_barrier((recv, scale))
        parts, denom = call(pack_kernel, (arr((N_TM, 112, PS), BF16), arr((CH, PS), BF16)), [VM] * 3)(
            keep, recv, denom
        )
        parts = exchange(parts)
        probe_part = call(probe_sum_kernel, arr((80, PS), BF16), [VM] * 2)(parts, denom)
        others = over_tiles(probe_part)
        if iteration == 0:
            objs, denom, upd = call(
                update_kernel,
                (slot, denom_shape, arr(chunk, F32)),
                [SM] + [VM] * 3,
                scratch=[pltpu.VMEM(chunk, F32)],
            )(meta, parts, scale, high)
        else:
            objs = call(last_update_kernel, slot, [SM] + [VM] * 3, scratch=[pltpu.VMEM(chunk, F32)])(
                meta, parts, scale, upd
            )
        h_first = h_own
        h_own = exchange(
            call(probe_update_kernel, arr((N_TM, 96, PS), BF16), [VM] * 5)(probe_part, *others, objs)
        )

    h_oth = swap(h_own)
    probe_out = call(final_probe_kernel, arr((2, 2, PS, PS), F32), [VM] * 3)(probe_modes, h_first, h_own)
    object_out = call(final_object_kernel, arr((2, BH, PS), F32), [VM] * 3)(object_field, h_own, h_oth)
    return (object_out, probe_out)


def solution(mesh):
    placed = (
        P(None, "tile", "tm"),
        P("mode", None, None, None),
        P(("tile", "tm"), None, None),
        P(("tile", "tm"), None),
        P(("tile", "tm")),
        P(("tile", "tm")),
        P(("tile", "tm")),
    )
    return jax.shard_map(
        body,
        mesh=mesh,
        in_specs=placed,
        out_specs=(P(None, "tile", "tm"), P("mode", None, None, None)),
        check_vma=False,
    )
```

profile of v0, /device:TPU:1, one launch (start us, length us, event | category | flops | bytes accessed | tf_op | source)
XLA Modules:
  0.0 139.9 jit_solution(13673575971444071595)
XLA Ops:
  0.6 1.5 %collective-permute-start = (f32[2,2,256,256]{3,2,1,0:T(8,128)}, f32[2,2,256,256]{3,2,1,0:T(8,128)S(1)}, u32[]{:S(2)}, u32[]{:S(2)}) collective-permute-start(f32[2,2,256,256]{3,2,1,0:T(8,128)} %p_own.5), channel_id=1, source_target_pairs={{0,1},{1,0},{2,3},{3,2},{4,5},{5,4},{6,7},{7,6},{8,9},{9,8},{10,11... | collective-permute-start | bytes 3145736 | tf_op jit(solution)/shard_map/ppermute | solution.py:471
  2.8 1.8 %shard_map.167 = bf16[16,32,256]{2,1,0:T(8,128)(2,1)} custom-call(s32[2]{0:T(128)} %bitcast.9, s32[2]{0:T(128)} %row_offset.1, s32[2]{0:T(128)} %col_offset.1, s32[1]{0:T(128)S(6)} %copy.35.live_counts, f32[2,264,256]{2,1,0:T(8,128)} %obj.3), custom_call_target="tpu_custom_call" | custom-call | bytes 1048576 | tf_op jit(solution)/shard_map/pallas_call | solution.py:480
  4.6 8.0 %all-to-all-start = ((bf16[16,32,256]{2,1,0:T(8,128)(2,1)}), bf16[16,32,256]{2,1,0:T(8,128)(2,1)S(1)}, u32[]{:S(2)}, u32[]{:S(2)}) async-start(bf16[16,32,256]{2,1,0:T(8,128)(2,1)} %shard_map.167), calls=%async_computation | async-start | bytes 524288 | tf_op jit(solution)/shard_map/all_to_all | solution.py:468
  13.1 7.3 %all-to-all-done.high = bf16[16,32,256]{2,1,0:T(8,128)(2,1)S(1)} async-done(((bf16[16,32,256]{2,1,0:T(8,128)(2,1)}), bf16[16,32,256]{2,1,0:T(8,128)(2,1)S(1)}, u32[]{:S(2)}, u32[]{:S(2)}) %all-to-all-start) | async-done | bytes 262176 | tf_op jit(solution)/shard_map/all_to_all | solution.py:468
  20.5 1.3 shard_map.169
  21.8 14.2 %all_to_all.30.h_own.h_oth = bf16[32,16,256]{2,1,0:T(8,128)(2,1)S(1)} all-to-all(bf16[32,16,256]{2,1,0:T(8,128)(2,1)S(1)} %get-tuple-element.24), channel_id=1, replica_groups=mesh['tile'=4,'tm'=16,'mode'=2] {'tm','mode'}, dimensions={0} | all-to-all | bytes 524288 | tf_op jit(solution)/shard_map/all_to_all | solution.py:497
  36.1 4.2 %shard_map.170 = (bf16[16,96,256]{2,1,0:T(8,128)(2,1)S(1)}, bf16[16,96,256]{2,1,0:T(8,128)(2,1)S(1)}, f32[272,256]{1,0:T(8,128)S(1)}) custom-call(s32[16,8]{1,0:T(8,128)S(1)} %bitcast.3, bf16[256,256]{1,0:T(8,128)(2,1)S(1)} %copy-done.5, bf16[256,256]{1,0:T(8,128)(2,1)S(1)} %copy-done.4, bf16[256,256]{1,0:T(8,128)(2,1)S(1)} %copy-done.3, ...), custom_call_target="tpu_custom_call" | custom-call | flops 1073741824 | bytes 10485760 | tf_op jit(solution)/shard_map/pallas_call | solution.py:413
  40.5 1.2 shard_map.171.scale
  41.7 0.9 collective-permute-done.1.recv
  42.8 16.8 %all_to_all.31.parts = bf16[16,112,256]{2,1,0:T(8,128)(2,1)S(1)} all-to-all(bf16[16,112,256]{2,1,0:T(8,128)(2,1)S(1)} %get-tuple-element.31), channel_id=1, replica_groups=mesh['tile'=4,'tm'=16,'mode'=2] {'tm'}, dimensions={0} | all-to-all | bytes 1835008 | tf_op jit(solution)/shard_map/all_to_all | solution.py:468
  59.8 2.5 %collective-permute-start.4 = (bf16[80,256]{1,0:T(8,128)(2,1)S(1)}, bf16[80,256]{1,0:T(8,128)(2,1)S(1)}, u32[]{:S(2)}, u32[]{:S(2)}) collective-permute-start(bf16[80,256]{1,0:T(8,128)(2,1)S(1)} %shard_map.173.own), channel_id=1, source_target_pairs={{0,96},{32,0},{64,32},{96,64},{1,97},{33,1},{65,33},{97,65},{2,98}... | collective-permute-start | bytes 122888 | tf_op jit(solution)/shard_map/ppermute | solution.py:475
  63.5 1.6 %shard_map.174 = (bf16[16,32,256]{2,1,0:T(8,128)(2,1)S(1)}, f32[16,256]{1,0:T(8,128)S(1)}, f32[16,24,256]{2,1,0:T(8,128)S(1)}) custom-call(s32[16,8]{1,0:T(8,128)S(1)} %bitcast.5, bf16[16,112,256]{2,1,0:T(8,128)(2,1)S(1)} %all_to_all.31.parts, f32[16,24,256]{2,1,0:T(8,128)S(1)} %shard_map.171.scale, bf16[16,32,256]{2,1,0:T(8,128)(2,1)S(1)} %all-to-all-done.high), custom_call_target="tpu_custom_call" | custom-call | bytes 1048576 | tf_op jit(solution)/shard_map/pallas_call | solution.py:515
  65.1 1.7 %collective-permute-done.3.two = bf16[80,256]{1,0:T(8,128)(2,1)S(1)} collective-permute-done((bf16[80,256]{1,0:T(8,128)(2,1)S(1)}, bf16[80,256]{1,0:T(8,128)(2,1)S(1)}, u32[]{:S(2)}, u32[]{:S(2)}) %collective-permute-start.3) | collective-permute-done | bytes 40992 | tf_op jit(solution)/shard_map/ppermute | solution.py:475
  67.2 14.4 %all_to_all.32.h_own.h_one = bf16[16,96,256]{2,1,0:T(8,128)(2,1)S(1)} all-to-all(bf16[16,96,256]{2,1,0:T(8,128)(2,1)S(1)} %shard_map.175), channel_id=1, replica_groups=mesh['tile'=4,'tm'=16,'mode'=2] {'tm'}, dimensions={0} | all-to-all | bytes 1572864 | tf_op jit(solution)/shard_map/all_to_all | solution.py:468
  81.6 4.7 %collective-permute-start.5 = (bf16[16,96,256]{2,1,0:T(8,128)(2,1)S(1)}, bf16[16,96,256]{2,1,0:T(8,128)(2,1)S(1)}, u32[]{:S(2)}, u32[]{:S(2)}) collective-permute-start(bf16[16,96,256]{2,1,0:T(8,128)(2,1)S(1)} %all_to_all.32.h_own.h_one), channel_id=1, source_target_pairs={{0,1},{1,0},{2,3},{3,2},{4,5},{5,4},{6,7},{7,6},{8,9},{9,8},{10,11... | collective-permute-start | bytes 2359304 | tf_op jit(solution)/shard_map/ppermute | solution.py:471
  86.3 1.9 %collective-permute-done.5.h_oth = bf16[16,96,256]{2,1,0:T(8,128)(2,1)S(1)} collective-permute-done((bf16[16,96,256]{2,1,0:T(8,128)(2,1)S(1)}, bf16[16,96,256]{2,1,0:T(8,128)(2,1)S(1)}, u32[]{:S(2)}, u32[]{:S(2)}) %collective-permute-start.5) | collective-permute-done | bytes 786464 | tf_op jit(solution)/shard_map/ppermute | solution.py:471
  88.2 4.3 %shard_map.176 = (bf16[16,96,256]{2,1,0:T(8,128)(2,1)S(1)}, bf16[16,96,256]{2,1,0:T(8,128)(2,1)S(1)}, f32[272,256]{1,0:T(8,128)S(1)}) custom-call(s32[16,8]{1,0:T(8,128)S(1)} %bitcast.6, bf16[256,256]{1,0:T(8,128)(2,1)S(1)} %copy-done.5, bf16[256,256]{1,0:T(8,128)(2,1)S(1)} %copy-done.4, bf16[256,256]{1,0:T(8,128)(2,1)S(1)} %copy-done.3, ...), custom_call_target="tpu_custom_call" | custom-call | flops 1073741824 | bytes 10485760 | tf_op jit(solution)/shard_map/pallas_call | solution.py:413
  93.0 1.2 shard_map.177.scale
  95.1 17.2 %all_to_all.33.parts = bf16[16,112,256]{2,1,0:T(8,128)(2,1)S(1)} all-to-all(bf16[16,112,256]{2,1,0:T(8,128)(2,1)S(1)} %get-tuple-element.40), channel_id=1, replica_groups=mesh['tile'=4,'tm'=16,'mode'=2] {'tm'}, dimensions={0} | all-to-all | bytes 1835008 | tf_op jit(solution)/shard_map/all_to_all | solution.py:468
  114.5 1.0 shard_map.180.objs
  115.4 1.9 %collective-permute-done.8.two = bf16[80,256]{1,0:T(8,128)(2,1)S(1)} collective-permute-done((bf16[80,256]{1,0:T(8,128)(2,1)S(1)}, bf16[80,256]{1,0:T(8,128)(2,1)S(1)}, u32[]{:S(2)}, u32[]{:S(2)}) %collective-permute-start.8) | collective-permute-done | bytes 40992 | tf_op jit(solution)/shard_map/ppermute | solution.py:475
  118.0 14.4 %all_to_all.34.h_own.h_two = bf16[16,96,256]{2,1,0:T(8,128)(2,1)S(1)} all-to-all(bf16[16,96,256]{2,1,0:T(8,128)(2,1)S(1)} %shard_map.181), channel_id=1, replica_groups=mesh['tile'=4,'tm'=16,'mode'=2] {'tm'}, dimensions={0} | all-to-all | bytes 1572864 | tf_op jit(solution)/shard_map/all_to_all | solution.py:468
  132.4 4.7 %collective-permute-start.10 = (bf16[16,96,256]{2,1,0:T(8,128)(2,1)S(1)}, bf16[16,96,256]{2,1,0:T(8,128)(2,1)S(1)}, u32[]{:S(2)}, u32[]{:S(2)}) collective-permute-start(bf16[16,96,256]{2,1,0:T(8,128)(2,1)S(1)} %all_to_all.34.h_own.h_two), channel_id=1, source_target_pairs={{0,1},{1,0},{2,3},{3,2},{4,5},{5,4},{6,7},{7,6},{8,9},{9,8},{10,11... | collective-permute-start | bytes 2359304 | tf_op jit(solution)/shard_map/ppermute | solution.py:471
  137.1 1.2 shard_map.183
  (39 shorter events, 8.5 us)
Async XLA Ops:
  0.6 35.4 %collective-permute-start = (f32[2,2,256,256]{3,2,1,0:T(8,128)}, f32[2,2,256,256]{3,2,1,0:T(8,128)S(1)}, u32[]{:S(2)}, u32[]{:S(2)}) collective-permute-start(f32[2,2,256,256]{3,2,1,0:T(8,128)} %p_own.5), channel_id=1, source_target_pairs={{0,1},{1,0},{2,3},{3,2},{4,5},{5,4},{6,7},{7,6},{8,9},{9,8},{10,11... | collective-permute-start | bytes 3145736 | tf_op jit(solution)/shard_map/ppermute | solution.py:471
  2.8 9.8 %copy-start.6 = (f32[2,256,256]{2,1,0:T(8,128)S(1)}, f32[2,256,256]{2,1,0:T(8,128)}, u32[]{:S(2)}) copy-start(f32[2,256,256]{2,1,0:T(8,128)} %amp.1) | copy-start | bytes 1572868
  2.8 9.8 %copy-start.7 = (bf16[256,256]{1,0:T(8,128)(2,1)S(1)}, bf16[256,256]{1,0:T(8,128)(2,1)}, u32[]{:S(2)}) copy-start(bf16[256,256]{1,0:T(8,128)(2,1)} %constant.14.clone.table) | copy-start | bytes 393220
  4.6 31.4 %copy-start = (f32[2,2,256,256]{3,2,1,0:T(8,128)S(1)}, f32[2,2,256,256]{3,2,1,0:T(8,128)}, u32[]{:S(2)}) copy-start(f32[2,2,256,256]{3,2,1,0:T(8,128)} %p_own.5) | copy-start | bytes 3145732
  4.6 15.8 %all-to-all-start = ((bf16[16,32,256]{2,1,0:T(8,128)(2,1)}), bf16[16,32,256]{2,1,0:T(8,128)(2,1)S(1)}, u32[]{:S(2)}, u32[]{:S(2)}) async-start(bf16[16,32,256]{2,1,0:T(8,128)(2,1)} %shard_map.167), calls=%async_computation | async-start | bytes 524288 | tf_op jit(solution)/shard_map/all_to_all | solution.py:468
  21.7 14.3 %copy-start.2 = (bf16[256,256]{1,0:T(8,128)(2,1)S(1)}, bf16[256,256]{1,0:T(8,128)(2,1)}, u32[]{:S(2)}) copy-start(bf16[256,256]{1,0:T(8,128)(2,1)} %constant.13.clone.l_odd_t.r_odd_t) | copy-start | bytes 393220
  21.7 14.3 %copy-start.3 = (bf16[256,256]{1,0:T(8,128)(2,1)S(1)}, bf16[256,256]{1,0:T(8,128)(2,1)}, u32[]{:S(2)}) copy-start(bf16[256,256]{1,0:T(8,128)(2,1)} %constant.12.clone.l_odd.r_odd) | copy-start | bytes 393220
  21.8 14.3 %copy-start.4 = (bf16[256,256]{1,0:T(8,128)(2,1)S(1)}, bf16[256,256]{1,0:T(8,128)(2,1)}, u32[]{:S(2)}) copy-start(bf16[256,256]{1,0:T(8,128)(2,1)} %constant.11.clone.l_even_t.r_even_t) | copy-start | bytes 393220
  21.8 14.3 %copy-start.5 = (bf16[256,256]{1,0:T(8,128)(2,1)S(1)}, bf16[256,256]{1,0:T(8,128)(2,1)}, u32[]{:S(2)}) copy-start(bf16[256,256]{1,0:T(8,128)(2,1)} %constant.10.clone.l_even.r_even) | copy-start | bytes 393220
  40.2 2.4 %collective-permute-start.1 = (bf16[16,96,256]{2,1,0:T(8,128)(2,1)S(1)}, bf16[16,96,256]{2,1,0:T(8,128)(2,1)S(1)}, u32[]{:S(2)}, u32[]{:S(2)}) collective-permute-start(bf16[16,96,256]{2,1,0:T(8,128)(2,1)S(1)} %get-tuple-element.28), channel_id=1, source_target_pairs={{0,1},{1,0},{2,3},{3,2},{4,5},{5,4},{6,7},{7,6},{8,9},{9,8},{10,11... | collective-permute-start | bytes 2359304 | tf_op jit(solution)/shard_map/ppermute | solution.py:471
  59.8 5.3 %collective-permute-start.4 = (bf16[80,256]{1,0:T(8,128)(2,1)S(1)}, bf16[80,256]{1,0:T(8,128)(2,1)S(1)}, u32[]{:S(2)}, u32[]{:S(2)}) collective-permute-start(bf16[80,256]{1,0:T(8,128)(2,1)S(1)} %shard_map.173.own), channel_id=1, source_target_pairs={{0,96},{32,0},{64,32},{96,64},{1,97},{33,1},{65,33},{97,65},{2,98}... | collective-permute-start | bytes 122888 | tf_op jit(solution)/shard_map/ppermute | solution.py:475
  62.3 4.4 %collective-permute-start.3 = (bf16[80,256]{1,0:T(8,128)(2,1)S(1)}, bf16[80,256]{1,0:T(8,128)(2,1)S(1)}, u32[]{:S(2)}, u32[]{:S(2)}) collective-permute-start(bf16[80,256]{1,0:T(8,128)(2,1)S(1)} %shard_map.173.own), channel_id=1, source_target_pairs={{0,64},{32,96},{64,0},{96,32},{1,65},{33,97},{65,1},{97,33},{2,66}... | collective-permute-start | bytes 122888 | tf_op jit(solution)/shard_map/ppermute | solution.py:475
  62.8 4.3 %collective-permute-start.2 = (bf16[80,256]{1,0:T(8,128)(2,1)S(1)}, bf16[80,256]{1,0:T(8,128)(2,1)S(1)}, u32[]{:S(2)}, u32[]{:S(2)}) collective-permute-start(bf16[80,256]{1,0:T(8,128)(2,1)S(1)} %shard_map.173.own), channel_id=1, source_target_pairs={{0,32},{32,64},{64,96},{96,0},{1,33},{33,65},{65,97},{97,1},{2,34}... | collective-permute-start | bytes 122888 | tf_op jit(solution)/shard_map/ppermute | solution.py:475
  81.6 6.6 %collective-permute-start.5 = (bf16[16,96,256]{2,1,0:T(8,128)(2,1)S(1)}, bf16[16,96,256]{2,1,0:T(8,128)(2,1)S(1)}, u32[]{:S(2)}, u32[]{:S(2)}) collective-permute-start(bf16[16,96,256]{2,1,0:T(8,128)(2,1)S(1)} %all_to_all.32.h_own.h_one), channel_id=1, source_target_pairs={{0,1},{1,0},{2,3},{3,2},{4,5},{5,4},{6,7},{7,6},{8,9},{9,8},{10,11... | collective-permute-start | bytes 2359304 | tf_op jit(solution)/shard_map/ppermute | solution.py:471
  92.6 2.4 %collective-permute-start.6 = (bf16[16,96,256]{2,1,0:T(8,128)(2,1)S(1)}, bf16[16,96,256]{2,1,0:T(8,128)(2,1)S(1)}, u32[]{:S(2)}, u32[]{:S(2)}) collective-permute-start(bf16[16,96,256]{2,1,0:T(8,128)(2,1)S(1)} %get-tuple-element.37), channel_id=1, source_target_pairs={{0,1},{1,0},{2,3},{3,2},{4,5},{5,4},{6,7},{7,6},{8,9},{9,8},{10,11... | collective-permute-start | bytes 2359304 | tf_op jit(solution)/shard_map/ppermute | solution.py:471
  112.5 2.9 %collective-permute-start.9 = (bf16[80,256]{1,0:T(8,128)(2,1)S(1)}, bf16[80,256]{1,0:T(8,128)(2,1)S(1)}, u32[]{:S(2)}, u32[]{:S(2)}) collective-permute-start(bf16[80,256]{1,0:T(8,128)(2,1)S(1)} %shard_map.179.own), channel_id=1, source_target_pairs={{0,96},{32,0},{64,32},{96,64},{1,97},{33,1},{65,33},{97,65},{2,98}... | collective-permute-start | bytes 122888 | tf_op jit(solution)/shard_map/ppermute | solution.py:475
  113.0 4.4 %collective-permute-start.8 = (bf16[80,256]{1,0:T(8,128)(2,1)S(1)}, bf16[80,256]{1,0:T(8,128)(2,1)S(1)}, u32[]{:S(2)}, u32[]{:S(2)}) collective-permute-start(bf16[80,256]{1,0:T(8,128)(2,1)S(1)} %shard_map.179.own), channel_id=1, source_target_pairs={{0,64},{32,96},{64,0},{96,32},{1,65},{33,97},{65,1},{97,33},{2,66}... | collective-permute-start | bytes 122888 | tf_op jit(solution)/shard_map/ppermute | solution.py:475
  113.8 4.1 %collective-permute-start.7 = (bf16[80,256]{1,0:T(8,128)(2,1)S(1)}, bf16[80,256]{1,0:T(8,128)(2,1)S(1)}, u32[]{:S(2)}, u32[]{:S(2)}) collective-permute-start(bf16[80,256]{1,0:T(8,128)(2,1)S(1)} %shard_map.179.own), channel_id=1, source_target_pairs={{0,32},{32,64},{64,96},{96,0},{1,33},{33,65},{65,97},{97,1},{2,34}... | collective-permute-start | bytes 122888 | tf_op jit(solution)/shard_map/ppermute | solution.py:475
  132.4 6.7 %copy-start.1 = (f32[2,264,256]{2,1,0:T(8,128)S(1)}, f32[2,264,256]{2,1,0:T(8,128)}, u32[]{:S(2)}) copy-start(f32[2,264,256]{2,1,0:T(8,128)} %obj.3) | copy-start | bytes 1622020
  132.4 6.6 %collective-permute-start.10 = (bf16[16,96,256]{2,1,0:T(8,128)(2,1)S(1)}, bf16[16,96,256]{2,1,0:T(8,128)(2,1)S(1)}, u32[]{:S(2)}, u32[]{:S(2)}) collective-permute-start(bf16[16,96,256]{2,1,0:T(8,128)(2,1)S(1)} %all_to_all.34.h_own.h_two), channel_id=1, source_target_pairs={{0,1},{1,0},{2,3},{3,2},{4,5},{5,4},{6,7},{7,6},{8,9},{9,8},{10,11... | collective-permute-start | bytes 2359304 | tf_op jit(solution)/shard_map/ppermute | solution.py:471
where the time goes:
time: 140 us
  blocking collectives  77.1 us (55%)
  starting transfers between devices  25.3 us (18%)
  Pallas kernels  19.9 us (14%)
  waiting for transfers between devices  16.1 us (12%)
  between operations  1.51 us (1%)
    all_to_all x4, blocking collectives, exchange(): return lax.all_to_all(x, 'tm', 0, 0)  62.8 us
    all_to_all x1, blocking collectives, body(): h_own = h_oth = lax.all_to_all(windows, ('tm', 'mode'), 0, 0)  14.2 us
    ppermute x5, starting transfers between devices, swap(): return lax.ppermute(x, 'mode', SWAP)  11.7 us
    pallas_call x2, Pallas kernels, position(): call(functools.partial(position_kernel, with_update), (part, part, arr((2...  8.5 us
    all_to_all x1, starting transfers between devices, exchange(): return lax.all_to_all(x, 'tm', 0, 0)  8 us
    all_to_all x1, waiting for transfers between devices, exchange(): return lax.all_to_all(x, 'tm', 0, 0)  7.33 us
    ppermute x6, starting transfers between devices, over_tiles(): lax.ppermute(x, 'tile', [(i, (i + k) % n) for i in range(n)])  5.63 us
    ppermute x6, waiting for transfers between devices, over_tiles(): lax.ppermute(x, 'tile', [(i, (i + k) % n) for i in range(n)])  4.52 us
  transfers between devices with their start and end apart: 12, of which 9 were waited for; matrix products, arithmetic and copies ran while one was open for 0% of the time, Pallas kernels for 7%

commit v1 on v0

--- a/solution.py
+++ b/solution.py
@@ -14,7 +14,7 @@
 PARTS = 1
 BH = 264
 N_TM = 16
-UNROLL = 8
+UNROLL = 16
 CH = 16
 HALO = 24
 FLOOR_VALUE = 0.5
@@ -97,7 +97,7 @@
     lane = lanes(8)
     meta = jnp.zeros((8, PS), F32)
     for p in range(2):
-        alive = jnp.where(p < ints[3][0], 1, 0)
+        alive = jnp.where(p < ints[3][0, 0], 1, 0)
         for k, value in enumerate((ints[0][p], ints[1][p], ints[2][p], alive)):
             meta = jnp.where(lane == 4 * p + k, value.astype(F32), meta)
     copies[0].wait()
@@ -312,7 +312,7 @@
                 put_left(x_odd, i * CH + k * HALF, mode_cols(m), a - b)
         return carry
 
-    lax.fori_loop(0, HALF // CH, forward_rows, 0, unroll=UNROLL)
+    lax.fori_loop(0, HALF // CH, forward_rows, 0, unroll=8)
     half_even[...] = dot(l_even[...], x_even[...])
     half_odd[...] = dot(l_odd[...], x_odd[...])
 
@@ -326,7 +326,7 @@
                     put_right(y_odd, rows, k * HALF, value[:, 0:HALF] - value[:, HALF:PS])
         return carry
 
-    lax.fori_loop(0, HALF // CH, forward_cols, 0, unroll=UNROLL)
+    lax.fori_loop(0, HALF // CH, forward_cols, 0, unroll=8)
     far_even[...] = dot(y_even[...], r_even_t[...])
     far_odd[...] = dot(y_odd[...], r_odd_t[...])
 
@@ -359,7 +359,7 @@
                     put_left(x, i * CH + k * HALF, slice(m * PS + HALF, (m + 1) * PS), diff[:, part])
         return carry
 
-    lax.fori_loop(0, HALF // CH, backward_cols, 0, unroll=UNROLL)
+    lax.fori_loop(0, HALF // CH, backward_cols, 0, unroll=8)
     half_even[...] = dot(l_even_t[...], x_even[...])
     half_odd[...] = dot(l_odd_t[...], x_odd[...])
 
@@ -392,7 +392,7 @@
 
     shifted[:, 0:8, :] = jnp.zeros((2, 8, PS), F32)
     shifted[:, 264:272, :] = jnp.zeros((2, 8, PS), F32)
-    lax.fori_loop(0, HALF // CH, outputs, 0, unroll=UNROLL)
+    lax.fori_loop(0, HALF // CH, outputs, 0, unroll=8)
 
     def emit(i, carry):
         rows = pl.ds(pl.multiple_of(i * CH, CH), 32)
@@ -483,17 +483,18 @@
         [pl.BlockSpec(memory_space=pltpu.HBM)] * 5,
         scratch=[
             pltpu.VMEM((BH, PS), F32),
-            [pltpu.SMEM((n,), jnp.int32) for n in (2, 2, 2, 1)],
+            [pltpu.SMEM(shape, jnp.int32) for shape in ((2,), (2,), (2,), (1, 1))],
             pltpu.SemaphoreType.DMA((5,)),
         ],
         vmem=60,
-    )(anchors.reshape(-1), row_offset, col_offset, live_counts, object_field)
-    probe_other = swap(probe_modes)
+    )(anchors.reshape(-1), row_offset, col_offset, live_counts.reshape(1, 1), object_field)
     high = exchange(high)
     amp = call(order_kernel, arr((PS, PS), F32), [VM, VM])(jnp.asarray(order_table()), amplitudes)
     high, amp = lax.optimization_barrier((high, amp))
     meta = high[:, HALO, 0:8].astype(jnp.int32)
     windows, denom = call(window_kernel, (arr((2 * N_TM, CH, PS), BF16), denom_shape), [SM, VM])(meta, high)
+    windows, own = lax.optimization_barrier((windows, probe_modes))
+    probe_other = swap(own)
     h_own = h_oth = lax.all_to_all(windows, ("tm", "mode"), 0, 0)
 
     for iteration in range(2):

time: 140 us -> 139 us (level)
  blocking collectives: 77.1 us -> 75.4 us
  starting transfers between devices: 25.3 us -> 26.8 us
    all_to_all x1, blocking collectives: 14.2 us -> 12.6 us  [body(): h_own = h_oth = lax.all_to_all(windows, ('tm', 'mode'), 0, 0)]
  transfers between devices with their start and end apart: 12 -> 12, of which waited for: 9 -> 9; matrix products, arithmetic and copies ran while one was open for 0% -> 0% of each run, Pallas kernels for 7% -> 5%
where the time goes in v1:
time: 139 us; the launch traced here: 138 us
  blocking collectives  75.4 us (54%)
  starting transfers between devices  26.8 us (19%)
  Pallas kernels  18.6 us (13%)
  waiting for transfers between devices  15.9 us (11%)
  between operations  1.49 us (1%)
    all_to_all x4, blocking collectives, exchange(): return lax.all_to_all(x, 'tm', 0, 0)  62.8 us
    all_to_all x1, blocking collectives, body(): h_own = h_oth = lax.all_to_all(windows, ('tm', 'mode'), 0, 0)  12.6 us
    ppermute x5, starting transfers between devices, swap(): return lax.ppermute(x, 'mode', SWAP)  12.4 us
    all_to_all x1, starting transfers between devices, exchange(): return lax.all_to_all(x, 'tm', 0, 0)  8.74 us
    pallas_call x2, Pallas kernels, position(): call(functools.partial(position_kernel, with_update), (part, part, arr((2...  7.49 us
    all_to_all x1, waiting for transfers between devices, exchange(): return lax.all_to_all(x, 'tm', 0, 0)  6.96 us
    ppermute x6, starting transfers between devices, over_tiles(): lax.ppermute(x, 'tile', [(i, (i + k) % n) for i in range(n)])  5.64 us
    ppermute x6, waiting for transfers between devices, over_tiles(): lax.ppermute(x, 'tile', [(i, (i + k) % n) for i in range(n)])  4.54 us
  transfers between devices with their start and end apart: 12, of which 9 were waited for; matrix products, arithmetic and copies ran while one was open for 0% of the time, Pallas kernels for 5%

profile of v1, /device:TPU:1, one launch (start us, length us, event | category | flops | bytes accessed | tf_op | source)
XLA Modules:
  0.0 138.3 jit_solution(751387558613174573)
XLA Ops:
  1.3 1.8 %shard_map.167 = bf16[16,32,256]{2,1,0:T(8,128)(2,1)} custom-call(s32[2]{0:T(128)} %bitcast.11, s32[2]{0:T(128)} %row_offset.1, s32[2]{0:T(128)} %col_offset.1, s32[1,1]{1,0:T(1,128)} %bitcast.3.live_counts, f32[2,264,256]{2,1,0:T(8,128)} %obj.3), custom_call_target="tpu_custom_call" | custom-call | bytes 1048576 | tf_op jit(solution)/shard_map/pallas_call | solution.py:480
  3.1 8.7 %all-to-all-start = ((bf16[16,32,256]{2,1,0:T(8,128)(2,1)}), bf16[16,32,256]{2,1,0:T(8,128)(2,1)S(1)}, u32[]{:S(2)}, u32[]{:S(2)}) async-start(bf16[16,32,256]{2,1,0:T(8,128)(2,1)} %shard_map.167), calls=%async_computation | async-start | bytes 524288 | tf_op jit(solution)/shard_map/all_to_all | solution.py:468
  12.4 7.0 %all-to-all-done.high = bf16[16,32,256]{2,1,0:T(8,128)(2,1)S(1)} async-done(((bf16[16,32,256]{2,1,0:T(8,128)(2,1)}), bf16[16,32,256]{2,1,0:T(8,128)(2,1)S(1)}, u32[]{:S(2)}, u32[]{:S(2)}) %all-to-all-start) | async-done | bytes 262176 | tf_op jit(solution)/shard_map/all_to_all | solution.py:468
  19.3 1.3 shard_map.169
  20.7 2.1 %collective-permute-start = (f32[2,2,256,256]{3,2,1,0:T(8,128)S(1)}, f32[2,2,256,256]{3,2,1,0:T(8,128)S(1)}, u32[]{:S(2)}, u32[]{:S(2)}) collective-permute-start(f32[2,2,256,256]{3,2,1,0:T(8,128)S(1)} %copy-done), channel_id=1, source_target_pairs={{0,1},{1,0},{2,3},{3,2},{4,5},{5,4},{6,7},{7,6},{8,9},{9,8},{10,11... | collective-permute-start | bytes 3145736 | tf_op jit(solution)/shard_map/ppermute | solution.py:471
  22.8 12.6 %all_to_all.30.h_own.h_oth = bf16[32,16,256]{2,1,0:T(8,128)(2,1)S(1)} all-to-all(bf16[32,16,256]{2,1,0:T(8,128)(2,1)S(1)} %get-tuple-element.28), channel_id=1, replica_groups=mesh['tile'=4,'tm'=16,'mode'=2] {'tm','mode'}, dimensions={0} | all-to-all | bytes 524288 | tf_op jit(solution)/shard_map/all_to_all | solution.py:498
  35.4 3.7 %shard_map.170 = (bf16[16,96,256]{2,1,0:T(8,128)(2,1)S(1)}, bf16[16,96,256]{2,1,0:T(8,128)(2,1)S(1)}, f32[272,256]{1,0:T(8,128)S(1)}) custom-call(s32[16,8]{1,0:T(8,128)S(1)} %bitcast.5, bf16[256,256]{1,0:T(8,128)(2,1)S(1)} %copy-done.5, bf16[256,256]{1,0:T(8,128)(2,1)S(1)} %copy-done.4, bf16[256,256]{1,0:T(8,128)(2,1)S(1)} %copy-done.3, ...), custom_call_target="tpu_custom_call" | custom-call | flops 1073741824 | bytes 10485760 | tf_op jit(solution)/shard_map/pallas_call | solution.py:413
  39.4 1.1 shard_map.171.scale
  40.5 1.0 collective-permute-done.1.recv
  41.7 16.8 %all_to_all.31.parts = bf16[16,112,256]{2,1,0:T(8,128)(2,1)S(1)} all-to-all(bf16[16,112,256]{2,1,0:T(8,128)(2,1)S(1)} %get-tuple-element.35), channel_id=1, replica_groups=mesh['tile'=4,'tm'=16,'mode'=2] {'tm'}, dimensions={0} | all-to-all | bytes 1835008 | tf_op jit(solution)/shard_map/all_to_all | solution.py:468
  58.7 2.5 %collective-permute-start.4 = (bf16[80,256]{1,0:T(8,128)(2,1)S(1)}, bf16[80,256]{1,0:T(8,128)(2,1)S(1)}, u32[]{:S(2)}, u32[]{:S(2)}) collective-permute-start(bf16[80,256]{1,0:T(8,128)(2,1)S(1)} %shard_map.173.own), channel_id=1, source_target_pairs={{0,96},{32,0},{64,32},{96,64},{1,97},{33,1},{65,33},{97,65},{2,98}... | collective-permute-start | bytes 122888 | tf_op jit(solution)/shard_map/ppermute | solution.py:475
  62.3 1.6 %shard_map.174 = (bf16[16,32,256]{2,1,0:T(8,128)(2,1)S(1)}, f32[16,256]{1,0:T(8,128)S(1)}, f32[16,24,256]{2,1,0:T(8,128)S(1)}) custom-call(s32[16,8]{1,0:T(8,128)S(1)} %bitcast.7, bf16[16,112,256]{2,1,0:T(8,128)(2,1)S(1)} %all_to_all.31.parts, f32[16,24,256]{2,1,0:T(8,128)S(1)} %shard_map.171.scale, bf16[16,32,256]{2,1,0:T(8,128)(2,1)S(1)} %all-to-all-done.high), custom_call_target="tpu_custom_call" | custom-call | bytes 1048576 | tf_op jit(solution)/shard_map/pallas_call | solution.py:516
  63.9 1.7 %collective-permute-done.3.two = bf16[80,256]{1,0:T(8,128)(2,1)S(1)} collective-permute-done((bf16[80,256]{1,0:T(8,128)(2,1)S(1)}, bf16[80,256]{1,0:T(8,128)(2,1)S(1)}, u32[]{:S(2)}, u32[]{:S(2)}) %collective-permute-start.3) | collective-permute-done | bytes 40992 | tf_op jit(solution)/shard_map/ppermute | solution.py:475
  66.1 14.4 %all_to_all.32.h_own.h_one = bf16[16,96,256]{2,1,0:T(8,128)(2,1)S(1)} all-to-all(bf16[16,96,256]{2,1,0:T(8,128)(2,1)S(1)} %shard_map.175), channel_id=1, replica_groups=mesh['tile'=4,'tm'=16,'mode'=2] {'tm'}, dimensions={0} | all-to-all | bytes 1572864 | tf_op jit(solution)/shard_map/all_to_all | solution.py:468
  80.5 4.7 %collective-permute-start.5 = (bf16[16,96,256]{2,1,0:T(8,128)(2,1)S(1)}, bf16[16,96,256]{2,1,0:T(8,128)(2,1)S(1)}, u32[]{:S(2)}, u32[]{:S(2)}) collective-permute-start(bf16[16,96,256]{2,1,0:T(8,128)(2,1)S(1)} %all_to_all.32.h_own.h_one), channel_id=1, source_target_pairs={{0,1},{1,0},{2,3},{3,2},{4,5},{5,4},{6,7},{7,6},{8,9},{9,8},{10,11... | collective-permute-start | bytes 2359304 | tf_op jit(solution)/shard_map/ppermute | solution.py:471
  85.2 1.9 %collective-permute-done.5.h_oth = bf16[16,96,256]{2,1,0:T(8,128)(2,1)S(1)} collective-permute-done((bf16[16,96,256]{2,1,0:T(8,128)(2,1)S(1)}, bf16[16,96,256]{2,1,0:T(8,128)(2,1)S(1)}, u32[]{:S(2)}, u32[]{:S(2)}) %collective-permute-start.5) | collective-permute-done | bytes 786464 | tf_op jit(solution)/shard_map/ppermute | solution.py:471
  87.1 3.8 %shard_map.176 = (bf16[16,96,256]{2,1,0:T(8,128)(2,1)S(1)}, bf16[16,96,256]{2,1,0:T(8,128)(2,1)S(1)}, f32[272,256]{1,0:T(8,128)S(1)}) custom-call(s32[16,8]{1,0:T(8,128)S(1)} %bitcast.8, bf16[256,256]{1,0:T(8,128)(2,1)S(1)} %copy-done.5, bf16[256,256]{1,0:T(8,128)(2,1)S(1)} %copy-done.4, bf16[256,256]{1,0:T(8,128)(2,1)S(1)} %copy-done.3, ...), custom_call_target="tpu_custom_call" | custom-call | flops 1073741824 | bytes 10485760 | tf_op jit(solution)/shard_map/pallas_call | solution.py:413
  91.5 1.1 shard_map.177.scale
  93.6 17.2 %all_to_all.33.parts = bf16[16,112,256]{2,1,0:T(8,128)(2,1)S(1)} all-to-all(bf16[16,112,256]{2,1,0:T(8,128)(2,1)S(1)} %get-tuple-element.44), channel_id=1, replica_groups=mesh['tile'=4,'tm'=16,'mode'=2] {'tm'}, dimensions={0} | all-to-all | bytes 1835008 | tf_op jit(solution)/shard_map/all_to_all | solution.py:468
  113.0 1.0 shard_map.180.objs
  113.9 1.9 %collective-permute-done.8.two = bf16[80,256]{1,0:T(8,128)(2,1)S(1)} collective-permute-done((bf16[80,256]{1,0:T(8,128)(2,1)S(1)}, bf16[80,256]{1,0:T(8,128)(2,1)S(1)}, u32[]{:S(2)}, u32[]{:S(2)}) %collective-permute-start.8) | collective-permute-done | bytes 40992 | tf_op jit(solution)/shard_map/ppermute | solution.py:475
  116.5 14.4 %all_to_all.34.h_own.h_two = bf16[16,96,256]{2,1,0:T(8,128)(2,1)S(1)} all-to-all(bf16[16,96,256]{2,1,0:T(8,128)(2,1)S(1)} %shard_map.181), channel_id=1, replica_groups=mesh['tile'=4,'tm'=16,'mode'=2] {'tm'}, dimensions={0} | all-to-all | bytes 1572864 | tf_op jit(solution)/shard_map/all_to_all | solution.py:468
  130.8 4.7 %collective-permute-start.10 = (bf16[16,96,256]{2,1,0:T(8,128)(2,1)S(1)}, bf16[16,96,256]{2,1,0:T(8,128)(2,1)S(1)}, u32[]{:S(2)}, u32[]{:S(2)}) collective-permute-start(bf16[16,96,256]{2,1,0:T(8,128)(2,1)S(1)} %all_to_all.34.h_own.h_two), channel_id=1, source_target_pairs={{0,1},{1,0},{2,3},{3,2},{4,5},{5,4},{6,7},{7,6},{8,9},{9,8},{10,11... | collective-permute-start | bytes 2359304 | tf_op jit(solution)/shard_map/ppermute | solution.py:471
  135.6 1.2 shard_map.183
  (39 shorter events, 8.7 us)
Async XLA Ops:
  1.3 10.6 %copy-start.6 = (f32[2,256,256]{2,1,0:T(8,128)S(1)}, f32[2,256,256]{2,1,0:T(8,128)}, u32[]{:S(2)}) copy-start(f32[2,256,256]{2,1,0:T(8,128)} %amp.1) | copy-start | bytes 1572868
  1.3 10.6 %copy-start.7 = (bf16[256,256]{1,0:T(8,128)(2,1)S(1)}, bf16[256,256]{1,0:T(8,128)(2,1)}, u32[]{:S(2)}) copy-start(bf16[256,256]{1,0:T(8,128)(2,1)} %constant.14.clone.table) | copy-start | bytes 393220
  3.1 17.5 %copy-start = (f32[2,2,256,256]{3,2,1,0:T(8,128)S(1)}, f32[2,2,256,256]{3,2,1,0:T(8,128)}, u32[]{:S(2)}) copy-start(f32[2,2,256,256]{3,2,1,0:T(8,128)} %p_own.5) | copy-start | bytes 3145732
  3.1 16.2 %all-to-all-start = ((bf16[16,32,256]{2,1,0:T(8,128)(2,1)}), bf16[16,32,256]{2,1,0:T(8,128)(2,1)S(1)}, u32[]{:S(2)}, u32[]{:S(2)}) async-start(bf16[16,32,256]{2,1,0:T(8,128)(2,1)} %shard_map.167), calls=%async_computation | async-start | bytes 524288 | tf_op jit(solution)/shard_map/all_to_all | solution.py:468
  20.6 14.8 %copy-start.2 = (bf16[256,256]{1,0:T(8,128)(2,1)S(1)}, bf16[256,256]{1,0:T(8,128)(2,1)}, u32[]{:S(2)}) copy-start(bf16[256,256]{1,0:T(8,128)(2,1)} %constant.13.clone.l_odd_t.r_odd_t) | copy-start | bytes 393220
  20.6 14.8 %copy-start.3 = (bf16[256,256]{1,0:T(8,128)(2,1)S(1)}, bf16[256,256]{1,0:T(8,128)(2,1)}, u32[]{:S(2)}) copy-start(bf16[256,256]{1,0:T(8,128)(2,1)} %constant.12.clone.l_odd.r_odd) | copy-start | bytes 393220
  20.6 14.7 %copy-start.4 = (bf16[256,256]{1,0:T(8,128)(2,1)S(1)}, bf16[256,256]{1,0:T(8,128)(2,1)}, u32[]{:S(2)}) copy-start(bf16[256,256]{1,0:T(8,128)(2,1)} %constant.11.clone.l_even_t.r_even_t) | copy-start | bytes 393220
  20.7 14.7 %copy-start.5 = (bf16[256,256]{1,0:T(8,128)(2,1)S(1)}, bf16[256,256]{1,0:T(8,128)(2,1)}, u32[]{:S(2)}) copy-start(bf16[256,256]{1,0:T(8,128)(2,1)} %constant.10.clone.l_even.r_even) | copy-start | bytes 393220
  20.7 14.7 %collective-permute-start = (f32[2,2,256,256]{3,2,1,0:T(8,128)S(1)}, f32[2,2,256,256]{3,2,1,0:T(8,128)S(1)}, u32[]{:S(2)}, u32[]{:S(2)}) collective-permute-start(f32[2,2,256,256]{3,2,1,0:T(8,128)S(1)} %copy-done), channel_id=1, source_target_pairs={{0,1},{1,0},{2,3},{3,2},{4,5},{5,4},{6,7},{7,6},{8,9},{9,8},{10,11... | collective-permute-start | bytes 3145736 | tf_op jit(solution)/shard_map/ppermute | solution.py:471
  39.1 2.4 %collective-permute-start.1 = (bf16[16,96,256]{2,1,0:T(8,128)(2,1)S(1)}, bf16[16,96,256]{2,1,0:T(8,128)(2,1)S(1)}, u32[]{:S(2)}, u32[]{:S(2)}) collective-permute-start(bf16[16,96,256]{2,1,0:T(8,128)(2,1)S(1)} %get-tuple-element.32), channel_id=1, source_target_pairs={{0,1},{1,0},{2,3},{3,2},{4,5},{5,4},{6,7},{7,6},{8,9},{9,8},{10,11... | collective-permute-start | bytes 2359304 | tf_op jit(solution)/shard_map/ppermute | solution.py:471
  58.7 5.3 %collective-permute-start.4 = (bf16[80,256]{1,0:T(8,128)(2,1)S(1)}, bf16[80,256]{1,0:T(8,128)(2,1)S(1)}, u32[]{:S(2)}, u32[]{:S(2)}) collective-permute-start(bf16[80,256]{1,0:T(8,128)(2,1)S(1)} %shard_map.173.own), channel_id=1, source_target_pairs={{0,96},{32,0},{64,32},{96,64},{1,97},{33,1},{65,33},{97,65},{2,98}... | collective-permute-start | bytes 122888 | tf_op jit(solution)/shard_map/ppermute | solution.py:475
  61.2 4.4 %collective-permute-start.3 = (bf16[80,256]{1,0:T(8,128)(2,1)S(1)}, bf16[80,256]{1,0:T(8,128)(2,1)S(1)}, u32[]{:S(2)}, u32[]{:S(2)}) collective-permute-start(bf16[80,256]{1,0:T(8,128)(2,1)S(1)} %shard_map.173.own), channel_id=1, source_target_pairs={{0,64},{32,96},{64,0},{96,32},{1,65},{33,97},{65,1},{97,33},{2,66}... | collective-permute-start | bytes 122888 | tf_op jit(solution)/shard_map/ppermute | solution.py:475
  61.7 4.3 %collective-permute-start.2 = (bf16[80,256]{1,0:T(8,128)(2,1)S(1)}, bf16[80,256]{1,0:T(8,128)(2,1)S(1)}, u32[]{:S(2)}, u32[]{:S(2)}) collective-permute-start(bf16[80,256]{1,0:T(8,128)(2,1)S(1)} %shard_map.173.own), channel_id=1, source_target_pairs={{0,32},{32,64},{64,96},{96,0},{1,33},{33,65},{65,97},{97,1},{2,34}... | collective-permute-start | bytes 122888 | tf_op jit(solution)/shard_map/ppermute | solution.py:475
  80.5 6.6 %collective-permute-start.5 = (bf16[16,96,256]{2,1,0:T(8,128)(2,1)S(1)}, bf16[16,96,256]{2,1,0:T(8,128)(2,1)S(1)}, u32[]{:S(2)}, u32[]{:S(2)}) collective-permute-start(bf16[16,96,256]{2,1,0:T(8,128)(2,1)S(1)} %all_to_all.32.h_own.h_one), channel_id=1, source_target_pairs={{0,1},{1,0},{2,3},{3,2},{4,5},{5,4},{6,7},{7,6},{8,9},{9,8},{10,11... | collective-permute-start | bytes 2359304 | tf_op jit(solution)/shard_map/ppermute | solution.py:471
  90.9 2.5 %collective-permute-start.6 = (bf16[16,96,256]{2,1,0:T(8,128)(2,1)S(1)}, bf16[16,96,256]{2,1,0:T(8,128)(2,1)S(1)}, u32[]{:S(2)}, u32[]{:S(2)}) collective-permute-start(bf16[16,96,256]{2,1,0:T(8,128)(2,1)S(1)} %get-tuple-element.41), channel_id=1, source_target_pairs={{0,1},{1,0},{2,3},{3,2},{4,5},{5,4},{6,7},{7,6},{8,9},{9,8},{10,11... | collective-permute-start | bytes 2359304 | tf_op jit(solution)/shard_map/ppermute | solution.py:471
  111.0 2.9 %collective-permute-start.9 = (bf16[80,256]{1,0:T(8,128)(2,1)S(1)}, bf16[80,256]{1,0:T(8,128)(2,1)S(1)}, u32[]{:S(2)}, u32[]{:S(2)}) collective-permute-start(bf16[80,256]{1,0:T(8,128)(2,1)S(1)} %shard_map.179.own), channel_id=1, source_target_pairs={{0,96},{32,0},{64,32},{96,64},{1,97},{33,1},{65,33},{97,65},{2,98}... | collective-permute-start | bytes 122888 | tf_op jit(solution)/shard_map/ppermute | solution.py:475
  111.5 4.4 %collective-permute-start.8 = (bf16[80,256]{1,0:T(8,128)(2,1)S(1)}, bf16[80,256]{1,0:T(8,128)(2,1)S(1)}, u32[]{:S(2)}, u32[]{:S(2)}) collective-permute-start(bf16[80,256]{1,0:T(8,128)(2,1)S(1)} %shard_map.179.own), channel_id=1, source_target_pairs={{0,64},{32,96},{64,0},{96,32},{1,65},{33,97},{65,1},{97,33},{2,66}... | collective-permute-start | bytes 122888 | tf_op jit(solution)/shard_map/ppermute | solution.py:475
  112.3 4.1 %collective-permute-start.7 = (bf16[80,256]{1,0:T(8,128)(2,1)S(1)}, bf16[80,256]{1,0:T(8,128)(2,1)S(1)}, u32[]{:S(2)}, u32[]{:S(2)}) collective-permute-start(bf16[80,256]{1,0:T(8,128)(2,1)S(1)} %shard_map.179.own), channel_id=1, source_target_pairs={{0,32},{32,64},{64,96},{96,0},{1,33},{33,65},{65,97},{97,1},{2,34}... | collective-permute-start | bytes 122888 | tf_op jit(solution)/shard_map/ppermute | solution.py:475
  130.8 6.7 %copy-start.1 = (f32[2,264,256]{2,1,0:T(8,128)S(1)}, f32[2,264,256]{2,1,0:T(8,128)}, u32[]{:S(2)}) copy-start(f32[2,264,256]{2,1,0:T(8,128)} %obj.3) | copy-start | bytes 1622020
  130.8 6.6 %collective-permute-start.10 = (bf16[16,96,256]{2,1,0:T(8,128)(2,1)S(1)}, bf16[16,96,256]{2,1,0:T(8,128)(2,1)S(1)}, u32[]{:S(2)}, u32[]{:S(2)}) collective-permute-start(bf16[16,96,256]{2,1,0:T(8,128)(2,1)S(1)} %all_to_all.34.h_own.h_two), channel_id=1, source_target_pairs={{0,1},{1,0},{2,3},{3,2},{4,5},{5,4},{6,7},{7,6},{8,9},{9,8},{10,11... | collective-permute-start | bytes 2359304 | tf_op jit(solution)/shard_map/ppermute | solution.py:471

commit v2 on v1

--- a/solution.py
+++ b/solution.py
@@ -11,7 +11,7 @@
 
 PS = 256
 HALF = 128
-PARTS = 1
+PARTS = 3
 BH = 264
 N_TM = 16
 UNROLL = 16
@@ -39,14 +39,11 @@
 
 def dft_tables():
     n = np.arange(HALF)
-    left, right = [], []
+    parts = []
     for k in (2 * n, 2 * n + 1):
         table = real_form(np.exp(-2j * np.pi * ((k[:, None] * n[None, :]) % PS) / PS) / np.sqrt(PS))
-        for form in (table, np.ascontiguousarray(table.T)):
-            high, low = halves(form)
-            left.append(np.concatenate([high, low][:PARTS], axis=1))
-            right.append(np.concatenate([high, low][:PARTS], axis=0))
-    return left + right
+        parts += [halves(table), halves(table.T)]
+    return np.stack([np.stack([p[k] for p in parts]) for k in range(min(PARTS, 2))])
 
 
 def order_table():
@@ -243,21 +240,31 @@
     denom_out[...] = (denom[...] + jnp.concatenate(theirs, axis=0)).astype(BF16)
 
 
+def parts_of(value):
+    high, low = split(value)
+    return (high, low, high)[:PARTS]
+
+
 def put_left(ref, row, cols, value):
-    for k in range(PARTS):
-        ref[pl.ds(pl.multiple_of(row + k * PS, CH), CH), cols] = value.astype(BF16)
+    for k, part in enumerate(parts_of(value)):
+        ref[pl.ds(pl.multiple_of(row + k * PS, CH), CH), cols] = part
 
 
 def put_right(ref, rows, lane, value):
-    for k in range(PARTS):
-        ref[rows, lane + k * PS : lane + k * PS + HALF] = value.astype(BF16)
+    for k, part in enumerate(parts_of(value)):
+        ref[rows, lane + k * PS : lane + k * PS + HALF] = part
 
 
 def position_kernel(
-    with_update, meta,
-    l_even, l_even_t, l_odd, l_odd_t, r_even, r_even_t, r_odd, r_odd_t, p_own, p_oth, h_own, h_oth, amp, denom,
+    with_update, meta, tables, p_own, p_oth, h_own, h_oth, amp, denom,
     keep, send, power, obj, probe, x_even, x_odd, y_even, y_odd, half_even, half_odd, far_even, far_odd, shifted,
+    left, right,
 ):
+    for k in range(4):
+        for part, which in enumerate((0, 0, 1)[:PARTS]):
+            left[k, :, part * PS : (part + 1) * PS] = tables[which, k]
+            right[k, part * PS : (part + 1) * PS, :] = tables[which, k]
+    even, even_t, odd, odd_t = range(4)
     core = lax.axis_index("mode")
     first = core == 0
     col, row, alive = (meta[lax.axis_index("tm"), 4 * core + k] for k in (1, 2, 3))
@@ -313,8 +320,8 @@
         return carry
 
     lax.fori_loop(0, HALF // CH, forward_rows, 0, unroll=8)
-    half_even[...] = dot(l_even[...], x_even[...])
-    half_odd[...] = dot(l_odd[...], x_odd[...])
+    half_even[...] = dot(left[even], x_even[...])
+    half_odd[...] = dot(left[odd], x_odd[...])
 
     def forward_cols(i, carry):
         for m in range(4):
@@ -327,8 +334,8 @@
         return carry
 
     lax.fori_loop(0, HALF // CH, forward_cols, 0, unroll=8)
-    far_even[...] = dot(y_even[...], r_even_t[...])
-    far_odd[...] = dot(y_odd[...], r_odd_t[...])
+    far_even[...] = dot(y_even[...], right[even_t])
+    far_odd[...] = dot(y_odd[...], right[odd_t])
 
     def rescale(i, carry):
         for b, (far, y) in enumerate(((far_even, y_even), (far_odd, y_odd))):
@@ -344,15 +351,15 @@
         return carry
 
     lax.fori_loop(0, N_TM, rescale, 0, unroll=UNROLL)
-    far_even[...] = dot(y_even[...], r_even[...])
-    far_odd[...] = dot(y_odd[...], r_odd[...])
+    far_even[...] = dot(y_even[...], right[even])
+    far_odd[...] = dot(y_odd[...], right[odd])
 
     def backward_cols(i, carry):
         for m in range(4):
             for b, x in enumerate((x_even, x_odd)):
                 rows = rows_of(i, m * PS + b * HALF)
-                even, odd = far_even[rows, :], far_odd[rows, :]
-                total, diff = even + odd, even - odd
+                one, two = far_even[rows, :], far_odd[rows, :]
+                total, diff = one + two, one - two
                 for k in range(2):
                     part = slice(k * HALF, (k + 1) * HALF)
                     put_left(x, i * CH + k * HALF, slice(m * PS, m * PS + HALF), total[:, part])
@@ -360,8 +367,8 @@
         return carry
 
     lax.fori_loop(0, HALF // CH, backward_cols, 0, unroll=8)
-    half_even[...] = dot(l_even_t[...], x_even[...])
-    half_odd[...] = dot(l_odd_t[...], x_odd[...])
+    half_even[...] = dot(left[even_t], x_even[...])
+    half_odd[...] = dot(left[odd_t], x_odd[...])
 
     def outputs(i, carry):
         for s in range(2):
@@ -375,8 +382,8 @@
                     res = []
                     for k in range(2):
                         at = rows_of(i, k * HALF)
-                        even, odd = half_even[at, mode_cols(m)], half_odd[at, mode_cols(m)]
-                        res.append(even + odd if s == 0 else even - odd)
+                        one, two = half_even[at, mode_cols(m)], half_odd[at, mode_cols(m)]
+                        res.append(one + two if s == 0 else one - two)
                     dr, di = res[0] * alive, res[1] * alive
                     chunk = i + s * (HALF // CH)
                     target[chunk, 2 * mm * CH : (2 * mm + 1) * CH, :] = (o_r * dr + o_i * di).astype(BF16)
@@ -413,7 +420,7 @@
     return call(
         functools.partial(position_kernel, with_update),
         (part, part, arr((272, PS), F32)),
-        [SM] + [VM] * 14,
+        [SM] + [VM] * 7,
         scratch=[
             pltpu.VMEM((2, PS, PS), F32),
             pltpu.VMEM((4, 2, PS, PS), F32),
@@ -426,10 +433,12 @@
             pltpu.VMEM((4 * PS, PS), F32),
             pltpu.VMEM((4 * PS, PS), F32),
             pltpu.VMEM((2, 272, PS), F32),
+            pltpu.VMEM((4, PS, PARTS * PS), BF16),
+            pltpu.VMEM((4, PARTS * PS, PS), BF16),
         ],
         flops=32 * PARTS * 2 * 256 * 256 * 256,
         nbytes=10 << 20,
-        vmem=24,
+        vmem=32,
     )(*args)
 
 
@@ -462,7 +471,7 @@
 
 
 def body(object_field, probe_modes, amplitudes, anchors, row_offset, col_offset, live_counts):
-    tables = [jnp.asarray(t) for t in dft_tables()]
+    tables = jnp.asarray(dft_tables())
 
     def exchange(x):
         return lax.all_to_all(x, "tm", 0, 0)
@@ -501,7 +510,7 @@
         if iteration > 0:
             h_oth = swap(h_own)
         keep, send, power = position(
-            iteration > 0, meta, *tables, probe_modes, probe_other, h_own, h_oth, amp, denom
+            iteration > 0, meta, tables, probe_modes, probe_other, h_own, h_oth, amp, denom
         )
         recv = swap(send)
         scale = call(weight_kernel, arr(chunk, F32), [SM, VM])(meta, power)

time: 139 us -> 144 us (1.036)
  Pallas kernels: 18.6 us -> 24.1 us
    pallas_call x2, Pallas kernels: 7.49 us -> 13 us  [position(): call(functools.partial(position_kernel, with_update), (part, part, arr((2...]
  transfers between devices with their start and end apart: 12 -> 12, of which waited for: 9 -> 9; matrix products, arithmetic and copies ran while one was open for 0% -> 0% of each run, Pallas kernels for 5% -> 4%
where the time goes in v2:
time: 144 us
  blocking collectives  75.4 us (52%)
  starting transfers between devices  26.6 us (18%)
  Pallas kernels  24.1 us (17%)
  waiting for transfers between devices  15.9 us (11%)
  between operations  1.45 us (1%)
    all_to_all x4, blocking collectives, exchange(): return lax.all_to_all(x, 'tm', 0, 0)  62.8 us
    pallas_call x2, Pallas kernels, position(): call(functools.partial(position_kernel, with_update), (part, part, arr((2...  13 us
    all_to_all x1, blocking collectives, body(): h_own = h_oth = lax.all_to_all(windows, ('tm', 'mode'), 0, 0)  12.6 us
    ppermute x5, starting transfers between devices, swap(): return lax.ppermute(x, 'mode', SWAP)  12.3 us
    all_to_all x1, starting transfers between devices, exchange(): return lax.all_to_all(x, 'tm', 0, 0)  8.74 us
    all_to_all x1, waiting for transfers between devices, exchange(): return lax.all_to_all(x, 'tm', 0, 0)  6.96 us
    ppermute x6, starting transfers between devices, over_tiles(): lax.ppermute(x, 'tile', [(i, (i + k) % n) for i in range(n)])  5.64 us
    ppermute x6, waiting for transfers between devices, over_tiles(): lax.ppermute(x, 'tile', [(i, (i + k) % n) for i in range(n)])  4.52 us
  transfers between devices with their start and end apart: 12, of which 9 were waited for; matrix products, arithmetic and copies ran while one was open for 0% of the time, Pallas kernels for 4%

profile of v2, /device:TPU:1, one launch (start us, length us, event | category | flops | bytes accessed | tf_op | source)
XLA Modules:
  0.0 143.6 jit_solution(13249718909587312231)
XLA Ops:
  1.3 1.8 %shard_map.104 = bf16[16,32,256]{2,1,0:T(8,128)(2,1)} custom-call(s32[2]{0:T(128)} %bitcast.11, s32[2]{0:T(128)} %row_offset.1, s32[2]{0:T(128)} %col_offset.1, s32[1,1]{1,0:T(1,128)} %bitcast.3.live_counts, f32[2,264,256]{2,1,0:T(8,128)} %obj.3), custom_call_target="tpu_custom_call" | custom-call | bytes 1048576 | tf_op jit(solution)/shard_map/pallas_call | solution.py:489
  3.1 8.7 %all-to-all-start = ((bf16[16,32,256]{2,1,0:T(8,128)(2,1)}), bf16[16,32,256]{2,1,0:T(8,128)(2,1)S(1)}, u32[]{:S(2)}, u32[]{:S(2)}) async-start(bf16[16,32,256]{2,1,0:T(8,128)(2,1)} %shard_map.104), calls=%async_computation | async-start | bytes 524288 | tf_op jit(solution)/shard_map/all_to_all | solution.py:477
  12.4 7.0 %all-to-all-done.high = bf16[16,32,256]{2,1,0:T(8,128)(2,1)S(1)} async-done(((bf16[16,32,256]{2,1,0:T(8,128)(2,1)}), bf16[16,32,256]{2,1,0:T(8,128)(2,1)S(1)}, u32[]{:S(2)}, u32[]{:S(2)}) %all-to-all-start) | async-done | bytes 262176 | tf_op jit(solution)/shard_map/all_to_all | solution.py:477
  19.3 1.3 shard_map.106
  20.6 2.1 %collective-permute-start = (f32[2,2,256,256]{3,2,1,0:T(8,128)S(1)}, f32[2,2,256,256]{3,2,1,0:T(8,128)S(1)}, u32[]{:S(2)}, u32[]{:S(2)}) collective-permute-start(f32[2,2,256,256]{3,2,1,0:T(8,128)S(1)} %copy-done.1), channel_id=1, source_target_pairs={{0,1},{1,0},{2,3},{3,2},{4,5},{5,4},{6,7},{7,6},{8,9},{9,8},{10,11... | collective-permute-start | bytes 3145736 | tf_op jit(solution)/shard_map/ppermute | solution.py:480
  22.7 12.6 %all_to_all.30.h_own.h_oth = bf16[32,16,256]{2,1,0:T(8,128)(2,1)S(1)} all-to-all(bf16[32,16,256]{2,1,0:T(8,128)(2,1)S(1)} %get-tuple-element.28), channel_id=1, replica_groups=mesh['tile'=4,'tm'=16,'mode'=2] {'tm','mode'}, dimensions={0} | all-to-all | bytes 524288 | tf_op jit(solution)/shard_map/all_to_all | solution.py:507
  35.3 6.5 %shard_map.107 = (bf16[16,96,256]{2,1,0:T(8,128)(2,1)S(1)}, bf16[16,96,256]{2,1,0:T(8,128)(2,1)S(1)}, f32[272,256]{1,0:T(8,128)S(1)}) custom-call(s32[16,8]{1,0:T(8,128)S(1)} %bitcast.5, bf16[2,4,256,256]{3,2,1,0:T(8,128)(2,1)S(1)} %copy-done.4, f32[2,2,256,256]{3,2,1,0:T(8,128)S(1)} %copy-done.1, f32[2,2,256,256]{3,2,1,0:T(8,128)S(1)} %collective-permute-done.p_oth, ...), custom_call_target="tpu_custom_call" | custom-call | flops 3221225472 | bytes 10485760 | tf_op jit(solution)/shard_map/pallas_call | solution.py:420
  42.0 1.1 shard_map.108.scale
  43.2 1.0 collective-permute-done.1.recv
  44.3 16.8 %all_to_all.31.parts = bf16[16,112,256]{2,1,0:T(8,128)(2,1)S(1)} all-to-all(bf16[16,112,256]{2,1,0:T(8,128)(2,1)S(1)} %get-tuple-element.35), channel_id=1, replica_groups=mesh['tile'=4,'tm'=16,'mode'=2] {'tm'}, dimensions={0} | all-to-all | bytes 1835008 | tf_op jit(solution)/shard_map/all_to_all | solution.py:477
  61.3 2.5 %collective-permute-start.4 = (bf16[80,256]{1,0:T(8,128)(2,1)S(1)}, bf16[80,256]{1,0:T(8,128)(2,1)S(1)}, u32[]{:S(2)}, u32[]{:S(2)}) collective-permute-start(bf16[80,256]{1,0:T(8,128)(2,1)S(1)} %shard_map.110.own), channel_id=1, source_target_pairs={{0,96},{32,0},{64,32},{96,64},{1,97},{33,1},{65,33},{97,65},{2,98}... | collective-permute-start | bytes 122888 | tf_op jit(solution)/shard_map/ppermute | solution.py:484
  65.0 1.6 %shard_map.111 = (bf16[16,32,256]{2,1,0:T(8,128)(2,1)S(1)}, f32[16,256]{1,0:T(8,128)S(1)}, f32[16,24,256]{2,1,0:T(8,128)S(1)}) custom-call(s32[16,8]{1,0:T(8,128)S(1)} %bitcast.7, bf16[16,112,256]{2,1,0:T(8,128)(2,1)S(1)} %all_to_all.31.parts, f32[16,24,256]{2,1,0:T(8,128)S(1)} %shard_map.108.scale, bf16[16,32,256]{2,1,0:T(8,128)(2,1)S(1)} %all-to-all-done.high), custom_call_target="tpu_custom_call" | custom-call | bytes 1048576 | tf_op jit(solution)/shard_map/pallas_call | solution.py:525
  66.6 1.6 %collective-permute-done.3.two = bf16[80,256]{1,0:T(8,128)(2,1)S(1)} collective-permute-done((bf16[80,256]{1,0:T(8,128)(2,1)S(1)}, bf16[80,256]{1,0:T(8,128)(2,1)S(1)}, u32[]{:S(2)}, u32[]{:S(2)}) %collective-permute-start.3) | collective-permute-done | bytes 40992 | tf_op jit(solution)/shard_map/ppermute | solution.py:484
  68.7 14.4 %all_to_all.32.h_own.h_one = bf16[16,96,256]{2,1,0:T(8,128)(2,1)S(1)} all-to-all(bf16[16,96,256]{2,1,0:T(8,128)(2,1)S(1)} %shard_map.112), channel_id=1, replica_groups=mesh['tile'=4,'tm'=16,'mode'=2] {'tm'}, dimensions={0} | all-to-all | bytes 1572864 | tf_op jit(solution)/shard_map/all_to_all | solution.py:477
  83.1 4.7 %collective-permute-start.5 = (bf16[16,96,256]{2,1,0:T(8,128)(2,1)S(1)}, bf16[16,96,256]{2,1,0:T(8,128)(2,1)S(1)}, u32[]{:S(2)}, u32[]{:S(2)}) collective-permute-start(bf16[16,96,256]{2,1,0:T(8,128)(2,1)S(1)} %all_to_all.32.h_own.h_one), channel_id=1, source_target_pairs={{0,1},{1,0},{2,3},{3,2},{4,5},{5,4},{6,7},{7,6},{8,9},{9,8},{10,11... | collective-permute-start | bytes 2359304 | tf_op jit(solution)/shard_map/ppermute | solution.py:480
  87.8 1.9 %collective-permute-done.5.h_oth = bf16[16,96,256]{2,1,0:T(8,128)(2,1)S(1)} collective-permute-done((bf16[16,96,256]{2,1,0:T(8,128)(2,1)S(1)}, bf16[16,96,256]{2,1,0:T(8,128)(2,1)S(1)}, u32[]{:S(2)}, u32[]{:S(2)}) %collective-permute-start.5) | collective-permute-done | bytes 786464 | tf_op jit(solution)/shard_map/ppermute | solution.py:480
  89.8 6.5 %shard_map.113 = (bf16[16,96,256]{2,1,0:T(8,128)(2,1)S(1)}, bf16[16,96,256]{2,1,0:T(8,128)(2,1)S(1)}, f32[272,256]{1,0:T(8,128)S(1)}) custom-call(s32[16,8]{1,0:T(8,128)S(1)} %bitcast.8, bf16[2,4,256,256]{3,2,1,0:T(8,128)(2,1)S(1)} %copy-done.4, f32[2,2,256,256]{3,2,1,0:T(8,128)S(1)} %copy-done.1, f32[2,2,256,256]{3,2,1,0:T(8,128)S(1)} %collective-permute-done.p_oth, ...), custom_call_target="tpu_custom_call" | custom-call | flops 3221225472 | bytes 10485760 | tf_op jit(solution)/shard_map/pallas_call | solution.py:420
  96.7 1.1 shard_map.114.scale
  98.8 17.2 %all_to_all.33.parts = bf16[16,112,256]{2,1,0:T(8,128)(2,1)S(1)} all-to-all(bf16[16,112,256]{2,1,0:T(8,128)(2,1)S(1)} %get-tuple-element.44), channel_id=1, replica_groups=mesh['tile'=4,'tm'=16,'mode'=2] {'tm'}, dimensions={0} | all-to-all | bytes 1835008 | tf_op jit(solution)/shard_map/all_to_all | solution.py:477
  118.2 1.0 shard_map.117.objs
  119.2 1.9 %collective-permute-done.8.two = bf16[80,256]{1,0:T(8,128)(2,1)S(1)} collective-permute-done((bf16[80,256]{1,0:T(8,128)(2,1)S(1)}, bf16[80,256]{1,0:T(8,128)(2,1)S(1)}, u32[]{:S(2)}, u32[]{:S(2)}) %collective-permute-start.8) | collective-permute-done | bytes 40992 | tf_op jit(solution)/shard_map/ppermute | solution.py:484
  121.7 14.4 %all_to_all.34.h_own.h_two = bf16[16,96,256]{2,1,0:T(8,128)(2,1)S(1)} all-to-all(bf16[16,96,256]{2,1,0:T(8,128)(2,1)S(1)} %shard_map.118), channel_id=1, replica_groups=mesh['tile'=4,'tm'=16,'mode'=2] {'tm'}, dimensions={0} | all-to-all | bytes 1572864 | tf_op jit(solution)/shard_map/all_to_all | solution.py:477
  136.1 4.7 %collective-permute-start.10 = (bf16[16,96,256]{2,1,0:T(8,128)(2,1)S(1)}, bf16[16,96,256]{2,1,0:T(8,128)(2,1)S(1)}, u32[]{:S(2)}, u32[]{:S(2)}) collective-permute-start(bf16[16,96,256]{2,1,0:T(8,128)(2,1)S(1)} %all_to_all.34.h_own.h_two), channel_id=1, source_target_pairs={{0,1},{1,0},{2,3},{3,2},{4,5},{5,4},{6,7},{7,6},{8,9},{9,8},{10,11... | collective-permute-start | bytes 2359304 | tf_op jit(solution)/shard_map/ppermute | solution.py:480
  140.8 1.1 shard_map.120
  (33 shorter events, 8.5 us)
Async XLA Ops:
  1.3 10.6 %copy-start.2 = (f32[2,256,256]{2,1,0:T(8,128)S(1)}, f32[2,256,256]{2,1,0:T(8,128)}, u32[]{:S(2)}) copy-start(f32[2,256,256]{2,1,0:T(8,128)} %amp.1) | copy-start | bytes 1572868
  1.3 10.6 %copy-start.3 = (bf16[256,256]{1,0:T(8,128)(2,1)S(1)}, bf16[256,256]{1,0:T(8,128)(2,1)}, u32[]{:S(2)}) copy-start(bf16[256,256]{1,0:T(8,128)(2,1)} %constant.5.clone.table) | copy-start | bytes 393220
  3.1 17.5 %copy-start.1 = (f32[2,2,256,256]{3,2,1,0:T(8,128)S(1)}, f32[2,2,256,256]{3,2,1,0:T(8,128)}, u32[]{:S(2)}) copy-start(f32[2,2,256,256]{3,2,1,0:T(8,128)} %p_own.5) | copy-start | bytes 3145732
  3.1 32.2 %copy-start.4 = (bf16[2,4,256,256]{3,2,1,0:T(8,128)(2,1)S(1)}, bf16[2,4,256,256]{3,2,1,0:T(8,128)(2,1)}, u32[]{:S(2)}) copy-start(bf16[2,4,256,256]{3,2,1,0:T(8,128)(2,1)} %constant.4.clone.tables) | copy-start | bytes 3145732
  3.1 16.2 %all-to-all-start = ((bf16[16,32,256]{2,1,0:T(8,128)(2,1)}), bf16[16,32,256]{2,1,0:T(8,128)(2,1)S(1)}, u32[]{:S(2)}, u32[]{:S(2)}) async-start(bf16[16,32,256]{2,1,0:T(8,128)(2,1)} %shard_map.104), calls=%async_computation | async-start | bytes 524288 | tf_op jit(solution)/shard_map/all_to_all | solution.py:477
  20.6 14.7 %collective-permute-start = (f32[2,2,256,256]{3,2,1,0:T(8,128)S(1)}, f32[2,2,256,256]{3,2,1,0:T(8,128)S(1)}, u32[]{:S(2)}, u32[]{:S(2)}) collective-permute-start(f32[2,2,256,256]{3,2,1,0:T(8,128)S(1)} %copy-done.1), channel_id=1, source_target_pairs={{0,1},{1,0},{2,3},{3,2},{4,5},{5,4},{6,7},{7,6},{8,9},{9,8},{10,11... | collective-permute-start | bytes 3145736 | tf_op jit(solution)/shard_map/ppermute | solution.py:480
  41.8 2.4 %collective-permute-start.1 = (bf16[16,96,256]{2,1,0:T(8,128)(2,1)S(1)}, bf16[16,96,256]{2,1,0:T(8,128)(2,1)S(1)}, u32[]{:S(2)}, u32[]{:S(2)}) collective-permute-start(bf16[16,96,256]{2,1,0:T(8,128)(2,1)S(1)} %get-tuple-element.32), channel_id=1, source_target_pairs={{0,1},{1,0},{2,3},{3,2},{4,5},{5,4},{6,7},{7,6},{8,9},{9,8},{10,11... | collective-permute-start | bytes 2359304 | tf_op jit(solution)/shard_map/ppermute | solution.py:480
  61.3 5.3 %collective-permute-start.4 = (bf16[80,256]{1,0:T(8,128)(2,1)S(1)}, bf16[80,256]{1,0:T(8,128)(2,1)S(1)}, u32[]{:S(2)}, u32[]{:S(2)}) collective-permute-start(bf16[80,256]{1,0:T(8,128)(2,1)S(1)} %shard_map.110.own), channel_id=1, source_target_pairs={{0,96},{32,0},{64,32},{96,64},{1,97},{33,1},{65,33},{97,65},{2,98}... | collective-permute-start | bytes 122888 | tf_op jit(solution)/shard_map/ppermute | solution.py:484
  63.9 4.4 %collective-permute-start.3 = (bf16[80,256]{1,0:T(8,128)(2,1)S(1)}, bf16[80,256]{1,0:T(8,128)(2,1)S(1)}, u32[]{:S(2)}, u32[]{:S(2)}) collective-permute-start(bf16[80,256]{1,0:T(8,128)(2,1)S(1)} %shard_map.110.own), channel_id=1, source_target_pairs={{0,64},{32,96},{64,0},{96,32},{1,65},{33,97},{65,1},{97,33},{2,66}... | collective-permute-start | bytes 122888 | tf_op jit(solution)/shard_map/ppermute | solution.py:484
  64.4 4.3 %collective-permute-start.2 = (bf16[80,256]{1,0:T(8,128)(2,1)S(1)}, bf16[80,256]{1,0:T(8,128)(2,1)S(1)}, u32[]{:S(2)}, u32[]{:S(2)}) collective-permute-start(bf16[80,256]{1,0:T(8,128)(2,1)S(1)} %shard_map.110.own), channel_id=1, source_target_pairs={{0,32},{32,64},{64,96},{96,0},{1,33},{33,65},{65,97},{97,1},{2,34}... | collective-permute-start | bytes 122888 | tf_op jit(solution)/shard_map/ppermute | solution.py:484
  83.1 6.6 %collective-permute-start.5 = (bf16[16,96,256]{2,1,0:T(8,128)(2,1)S(1)}, bf16[16,96,256]{2,1,0:T(8,128)(2,1)S(1)}, u32[]{:S(2)}, u32[]{:S(2)}) collective-permute-start(bf16[16,96,256]{2,1,0:T(8,128)(2,1)S(1)} %all_to_all.32.h_own.h_one), channel_id=1, source_target_pairs={{0,1},{1,0},{2,3},{3,2},{4,5},{5,4},{6,7},{7,6},{8,9},{9,8},{10,11... | collective-permute-start | bytes 2359304 | tf_op jit(solution)/shard_map/ppermute | solution.py:480
  96.3 2.4 %collective-permute-start.6 = (bf16[16,96,256]{2,1,0:T(8,128)(2,1)S(1)}, bf16[16,96,256]{2,1,0:T(8,128)(2,1)S(1)}, u32[]{:S(2)}, u32[]{:S(2)}) collective-permute-start(bf16[16,96,256]{2,1,0:T(8,128)(2,1)S(1)} %get-tuple-element.41), channel_id=1, source_target_pairs={{0,1},{1,0},{2,3},{3,2},{4,5},{5,4},{6,7},{7,6},{8,9},{9,8},{10,11... | collective-permute-start | bytes 2359304 | tf_op jit(solution)/shard_map/ppermute | solution.py:480
  116.2 2.9 %collective-permute-start.9 = (bf16[80,256]{1,0:T(8,128)(2,1)S(1)}, bf16[80,256]{1,0:T(8,128)(2,1)S(1)}, u32[]{:S(2)}, u32[]{:S(2)}) collective-permute-start(bf16[80,256]{1,0:T(8,128)(2,1)S(1)} %shard_map.116.own), channel_id=1, source_target_pairs={{0,96},{32,0},{64,32},{96,64},{1,97},{33,1},{65,33},{97,65},{2,98}... | collective-permute-start | bytes 122888 | tf_op jit(solution)/shard_map/ppermute | solution.py:484
  116.7 4.4 %collective-permute-start.8 = (bf16[80,256]{1,0:T(8,128)(2,1)S(1)}, bf16[80,256]{1,0:T(8,128)(2,1)S(1)}, u32[]{:S(2)}, u32[]{:S(2)}) collective-permute-start(bf16[80,256]{1,0:T(8,128)(2,1)S(1)} %shard_map.116.own), channel_id=1, source_target_pairs={{0,64},{32,96},{64,0},{96,32},{1,65},{33,97},{65,1},{97,33},{2,66}... | collective-permute-start | bytes 122888 | tf_op jit(solution)/shard_map/ppermute | solution.py:484
  117.5 4.1 %collective-permute-start.7 = (bf16[80,256]{1,0:T(8,128)(2,1)S(1)}, bf16[80,256]{1,0:T(8,128)(2,1)S(1)}, u32[]{:S(2)}, u32[]{:S(2)}) collective-permute-start(bf16[80,256]{1,0:T(8,128)(2,1)S(1)} %shard_map.116.own), channel_id=1, source_target_pairs={{0,32},{32,64},{64,96},{96,0},{1,33},{33,65},{65,97},{97,1},{2,34}... | collective-permute-start | bytes 122888 | tf_op jit(solution)/shard_map/ppermute | solution.py:484
  136.1 6.7 %copy-start = (f32[2,264,256]{2,1,0:T(8,128)S(1)}, f32[2,264,256]{2,1,0:T(8,128)}, u32[]{:S(2)}) copy-start(f32[2,264,256]{2,1,0:T(8,128)} %obj.3) | copy-start | bytes 1622020
  136.1 6.6 %collective-permute-start.10 = (bf16[16,96,256]{2,1,0:T(8,128)(2,1)S(1)}, bf16[16,96,256]{2,1,0:T(8,128)(2,1)S(1)}, u32[]{:S(2)}, u32[]{:S(2)}) collective-permute-start(bf16[16,96,256]{2,1,0:T(8,128)(2,1)S(1)} %all_to_all.34.h_own.h_two), channel_id=1, source_target_pairs={{0,1},{1,0},{2,3},{3,2},{4,5},{5,4},{6,7},{7,6},{8,9},{9,8},{10,11... | collective-permute-start | bytes 2359304 | tf_op jit(solution)/shard_map/ppermute | solution.py:480

commit v3 on v2

--- a/solution.py
+++ b/solution.py
@@ -210,10 +210,12 @@
     out[64:80, :] = denom[...]
 
 
-def probe_update_kernel(own, one, two, three, objs, out):
+def probe_update_kernel(own, one, two, three, objs, left_out, out, left_out_now):
     total = (own[...].astype(F32) + two[...].astype(F32)) + (one[...].astype(F32) + three[...].astype(F32))
     scale = 1.0 / (total[64:80] + PROBE_REG)
-    step = (total[0:64] * jnp.concatenate([scale] * 4, axis=0)).astype(BF16)
+    exact = total[0:64] * jnp.concatenate([scale] * 4, axis=0) + left_out[...]
+    step = exact.astype(BF16)
+    left_out_now[...] = exact - step.astype(F32)
 
     def visit(t, carry):
         out[t, 0:32, :] = objs[t]
@@ -506,6 +508,7 @@
     probe_other = swap(own)
     h_own = h_oth = lax.all_to_all(windows, ("tm", "mode"), 0, 0)
 
+    left_out = jnp.zeros((64, PS), F32)
     for iteration in range(2):
         if iteration > 0:
             h_oth = swap(h_own)
@@ -533,9 +536,10 @@
                 meta, parts, scale, upd
             )
         h_first = h_own
-        h_own = exchange(
-            call(probe_update_kernel, arr((N_TM, 96, PS), BF16), [VM] * 5)(probe_part, *others, objs)
-        )
+        updates, left_out = call(
+            probe_update_kernel, (arr((N_TM, 96, PS), BF16), arr((64, PS), F32)), [VM] * 6
+        )(probe_part, *others, objs, left_out)
+        h_own = exchange(updates)
 
     h_oth = swap(h_own)
     probe_out = call(final_probe_kernel, arr((2, 2, PS, PS), F32), [VM] * 3)(probe_modes, h_first, h_own)

time: 144 us -> 145 us (level)
  no operation moved by 1% of the time
where the time goes in v3:
time: 145 us; the launch traced here: 144 us
  blocking collectives  75.4 us (52%)
  starting transfers between devices  26.6 us (18%)
  Pallas kernels  24.8 us (17%)
  waiting for transfers between devices  15.9 us (11%)
    all_to_all x4, blocking collectives, exchange(): return lax.all_to_all(x, 'tm', 0, 0)  62.8 us
    pallas_call x2, Pallas kernels, position(): call(functools.partial(position_kernel, with_update), (part, part, arr((2...  13 us
    all_to_all x1, blocking collectives, body(): h_own = h_oth = lax.all_to_all(windows, ('tm', 'mode'), 0, 0)  12.6 us
    ppermute x5, starting transfers between devices, swap(): return lax.ppermute(x, 'mode', SWAP)  12.3 us
    all_to_all x1, starting transfers between devices, exchange(): return lax.all_to_all(x, 'tm', 0, 0)  8.74 us
    all_to_all x1, waiting for transfers between devices, exchange(): return lax.all_to_all(x, 'tm', 0, 0)  6.96 us
    ppermute x6, starting transfers between devices, over_tiles(): lax.ppermute(x, 'tile', [(i, (i + k) % n) for i in range(n)])  5.65 us
    ppermute x6, waiting for transfers between devices, over_tiles(): lax.ppermute(x, 'tile', [(i, (i + k) % n) for i in range(n)])  4.52 us
  transfers between devices with their start and end apart: 12, of which 9 were waited for; matrix products, arithmetic and copies ran while one was open for 0% of the time, Pallas kernels for 4%

profile of v3, /device:TPU:1, one launch (start us, length us, event | category | flops | bytes accessed | tf_op | source)
XLA Modules:
  0.0 144.2 jit_solution(3768491553718861760)
XLA Ops:
  1.3 1.8 %shard_map.104 = bf16[16,32,256]{2,1,0:T(8,128)(2,1)} custom-call(s32[2]{0:T(128)} %bitcast.11, s32[2]{0:T(128)} %row_offset.1, s32[2]{0:T(128)} %col_offset.1, s32[1,1]{1,0:T(1,128)} %bitcast.3.live_counts, f32[2,264,256]{2,1,0:T(8,128)} %obj.3), custom_call_target="tpu_custom_call" | custom-call | bytes 1048576 | tf_op jit(solution)/shard_map/pallas_call | solution.py:491
  3.1 8.7 %all-to-all-start = ((bf16[16,32,256]{2,1,0:T(8,128)(2,1)}), bf16[16,32,256]{2,1,0:T(8,128)(2,1)S(1)}, u32[]{:S(2)}, u32[]{:S(2)}) async-start(bf16[16,32,256]{2,1,0:T(8,128)(2,1)} %shard_map.104), calls=%async_computation | async-start | bytes 524288 | tf_op jit(solution)/shard_map/all_to_all | solution.py:479
  12.4 7.0 %all-to-all-done.high = bf16[16,32,256]{2,1,0:T(8,128)(2,1)S(1)} async-done(((bf16[16,32,256]{2,1,0:T(8,128)(2,1)}), bf16[16,32,256]{2,1,0:T(8,128)(2,1)S(1)}, u32[]{:S(2)}, u32[]{:S(2)}) %all-to-all-start) | async-done | bytes 262176 | tf_op jit(solution)/shard_map/all_to_all | solution.py:479
  19.3 1.3 shard_map.106
  20.6 2.1 %collective-permute-start = (f32[2,2,256,256]{3,2,1,0:T(8,128)S(1)}, f32[2,2,256,256]{3,2,1,0:T(8,128)S(1)}, u32[]{:S(2)}, u32[]{:S(2)}) collective-permute-start(f32[2,2,256,256]{3,2,1,0:T(8,128)S(1)} %copy-done.1), channel_id=1, source_target_pairs={{0,1},{1,0},{2,3},{3,2},{4,5},{5,4},{6,7},{7,6},{8,9},{9,8},{10,11... | collective-permute-start | bytes 3145736 | tf_op jit(solution)/shard_map/ppermute | solution.py:482
  22.7 12.6 %all_to_all.30.h_own.h_oth = bf16[32,16,256]{2,1,0:T(8,128)(2,1)S(1)} all-to-all(bf16[32,16,256]{2,1,0:T(8,128)(2,1)S(1)} %get-tuple-element.31), channel_id=1, replica_groups=mesh['tile'=4,'tm'=16,'mode'=2] {'tm','mode'}, dimensions={0} | all-to-all | bytes 524288 | tf_op jit(solution)/shard_map/all_to_all | solution.py:509
  35.3 6.5 %shard_map.107 = (bf16[16,96,256]{2,1,0:T(8,128)(2,1)S(1)}, bf16[16,96,256]{2,1,0:T(8,128)(2,1)S(1)}, f32[272,256]{1,0:T(8,128)S(1)}) custom-call(s32[16,8]{1,0:T(8,128)S(1)} %bitcast.5, bf16[2,4,256,256]{3,2,1,0:T(8,128)(2,1)S(1)} %copy-done.4, f32[2,2,256,256]{3,2,1,0:T(8,128)S(1)} %copy-done.1, f32[2,2,256,256]{3,2,1,0:T(8,128)S(1)} %collective-permute-done.p_oth, ...), custom_call_target="tpu_custom_call" | custom-call | flops 3221225472 | bytes 10485760 | tf_op jit(solution)/shard_map/pallas_call | solution.py:422
  42.0 1.1 shard_map.108.scale
  43.2 1.0 collective-permute-done.1.recv
  44.3 16.8 %all_to_all.31.parts = bf16[16,112,256]{2,1,0:T(8,128)(2,1)S(1)} all-to-all(bf16[16,112,256]{2,1,0:T(8,128)(2,1)S(1)} %get-tuple-element.38), channel_id=1, replica_groups=mesh['tile'=4,'tm'=16,'mode'=2] {'tm'}, dimensions={0} | all-to-all | bytes 1835008 | tf_op jit(solution)/shard_map/all_to_all | solution.py:479
  61.3 2.5 %collective-permute-start.4 = (bf16[80,256]{1,0:T(8,128)(2,1)S(1)}, bf16[80,256]{1,0:T(8,128)(2,1)S(1)}, u32[]{:S(2)}, u32[]{:S(2)}) collective-permute-start(bf16[80,256]{1,0:T(8,128)(2,1)S(1)} %shard_map.110.own), channel_id=1, source_target_pairs={{0,96},{32,0},{64,32},{96,64},{1,97},{33,1},{65,33},{97,65},{2,98}... | collective-permute-start | bytes 122888 | tf_op jit(solution)/shard_map/ppermute | solution.py:486
  65.0 1.6 %shard_map.111 = (bf16[16,32,256]{2,1,0:T(8,128)(2,1)S(1)}, f32[16,256]{1,0:T(8,128)S(1)}, f32[16,24,256]{2,1,0:T(8,128)S(1)}) custom-call(s32[16,8]{1,0:T(8,128)S(1)} %bitcast.7, bf16[16,112,256]{2,1,0:T(8,128)(2,1)S(1)} %all_to_all.31.parts, f32[16,24,256]{2,1,0:T(8,128)S(1)} %shard_map.108.scale, bf16[16,32,256]{2,1,0:T(8,128)(2,1)S(1)} %all-to-all-done.high), custom_call_target="tpu_custom_call" | custom-call | bytes 1048576 | tf_op jit(solution)/shard_map/pallas_call | solution.py:528
  66.6 1.6 %collective-permute-done.3.two = bf16[80,256]{1,0:T(8,128)(2,1)S(1)} collective-permute-done((bf16[80,256]{1,0:T(8,128)(2,1)S(1)}, bf16[80,256]{1,0:T(8,128)(2,1)S(1)}, u32[]{:S(2)}, u32[]{:S(2)}) %collective-permute-start.3) | collective-permute-done | bytes 40992 | tf_op jit(solution)/shard_map/ppermute | solution.py:486
  68.7 14.4 %all_to_all.32.h_own.h_one = bf16[16,96,256]{2,1,0:T(8,128)(2,1)S(1)} all-to-all(bf16[16,96,256]{2,1,0:T(8,128)(2,1)S(1)} %get-tuple-element.42), channel_id=1, replica_groups=mesh['tile'=4,'tm'=16,'mode'=2] {'tm'}, dimensions={0} | all-to-all | bytes 1572864 | tf_op jit(solution)/shard_map/all_to_all | solution.py:479
  83.1 4.7 %collective-permute-start.5 = (bf16[16,96,256]{2,1,0:T(8,128)(2,1)S(1)}, bf16[16,96,256]{2,1,0:T(8,128)(2,1)S(1)}, u32[]{:S(2)}, u32[]{:S(2)}) collective-permute-start(bf16[16,96,256]{2,1,0:T(8,128)(2,1)S(1)} %all_to_all.32.h_own.h_one), channel_id=1, source_target_pairs={{0,1},{1,0},{2,3},{3,2},{4,5},{5,4},{6,7},{7,6},{8,9},{9,8},{10,11... | collective-permute-start | bytes 2359304 | tf_op jit(solution)/shard_map/ppermute | solution.py:482
  87.8 1.9 %collective-permute-done.5.h_oth = bf16[16,96,256]{2,1,0:T(8,128)(2,1)S(1)} collective-permute-done((bf16[16,96,256]{2,1,0:T(8,128)(2,1)S(1)}, bf16[16,96,256]{2,1,0:T(8,128)(2,1)S(1)}, u32[]{:S(2)}, u32[]{:S(2)}) %collective-permute-start.5) | collective-permute-done | bytes 786464 | tf_op jit(solution)/shard_map/ppermute | solution.py:482
  89.7 6.5 %shard_map.113 = (bf16[16,96,256]{2,1,0:T(8,128)(2,1)S(1)}, bf16[16,96,256]{2,1,0:T(8,128)(2,1)S(1)}, f32[272,256]{1,0:T(8,128)S(1)}) custom-call(s32[16,8]{1,0:T(8,128)S(1)} %bitcast.8, bf16[2,4,256,256]{3,2,1,0:T(8,128)(2,1)S(1)} %copy-done.4, f32[2,2,256,256]{3,2,1,0:T(8,128)S(1)} %copy-done.1, f32[2,2,256,256]{3,2,1,0:T(8,128)S(1)} %collective-permute-done.p_oth, ...), custom_call_target="tpu_custom_call" | custom-call | flops 3221225472 | bytes 10485760 | tf_op jit(solution)/shard_map/pallas_call | solution.py:422
  96.7 1.1 shard_map.114.scale
  98.8 17.2 %all_to_all.33.parts = bf16[16,112,256]{2,1,0:T(8,128)(2,1)S(1)} all-to-all(bf16[16,112,256]{2,1,0:T(8,128)(2,1)S(1)} %get-tuple-element.48), channel_id=1, replica_groups=mesh['tile'=4,'tm'=16,'mode'=2] {'tm'}, dimensions={0} | all-to-all | bytes 1835008 | tf_op jit(solution)/shard_map/all_to_all | solution.py:479
  118.2 1.0 shard_map.117.objs
  119.2 1.9 %collective-permute-done.8.two = bf16[80,256]{1,0:T(8,128)(2,1)S(1)} collective-permute-done((bf16[80,256]{1,0:T(8,128)(2,1)S(1)}, bf16[80,256]{1,0:T(8,128)(2,1)S(1)}, u32[]{:S(2)}, u32[]{:S(2)}) %collective-permute-start.8) | collective-permute-done | bytes 40992 | tf_op jit(solution)/shard_map/ppermute | solution.py:486
  122.3 14.4 %all_to_all.34.h_own.h_two = bf16[16,96,256]{2,1,0:T(8,128)(2,1)S(1)} all-to-all(bf16[16,96,256]{2,1,0:T(8,128)(2,1)S(1)} %get-tuple-element.53), channel_id=1, replica_groups=mesh['tile'=4,'tm'=16,'mode'=2] {'tm'}, dimensions={0} | all-to-all | bytes 1572864 | tf_op jit(solution)/shard_map/all_to_all | solution.py:479
  136.7 4.7 %collective-permute-start.10 = (bf16[16,96,256]{2,1,0:T(8,128)(2,1)S(1)}, bf16[16,96,256]{2,1,0:T(8,128)(2,1)S(1)}, u32[]{:S(2)}, u32[]{:S(2)}) collective-permute-start(bf16[16,96,256]{2,1,0:T(8,128)(2,1)S(1)} %all_to_all.34.h_own.h_two), channel_id=1, source_target_pairs={{0,1},{1,0},{2,3},{3,2},{4,5},{5,4},{6,7},{7,6},{8,9},{9,8},{10,11... | collective-permute-start | bytes 2359304 | tf_op jit(solution)/shard_map/ppermute | solution.py:482
  141.4 1.2 shard_map.120
  (34 shorter events, 9.1 us)
Async XLA Ops:
  1.3 10.6 %copy-start.2 = (f32[2,256,256]{2,1,0:T(8,128)S(1)}, f32[2,256,256]{2,1,0:T(8,128)}, u32[]{:S(2)}) copy-start(f32[2,256,256]{2,1,0:T(8,128)} %amp.1) | copy-start | bytes 1572868
  1.3 10.6 %copy-start.3 = (bf16[256,256]{1,0:T(8,128)(2,1)S(1)}, bf16[256,256]{1,0:T(8,128)(2,1)}, u32[]{:S(2)}) copy-start(bf16[256,256]{1,0:T(8,128)(2,1)} %constant.7.clone.table) | copy-start | bytes 393220
  3.1 17.5 %copy-start.1 = (f32[2,2,256,256]{3,2,1,0:T(8,128)S(1)}, f32[2,2,256,256]{3,2,1,0:T(8,128)}, u32[]{:S(2)}) copy-start(f32[2,2,256,256]{3,2,1,0:T(8,128)} %p_own.5) | copy-start | bytes 3145732
  3.1 32.2 %copy-start.4 = (bf16[2,4,256,256]{3,2,1,0:T(8,128)(2,1)S(1)}, bf16[2,4,256,256]{3,2,1,0:T(8,128)(2,1)}, u32[]{:S(2)}) copy-start(bf16[2,4,256,256]{3,2,1,0:T(8,128)(2,1)} %constant.6.clone.tables) | copy-start | bytes 3145732
  3.1 16.2 %all-to-all-start = ((bf16[16,32,256]{2,1,0:T(8,128)(2,1)}), bf16[16,32,256]{2,1,0:T(8,128)(2,1)S(1)}, u32[]{:S(2)}, u32[]{:S(2)}) async-start(bf16[16,32,256]{2,1,0:T(8,128)(2,1)} %shard_map.104), calls=%async_computation | async-start | bytes 524288 | tf_op jit(solution)/shard_map/all_to_all | solution.py:479
  20.6 14.7 %collective-permute-start = (f32[2,2,256,256]{3,2,1,0:T(8,128)S(1)}, f32[2,2,256,256]{3,2,1,0:T(8,128)S(1)}, u32[]{:S(2)}, u32[]{:S(2)}) collective-permute-start(f32[2,2,256,256]{3,2,1,0:T(8,128)S(1)} %copy-done.1), channel_id=1, source_target_pairs={{0,1},{1,0},{2,3},{3,2},{4,5},{5,4},{6,7},{7,6},{8,9},{9,8},{10,11... | collective-permute-start | bytes 3145736 | tf_op jit(solution)/shard_map/ppermute | solution.py:482
  41.8 2.4 %collective-permute-start.1 = (bf16[16,96,256]{2,1,0:T(8,128)(2,1)S(1)}, bf16[16,96,256]{2,1,0:T(8,128)(2,1)S(1)}, u32[]{:S(2)}, u32[]{:S(2)}) collective-permute-start(bf16[16,96,256]{2,1,0:T(8,128)(2,1)S(1)} %get-tuple-element.35), channel_id=1, source_target_pairs={{0,1},{1,0},{2,3},{3,2},{4,5},{5,4},{6,7},{7,6},{8,9},{9,8},{10,11... | collective-permute-start | bytes 2359304 | tf_op jit(solution)/shard_map/ppermute | solution.py:482
  61.3 5.3 %collective-permute-start.4 = (bf16[80,256]{1,0:T(8,128)(2,1)S(1)}, bf16[80,256]{1,0:T(8,128)(2,1)S(1)}, u32[]{:S(2)}, u32[]{:S(2)}) collective-permute-start(bf16[80,256]{1,0:T(8,128)(2,1)S(1)} %shard_map.110.own), channel_id=1, source_target_pairs={{0,96},{32,0},{64,32},{96,64},{1,97},{33,1},{65,33},{97,65},{2,98}... | collective-permute-start | bytes 122888 | tf_op jit(solution)/shard_map/ppermute | solution.py:486
  63.9 4.4 %collective-permute-start.3 = (bf16[80,256]{1,0:T(8,128)(2,1)S(1)}, bf16[80,256]{1,0:T(8,128)(2,1)S(1)}, u32[]{:S(2)}, u32[]{:S(2)}) collective-permute-start(bf16[80,256]{1,0:T(8,128)(2,1)S(1)} %shard_map.110.own), channel_id=1, source_target_pairs={{0,64},{32,96},{64,0},{96,32},{1,65},{33,97},{65,1},{97,33},{2,66}... | collective-permute-start | bytes 122888 | tf_op jit(solution)/shard_map/ppermute | solution.py:486
  64.4 4.3 %collective-permute-start.2 = (bf16[80,256]{1,0:T(8,128)(2,1)S(1)}, bf16[80,256]{1,0:T(8,128)(2,1)S(1)}, u32[]{:S(2)}, u32[]{:S(2)}) collective-permute-start(bf16[80,256]{1,0:T(8,128)(2,1)S(1)} %shard_map.110.own), channel_id=1, source_target_pairs={{0,32},{32,64},{64,96},{96,0},{1,33},{33,65},{65,97},{97,1},{2,34}... | collective-permute-start | bytes 122888 | tf_op jit(solution)/shard_map/ppermute | solution.py:486
  83.1 6.6 %collective-permute-start.5 = (bf16[16,96,256]{2,1,0:T(8,128)(2,1)S(1)}, bf16[16,96,256]{2,1,0:T(8,128)(2,1)S(1)}, u32[]{:S(2)}, u32[]{:S(2)}) collective-permute-start(bf16[16,96,256]{2,1,0:T(8,128)(2,1)S(1)} %all_to_all.32.h_own.h_one), channel_id=1, source_target_pairs={{0,1},{1,0},{2,3},{3,2},{4,5},{5,4},{6,7},{7,6},{8,9},{9,8},{10,11... | collective-permute-start | bytes 2359304 | tf_op jit(solution)/shard_map/ppermute | solution.py:482
  96.3 2.4 %collective-permute-start.6 = (bf16[16,96,256]{2,1,0:T(8,128)(2,1)S(1)}, bf16[16,96,256]{2,1,0:T(8,128)(2,1)S(1)}, u32[]{:S(2)}, u32[]{:S(2)}) collective-permute-start(bf16[16,96,256]{2,1,0:T(8,128)(2,1)S(1)} %get-tuple-element.45), channel_id=1, source_target_pairs={{0,1},{1,0},{2,3},{3,2},{4,5},{5,4},{6,7},{7,6},{8,9},{9,8},{10,11... | collective-permute-start | bytes 2359304 | tf_op jit(solution)/shard_map/ppermute | solution.py:482
  116.2 3.0 %collective-permute-start.9 = (bf16[80,256]{1,0:T(8,128)(2,1)S(1)}, bf16[80,256]{1,0:T(8,128)(2,1)S(1)}, u32[]{:S(2)}, u32[]{:S(2)}) collective-permute-start(bf16[80,256]{1,0:T(8,128)(2,1)S(1)} %shard_map.116.own), channel_id=1, source_target_pairs={{0,96},{32,0},{64,32},{96,64},{1,97},{33,1},{65,33},{97,65},{2,98}... | collective-permute-start | bytes 122888 | tf_op jit(solution)/shard_map/ppermute | solution.py:486
  116.7 4.4 %collective-permute-start.8 = (bf16[80,256]{1,0:T(8,128)(2,1)S(1)}, bf16[80,256]{1,0:T(8,128)(2,1)S(1)}, u32[]{:S(2)}, u32[]{:S(2)}) collective-permute-start(bf16[80,256]{1,0:T(8,128)(2,1)S(1)} %shard_map.116.own), channel_id=1, source_target_pairs={{0,64},{32,96},{64,0},{96,32},{1,65},{33,97},{65,1},{97,33},{2,66}... | collective-permute-start | bytes 122888 | tf_op jit(solution)/shard_map/ppermute | solution.py:486
  117.6 4.1 %collective-permute-start.7 = (bf16[80,256]{1,0:T(8,128)(2,1)S(1)}, bf16[80,256]{1,0:T(8,128)(2,1)S(1)}, u32[]{:S(2)}, u32[]{:S(2)}) collective-permute-start(bf16[80,256]{1,0:T(8,128)(2,1)S(1)} %shard_map.116.own), channel_id=1, source_target_pairs={{0,32},{32,64},{64,96},{96,0},{1,33},{33,65},{65,97},{97,1},{2,34}... | collective-permute-start | bytes 122888 | tf_op jit(solution)/shard_map/ppermute | solution.py:486
  136.7 6.7 %copy-start = (f32[2,264,256]{2,1,0:T(8,128)S(1)}, f32[2,264,256]{2,1,0:T(8,128)}, u32[]{:S(2)}) copy-start(f32[2,264,256]{2,1,0:T(8,128)} %obj.3) | copy-start | bytes 1622020
  136.7 6.6 %collective-permute-start.10 = (bf16[16,96,256]{2,1,0:T(8,128)(2,1)S(1)}, bf16[16,96,256]{2,1,0:T(8,128)(2,1)S(1)}, u32[]{:S(2)}, u32[]{:S(2)}) collective-permute-start(bf16[16,96,256]{2,1,0:T(8,128)(2,1)S(1)} %all_to_all.34.h_own.h_two), channel_id=1, source_target_pairs={{0,1},{1,0},{2,3},{3,2},{4,5},{5,4},{6,7},{7,6},{8,9},{9,8},{10,11... | collective-permute-start | bytes 2359304 | tf_op jit(solution)/shard_map/ppermute | solution.py:482

commit v4 on v3

--- a/solution.py
+++ b/solution.py
@@ -11,7 +11,7 @@
 
 PS = 256
 HALF = 128
-PARTS = 3
+PARTS = 1
 BH = 264
 N_TM = 16
 UNROLL = 16

time: 145 us -> 139 us (0.959)
  Pallas kernels: 24.8 us -> 19.3 us
    pallas_call x2, Pallas kernels: 13 us -> 7.48 us  [position(): call(functools.partial(position_kernel, with_update), (part, part, arr((2...]
  transfers between devices with their start and end apart: 12 -> 12, of which waited for: 9 -> 9; matrix products, arithmetic and copies ran while one was open for 0% -> 0% of each run, Pallas kernels for 4% -> 5%
where the time goes in v4:
time: 139 us
  blocking collectives  75.4 us (54%)
  starting transfers between devices  26.8 us (19%)
  Pallas kernels  19.3 us (14%)
  waiting for transfers between devices  15.9 us (11%)
  between operations  1.44 us (1%)
    all_to_all x4, blocking collectives, exchange(): return lax.all_to_all(x, 'tm', 0, 0)  62.8 us
    all_to_all x1, blocking collectives, body(): h_own = h_oth = lax.all_to_all(windows, ('tm', 'mode'), 0, 0)  12.6 us
    ppermute x5, starting transfers between devices, swap(): return lax.ppermute(x, 'mode', SWAP)  12.4 us
    all_to_all x1, starting transfers between devices, exchange(): return lax.all_to_all(x, 'tm', 0, 0)  8.74 us
    pallas_call x2, Pallas kernels, position(): call(functools.partial(position_kernel, with_update), (part, part, arr((2...  7.48 us
    all_to_all x1, waiting for transfers between devices, exchange(): return lax.all_to_all(x, 'tm', 0, 0)  6.94 us
    ppermute x6, starting transfers between devices, over_tiles(): lax.ppermute(x, 'tile', [(i, (i + k) % n) for i in range(n)])  5.63 us
    ppermute x6, waiting for transfers between devices, over_tiles(): lax.ppermute(x, 'tile', [(i, (i + k) % n) for i in range(n)])  4.53 us
  transfers between devices with their start and end apart: 12, of which 9 were waited for; matrix products, arithmetic and copies ran while one was open for 0% of the time, Pallas kernels for 5%

profile of v4, /device:TPU:1, one launch (start us, length us, event | category | flops | bytes accessed | tf_op | source)
XLA Modules:
  0.0 138.8 jit_solution(3591236891919603294)
XLA Ops:
  1.3 1.8 %shard_map.104 = bf16[16,32,256]{2,1,0:T(8,128)(2,1)} custom-call(s32[2]{0:T(128)} %bitcast.11, s32[2]{0:T(128)} %row_offset.1, s32[2]{0:T(128)} %col_offset.1, s32[1,1]{1,0:T(1,128)} %bitcast.3.live_counts, f32[2,264,256]{2,1,0:T(8,128)} %obj.3), custom_call_target="tpu_custom_call" | custom-call | bytes 1048576 | tf_op jit(solution)/shard_map/pallas_call | solution.py:491
  3.1 8.7 %all-to-all-start = ((bf16[16,32,256]{2,1,0:T(8,128)(2,1)}), bf16[16,32,256]{2,1,0:T(8,128)(2,1)S(1)}, u32[]{:S(2)}, u32[]{:S(2)}) async-start(bf16[16,32,256]{2,1,0:T(8,128)(2,1)} %shard_map.104), calls=%async_computation | async-start | bytes 524288 | tf_op jit(solution)/shard_map/all_to_all | solution.py:479
  12.4 6.9 %all-to-all-done.high = bf16[16,32,256]{2,1,0:T(8,128)(2,1)S(1)} async-done(((bf16[16,32,256]{2,1,0:T(8,128)(2,1)}), bf16[16,32,256]{2,1,0:T(8,128)(2,1)S(1)}, u32[]{:S(2)}, u32[]{:S(2)}) %all-to-all-start) | async-done | bytes 262176 | tf_op jit(solution)/shard_map/all_to_all | solution.py:479
  19.3 1.3 shard_map.106
  20.6 2.1 %collective-permute-start = (f32[2,2,256,256]{3,2,1,0:T(8,128)S(1)}, f32[2,2,256,256]{3,2,1,0:T(8,128)S(1)}, u32[]{:S(2)}, u32[]{:S(2)}) collective-permute-start(f32[2,2,256,256]{3,2,1,0:T(8,128)S(1)} %copy-done), channel_id=1, source_target_pairs={{0,1},{1,0},{2,3},{3,2},{4,5},{5,4},{6,7},{7,6},{8,9},{9,8},{10,11... | collective-permute-start | bytes 3145736 | tf_op jit(solution)/shard_map/ppermute | solution.py:482
  22.7 12.6 %all_to_all.30.h_own.h_oth = bf16[32,16,256]{2,1,0:T(8,128)(2,1)S(1)} all-to-all(bf16[32,16,256]{2,1,0:T(8,128)(2,1)S(1)} %get-tuple-element.31), channel_id=1, replica_groups=mesh['tile'=4,'tm'=16,'mode'=2] {'tm','mode'}, dimensions={0} | all-to-all | bytes 524288 | tf_op jit(solution)/shard_map/all_to_all | solution.py:509
  35.3 3.7 %shard_map.107 = (bf16[16,96,256]{2,1,0:T(8,128)(2,1)S(1)}, bf16[16,96,256]{2,1,0:T(8,128)(2,1)S(1)}, f32[272,256]{1,0:T(8,128)S(1)}) custom-call(s32[16,8]{1,0:T(8,128)S(1)} %bitcast.5, bf16[1,4,256,256]{3,2,1,0:T(8,128)(2,1)S(1)} %copy-done.2, f32[2,2,256,256]{3,2,1,0:T(8,128)S(1)} %copy-done, f32[2,2,256,256]{3,2,1,0:T(8,128)S(1)} %collective-permute-done.p_oth, ...), custom_call_target="tpu_custom_call" | custom-call | flops 1073741824 | bytes 10485760 | tf_op jit(solution)/shard_map/pallas_call | solution.py:422
  39.2 1.1 shard_map.108.scale
  40.4 1.0 collective-permute-done.1.recv
  41.5 16.8 %all_to_all.31.parts = bf16[16,112,256]{2,1,0:T(8,128)(2,1)S(1)} all-to-all(bf16[16,112,256]{2,1,0:T(8,128)(2,1)S(1)} %get-tuple-element.38), channel_id=1, replica_groups=mesh['tile'=4,'tm'=16,'mode'=2] {'tm'}, dimensions={0} | all-to-all | bytes 1835008 | tf_op jit(solution)/shard_map/all_to_all | solution.py:479
  58.5 2.5 %collective-permute-start.4 = (bf16[80,256]{1,0:T(8,128)(2,1)S(1)}, bf16[80,256]{1,0:T(8,128)(2,1)S(1)}, u32[]{:S(2)}, u32[]{:S(2)}) collective-permute-start(bf16[80,256]{1,0:T(8,128)(2,1)S(1)} %shard_map.110.own), channel_id=1, source_target_pairs={{0,96},{32,0},{64,32},{96,64},{1,97},{33,1},{65,33},{97,65},{2,98}... | collective-permute-start | bytes 122888 | tf_op jit(solution)/shard_map/ppermute | solution.py:486
  62.2 1.6 %shard_map.111 = (bf16[16,32,256]{2,1,0:T(8,128)(2,1)S(1)}, f32[16,256]{1,0:T(8,128)S(1)}, f32[16,24,256]{2,1,0:T(8,128)S(1)}) custom-call(s32[16,8]{1,0:T(8,128)S(1)} %bitcast.7, bf16[16,112,256]{2,1,0:T(8,128)(2,1)S(1)} %all_to_all.31.parts, f32[16,24,256]{2,1,0:T(8,128)S(1)} %shard_map.108.scale, bf16[16,32,256]{2,1,0:T(8,128)(2,1)S(1)} %all-to-all-done.high), custom_call_target="tpu_custom_call" | custom-call | bytes 1048576 | tf_op jit(solution)/shard_map/pallas_call | solution.py:528
  63.8 1.7 %collective-permute-done.3.two = bf16[80,256]{1,0:T(8,128)(2,1)S(1)} collective-permute-done((bf16[80,256]{1,0:T(8,128)(2,1)S(1)}, bf16[80,256]{1,0:T(8,128)(2,1)S(1)}, u32[]{:S(2)}, u32[]{:S(2)}) %collective-permute-start.3) | collective-permute-done | bytes 40992 | tf_op jit(solution)/shard_map/ppermute | solution.py:486
  65.9 14.4 %all_to_all.32.h_own.h_one = bf16[16,96,256]{2,1,0:T(8,128)(2,1)S(1)} all-to-all(bf16[16,96,256]{2,1,0:T(8,128)(2,1)S(1)} %get-tuple-element.42), channel_id=1, replica_groups=mesh['tile'=4,'tm'=16,'mode'=2] {'tm'}, dimensions={0} | all-to-all | bytes 1572864 | tf_op jit(solution)/shard_map/all_to_all | solution.py:479
  80.3 4.7 %collective-permute-start.5 = (bf16[16,96,256]{2,1,0:T(8,128)(2,1)S(1)}, bf16[16,96,256]{2,1,0:T(8,128)(2,1)S(1)}, u32[]{:S(2)}, u32[]{:S(2)}) collective-permute-start(bf16[16,96,256]{2,1,0:T(8,128)(2,1)S(1)} %all_to_all.32.h_own.h_one), channel_id=1, source_target_pairs={{0,1},{1,0},{2,3},{3,2},{4,5},{5,4},{6,7},{7,6},{8,9},{9,8},{10,11... | collective-permute-start | bytes 2359304 | tf_op jit(solution)/shard_map/ppermute | solution.py:482
  85.1 1.9 %collective-permute-done.5.h_oth = bf16[16,96,256]{2,1,0:T(8,128)(2,1)S(1)} collective-permute-done((bf16[16,96,256]{2,1,0:T(8,128)(2,1)S(1)}, bf16[16,96,256]{2,1,0:T(8,128)(2,1)S(1)}, u32[]{:S(2)}, u32[]{:S(2)}) %collective-permute-start.5) | collective-permute-done | bytes 786464 | tf_op jit(solution)/shard_map/ppermute | solution.py:482
  87.0 3.8 %shard_map.113 = (bf16[16,96,256]{2,1,0:T(8,128)(2,1)S(1)}, bf16[16,96,256]{2,1,0:T(8,128)(2,1)S(1)}, f32[272,256]{1,0:T(8,128)S(1)}) custom-call(s32[16,8]{1,0:T(8,128)S(1)} %bitcast.8, bf16[1,4,256,256]{3,2,1,0:T(8,128)(2,1)S(1)} %copy-done.2, f32[2,2,256,256]{3,2,1,0:T(8,128)S(1)} %copy-done, f32[2,2,256,256]{3,2,1,0:T(8,128)S(1)} %collective-permute-done.p_oth, ...), custom_call_target="tpu_custom_call" | custom-call | flops 1073741824 | bytes 10485760 | tf_op jit(solution)/shard_map/pallas_call | solution.py:422
  91.4 1.1 shard_map.114.scale
  93.5 17.2 %all_to_all.33.parts = bf16[16,112,256]{2,1,0:T(8,128)(2,1)S(1)} all-to-all(bf16[16,112,256]{2,1,0:T(8,128)(2,1)S(1)} %get-tuple-element.48), channel_id=1, replica_groups=mesh['tile'=4,'tm'=16,'mode'=2] {'tm'}, dimensions={0} | all-to-all | bytes 1835008 | tf_op jit(solution)/shard_map/all_to_all | solution.py:479
  112.8 1.0 shard_map.117.objs
  113.8 1.9 %collective-permute-done.8.two = bf16[80,256]{1,0:T(8,128)(2,1)S(1)} collective-permute-done((bf16[80,256]{1,0:T(8,128)(2,1)S(1)}, bf16[80,256]{1,0:T(8,128)(2,1)S(1)}, u32[]{:S(2)}, u32[]{:S(2)}) %collective-permute-start.8) | collective-permute-done | bytes 40992 | tf_op jit(solution)/shard_map/ppermute | solution.py:486
  117.0 14.4 %all_to_all.34.h_own.h_two = bf16[16,96,256]{2,1,0:T(8,128)(2,1)S(1)} all-to-all(bf16[16,96,256]{2,1,0:T(8,128)(2,1)S(1)} %get-tuple-element.53), channel_id=1, replica_groups=mesh['tile'=4,'tm'=16,'mode'=2] {'tm'}, dimensions={0} | all-to-all | bytes 1572864 | tf_op jit(solution)/shard_map/all_to_all | solution.py:479
  131.3 4.7 %collective-permute-start.10 = (bf16[16,96,256]{2,1,0:T(8,128)(2,1)S(1)}, bf16[16,96,256]{2,1,0:T(8,128)(2,1)S(1)}, u32[]{:S(2)}, u32[]{:S(2)}) collective-permute-start(bf16[16,96,256]{2,1,0:T(8,128)(2,1)S(1)} %all_to_all.34.h_own.h_two), channel_id=1, source_target_pairs={{0,1},{1,0},{2,3},{3,2},{4,5},{5,4},{6,7},{7,6},{8,9},{9,8},{10,11... | collective-permute-start | bytes 2359304 | tf_op jit(solution)/shard_map/ppermute | solution.py:482
  136.1 1.2 shard_map.120
  (34 shorter events, 9.3 us)
Async XLA Ops:
  1.3 10.6 %copy-start.3 = (f32[2,256,256]{2,1,0:T(8,128)S(1)}, f32[2,256,256]{2,1,0:T(8,128)}, u32[]{:S(2)}) copy-start(f32[2,256,256]{2,1,0:T(8,128)} %amp.1) | copy-start | bytes 1572868
  1.3 10.6 %copy-start.4 = (bf16[256,256]{1,0:T(8,128)(2,1)S(1)}, bf16[256,256]{1,0:T(8,128)(2,1)}, u32[]{:S(2)}) copy-start(bf16[256,256]{1,0:T(8,128)(2,1)} %constant.7.clone.table) | copy-start | bytes 393220
  3.1 17.5 %copy-start = (f32[2,2,256,256]{3,2,1,0:T(8,128)S(1)}, f32[2,2,256,256]{3,2,1,0:T(8,128)}, u32[]{:S(2)}) copy-start(f32[2,2,256,256]{3,2,1,0:T(8,128)} %p_own.5) | copy-start | bytes 3145732
  3.1 16.2 %all-to-all-start = ((bf16[16,32,256]{2,1,0:T(8,128)(2,1)}), bf16[16,32,256]{2,1,0:T(8,128)(2,1)S(1)}, u32[]{:S(2)}, u32[]{:S(2)}) async-start(bf16[16,32,256]{2,1,0:T(8,128)(2,1)} %shard_map.104), calls=%async_computation | async-start | bytes 524288 | tf_op jit(solution)/shard_map/all_to_all | solution.py:479
  12.4 22.9 %copy-start.2 = (bf16[1,4,256,256]{3,2,1,0:T(8,128)(2,1)S(1)}, bf16[1,4,256,256]{3,2,1,0:T(8,128)(2,1)}, u32[]{:S(2)}) copy-start(bf16[1,4,256,256]{3,2,1,0:T(8,128)(2,1)} %constant.6.clone.tables) | copy-start | bytes 1572868
  20.6 14.7 %collective-permute-start = (f32[2,2,256,256]{3,2,1,0:T(8,128)S(1)}, f32[2,2,256,256]{3,2,1,0:T(8,128)S(1)}, u32[]{:S(2)}, u32[]{:S(2)}) collective-permute-start(f32[2,2,256,256]{3,2,1,0:T(8,128)S(1)} %copy-done), channel_id=1, source_target_pairs={{0,1},{1,0},{2,3},{3,2},{4,5},{5,4},{6,7},{7,6},{8,9},{9,8},{10,11... | collective-permute-start | bytes 3145736 | tf_op jit(solution)/shard_map/ppermute | solution.py:482
  39.0 2.4 %collective-permute-start.1 = (bf16[16,96,256]{2,1,0:T(8,128)(2,1)S(1)}, bf16[16,96,256]{2,1,0:T(8,128)(2,1)S(1)}, u32[]{:S(2)}, u32[]{:S(2)}) collective-permute-start(bf16[16,96,256]{2,1,0:T(8,128)(2,1)S(1)} %get-tuple-element.35), channel_id=1, source_target_pairs={{0,1},{1,0},{2,3},{3,2},{4,5},{5,4},{6,7},{7,6},{8,9},{9,8},{10,11... | collective-permute-start | bytes 2359304 | tf_op jit(solution)/shard_map/ppermute | solution.py:482
  58.5 5.3 %collective-permute-start.4 = (bf16[80,256]{1,0:T(8,128)(2,1)S(1)}, bf16[80,256]{1,0:T(8,128)(2,1)S(1)}, u32[]{:S(2)}, u32[]{:S(2)}) collective-permute-start(bf16[80,256]{1,0:T(8,128)(2,1)S(1)} %shard_map.110.own), channel_id=1, source_target_pairs={{0,96},{32,0},{64,32},{96,64},{1,97},{33,1},{65,33},{97,65},{2,98}... | collective-permute-start | bytes 122888 | tf_op jit(solution)/shard_map/ppermute | solution.py:486
  61.1 4.4 %collective-permute-start.3 = (bf16[80,256]{1,0:T(8,128)(2,1)S(1)}, bf16[80,256]{1,0:T(8,128)(2,1)S(1)}, u32[]{:S(2)}, u32[]{:S(2)}) collective-permute-start(bf16[80,256]{1,0:T(8,128)(2,1)S(1)} %shard_map.110.own), channel_id=1, source_target_pairs={{0,64},{32,96},{64,0},{96,32},{1,65},{33,97},{65,1},{97,33},{2,66}... | collective-permute-start | bytes 122888 | tf_op jit(solution)/shard_map/ppermute | solution.py:486
  61.6 4.3 %collective-permute-start.2 = (bf16[80,256]{1,0:T(8,128)(2,1)S(1)}, bf16[80,256]{1,0:T(8,128)(2,1)S(1)}, u32[]{:S(2)}, u32[]{:S(2)}) collective-permute-start(bf16[80,256]{1,0:T(8,128)(2,1)S(1)} %shard_map.110.own), channel_id=1, source_target_pairs={{0,32},{32,64},{64,96},{96,0},{1,33},{33,65},{65,97},{97,1},{2,34}... | collective-permute-start | bytes 122888 | tf_op jit(solution)/shard_map/ppermute | solution.py:486
  80.3 6.6 %collective-permute-start.5 = (bf16[16,96,256]{2,1,0:T(8,128)(2,1)S(1)}, bf16[16,96,256]{2,1,0:T(8,128)(2,1)S(1)}, u32[]{:S(2)}, u32[]{:S(2)}) collective-permute-start(bf16[16,96,256]{2,1,0:T(8,128)(2,1)S(1)} %all_to_all.32.h_own.h_one), channel_id=1, source_target_pairs={{0,1},{1,0},{2,3},{3,2},{4,5},{5,4},{6,7},{7,6},{8,9},{9,8},{10,11... | collective-permute-start | bytes 2359304 | tf_op jit(solution)/shard_map/ppermute | solution.py:482
  90.8 2.5 %collective-permute-start.6 = (bf16[16,96,256]{2,1,0:T(8,128)(2,1)S(1)}, bf16[16,96,256]{2,1,0:T(8,128)(2,1)S(1)}, u32[]{:S(2)}, u32[]{:S(2)}) collective-permute-start(bf16[16,96,256]{2,1,0:T(8,128)(2,1)S(1)} %get-tuple-element.45), channel_id=1, source_target_pairs={{0,1},{1,0},{2,3},{3,2},{4,5},{5,4},{6,7},{7,6},{8,9},{9,8},{10,11... | collective-permute-start | bytes 2359304 | tf_op jit(solution)/shard_map/ppermute | solution.py:482
  110.9 2.9 %collective-permute-start.9 = (bf16[80,256]{1,0:T(8,128)(2,1)S(1)}, bf16[80,256]{1,0:T(8,128)(2,1)S(1)}, u32[]{:S(2)}, u32[]{:S(2)}) collective-permute-start(bf16[80,256]{1,0:T(8,128)(2,1)S(1)} %shard_map.116.own), channel_id=1, source_target_pairs={{0,96},{32,0},{64,32},{96,64},{1,97},{33,1},{65,33},{97,65},{2,98}... | collective-permute-start | bytes 122888 | tf_op jit(solution)/shard_map/ppermute | solution.py:486
  111.3 4.4 %collective-permute-start.8 = (bf16[80,256]{1,0:T(8,128)(2,1)S(1)}, bf16[80,256]{1,0:T(8,128)(2,1)S(1)}, u32[]{:S(2)}, u32[]{:S(2)}) collective-permute-start(bf16[80,256]{1,0:T(8,128)(2,1)S(1)} %shard_map.116.own), channel_id=1, source_target_pairs={{0,64},{32,96},{64,0},{96,32},{1,65},{33,97},{65,1},{97,33},{2,66}... | collective-permute-start | bytes 122888 | tf_op jit(solution)/shard_map/ppermute | solution.py:486
  112.2 4.1 %collective-permute-start.7 = (bf16[80,256]{1,0:T(8,128)(2,1)S(1)}, bf16[80,256]{1,0:T(8,128)(2,1)S(1)}, u32[]{:S(2)}, u32[]{:S(2)}) collective-permute-start(bf16[80,256]{1,0:T(8,128)(2,1)S(1)} %shard_map.116.own), channel_id=1, source_target_pairs={{0,32},{32,64},{64,96},{96,0},{1,33},{33,65},{65,97},{97,1},{2,34}... | collective-permute-start | bytes 122888 | tf_op jit(solution)/shard_map/ppermute | solution.py:486
  131.3 6.7 %copy-start.1 = (f32[2,264,256]{2,1,0:T(8,128)S(1)}, f32[2,264,256]{2,1,0:T(8,128)}, u32[]{:S(2)}) copy-start(f32[2,264,256]{2,1,0:T(8,128)} %obj.3) | copy-start | bytes 1622020
  131.3 6.6 %collective-permute-start.10 = (bf16[16,96,256]{2,1,0:T(8,128)(2,1)S(1)}, bf16[16,96,256]{2,1,0:T(8,128)(2,1)S(1)}, u32[]{:S(2)}, u32[]{:S(2)}) collective-permute-start(bf16[16,96,256]{2,1,0:T(8,128)(2,1)S(1)} %all_to_all.34.h_own.h_two), channel_id=1, source_target_pairs={{0,1},{1,0},{2,3},{3,2},{4,5},{5,4},{6,7},{7,6},{8,9},{9,8},{10,11... | collective-permute-start | bytes 2359304 | tf_op jit(solution)/shard_map/ppermute | solution.py:482

commit v5 on v4

--- a/solution.py
+++ b/solution.py
@@ -11,7 +11,7 @@
 
 PS = 256
 HALF = 128
-PARTS = 1
+PARTS = 2
 BH = 264
 N_TM = 16
 UNROLL = 16

time: 139 us -> 142 us (1.022)
  Pallas kernels: 19.3 us -> 22.5 us
    pallas_call x2, Pallas kernels: 7.48 us -> 10.7 us  [position(): call(functools.partial(position_kernel, with_update), (part, part, arr((2...]
where the time goes in v5:
time: 142 us
  blocking collectives  75.4 us (53%)
  starting transfers between devices  26.6 us (19%)
  Pallas kernels  22.5 us (16%)
  waiting for transfers between devices  15.9 us (11%)
  between operations  1.44 us (1%)
    all_to_all x4, blocking collectives, exchange(): return lax.all_to_all(x, 'tm', 0, 0)  62.8 us
    all_to_all x1, blocking collectives, body(): h_own = h_oth = lax.all_to_all(windows, ('tm', 'mode'), 0, 0)  12.6 us
    ppermute x5, starting transfers between devices, swap(): return lax.ppermute(x, 'mode', SWAP)  12.3 us
    pallas_call x2, Pallas kernels, position(): call(functools.partial(position_kernel, with_update), (part, part, arr((2...  10.7 us
    all_to_all x1, starting transfers between devices, exchange(): return lax.all_to_all(x, 'tm', 0, 0)  8.74 us
    all_to_all x1, waiting for transfers between devices, exchange(): return lax.all_to_all(x, 'tm', 0, 0)  6.96 us
    ppermute x6, starting transfers between devices, over_tiles(): lax.ppermute(x, 'tile', [(i, (i + k) % n) for i in range(n)])  5.61 us
    ppermute x6, waiting for transfers between devices, over_tiles(): lax.ppermute(x, 'tile', [(i, (i + k) % n) for i in range(n)])  4.56 us
  transfers between devices with their start and end apart: 12, of which 9 were waited for; matrix products, arithmetic and copies ran while one was open for 0% of the time, Pallas kernels for 5%

profile of v5, /device:TPU:1, one launch (start us, length us, event | category | flops | bytes accessed | tf_op | source)
XLA Modules:
  0.0 141.9 jit_solution(5111097689952015055)
XLA Ops:
  1.3 1.8 %shard_map.104 = bf16[16,32,256]{2,1,0:T(8,128)(2,1)} custom-call(s32[2]{0:T(128)} %bitcast.11, s32[2]{0:T(128)} %row_offset.1, s32[2]{0:T(128)} %col_offset.1, s32[1,1]{1,0:T(1,128)} %bitcast.3.live_counts, f32[2,264,256]{2,1,0:T(8,128)} %obj.3), custom_call_target="tpu_custom_call" | custom-call | bytes 1048576 | tf_op jit(solution)/shard_map/pallas_call | solution.py:491
  3.1 8.7 %all-to-all-start = ((bf16[16,32,256]{2,1,0:T(8,128)(2,1)}), bf16[16,32,256]{2,1,0:T(8,128)(2,1)S(1)}, u32[]{:S(2)}, u32[]{:S(2)}) async-start(bf16[16,32,256]{2,1,0:T(8,128)(2,1)} %shard_map.104), calls=%async_computation | async-start | bytes 524288 | tf_op jit(solution)/shard_map/all_to_all | solution.py:479
  12.4 7.0 %all-to-all-done.high = bf16[16,32,256]{2,1,0:T(8,128)(2,1)S(1)} async-done(((bf16[16,32,256]{2,1,0:T(8,128)(2,1)}), bf16[16,32,256]{2,1,0:T(8,128)(2,1)S(1)}, u32[]{:S(2)}, u32[]{:S(2)}) %all-to-all-start) | async-done | bytes 262176 | tf_op jit(solution)/shard_map/all_to_all | solution.py:479
  19.3 1.3 shard_map.106
  20.6 2.1 %collective-permute-start = (f32[2,2,256,256]{3,2,1,0:T(8,128)S(1)}, f32[2,2,256,256]{3,2,1,0:T(8,128)S(1)}, u32[]{:S(2)}, u32[]{:S(2)}) collective-permute-start(f32[2,2,256,256]{3,2,1,0:T(8,128)S(1)} %copy-done.1), channel_id=1, source_target_pairs={{0,1},{1,0},{2,3},{3,2},{4,5},{5,4},{6,7},{7,6},{8,9},{9,8},{10,11... | collective-permute-start | bytes 3145736 | tf_op jit(solution)/shard_map/ppermute | solution.py:482
  22.7 12.6 %all_to_all.30.h_own.h_oth = bf16[32,16,256]{2,1,0:T(8,128)(2,1)S(1)} all-to-all(bf16[32,16,256]{2,1,0:T(8,128)(2,1)S(1)} %get-tuple-element.31), channel_id=1, replica_groups=mesh['tile'=4,'tm'=16,'mode'=2] {'tm','mode'}, dimensions={0} | all-to-all | bytes 524288 | tf_op jit(solution)/shard_map/all_to_all | solution.py:509
  35.3 5.3 %shard_map.107 = (bf16[16,96,256]{2,1,0:T(8,128)(2,1)S(1)}, bf16[16,96,256]{2,1,0:T(8,128)(2,1)S(1)}, f32[272,256]{1,0:T(8,128)S(1)}) custom-call(s32[16,8]{1,0:T(8,128)S(1)} %bitcast.5, bf16[2,4,256,256]{3,2,1,0:T(8,128)(2,1)S(1)} %copy-done.4, f32[2,2,256,256]{3,2,1,0:T(8,128)S(1)} %copy-done.1, f32[2,2,256,256]{3,2,1,0:T(8,128)S(1)} %collective-permute-done.p_oth, ...), custom_call_target="tpu_custom_call" | custom-call | flops 2147483648 | bytes 10485760 | tf_op jit(solution)/shard_map/pallas_call | solution.py:422
  40.9 1.1 shard_map.108.scale
  42.0 0.9 collective-permute-done.1.recv
  43.2 16.9 %all_to_all.31.parts = bf16[16,112,256]{2,1,0:T(8,128)(2,1)S(1)} all-to-all(bf16[16,112,256]{2,1,0:T(8,128)(2,1)S(1)} %get-tuple-element.38), channel_id=1, replica_groups=mesh['tile'=4,'tm'=16,'mode'=2] {'tm'}, dimensions={0} | all-to-all | bytes 1835008 | tf_op jit(solution)/shard_map/all_to_all | solution.py:479
  60.2 2.5 %collective-permute-start.4 = (bf16[80,256]{1,0:T(8,128)(2,1)S(1)}, bf16[80,256]{1,0:T(8,128)(2,1)S(1)}, u32[]{:S(2)}, u32[]{:S(2)}) collective-permute-start(bf16[80,256]{1,0:T(8,128)(2,1)S(1)} %shard_map.110.own), channel_id=1, source_target_pairs={{0,96},{32,0},{64,32},{96,64},{1,97},{33,1},{65,33},{97,65},{2,98}... | collective-permute-start | bytes 122888 | tf_op jit(solution)/shard_map/ppermute | solution.py:486
  63.8 1.6 %shard_map.111 = (bf16[16,32,256]{2,1,0:T(8,128)(2,1)S(1)}, f32[16,256]{1,0:T(8,128)S(1)}, f32[16,24,256]{2,1,0:T(8,128)S(1)}) custom-call(s32[16,8]{1,0:T(8,128)S(1)} %bitcast.7, bf16[16,112,256]{2,1,0:T(8,128)(2,1)S(1)} %all_to_all.31.parts, f32[16,24,256]{2,1,0:T(8,128)S(1)} %shard_map.108.scale, bf16[16,32,256]{2,1,0:T(8,128)(2,1)S(1)} %all-to-all-done.high), custom_call_target="tpu_custom_call" | custom-call | bytes 1048576 | tf_op jit(solution)/shard_map/pallas_call | solution.py:528
  65.4 1.7 %collective-permute-done.3.two = bf16[80,256]{1,0:T(8,128)(2,1)S(1)} collective-permute-done((bf16[80,256]{1,0:T(8,128)(2,1)S(1)}, bf16[80,256]{1,0:T(8,128)(2,1)S(1)}, u32[]{:S(2)}, u32[]{:S(2)}) %collective-permute-start.3) | collective-permute-done | bytes 40992 | tf_op jit(solution)/shard_map/ppermute | solution.py:486
  67.6 14.4 %all_to_all.32.h_own.h_one = bf16[16,96,256]{2,1,0:T(8,128)(2,1)S(1)} all-to-all(bf16[16,96,256]{2,1,0:T(8,128)(2,1)S(1)} %get-tuple-element.42), channel_id=1, replica_groups=mesh['tile'=4,'tm'=16,'mode'=2] {'tm'}, dimensions={0} | all-to-all | bytes 1572864 | tf_op jit(solution)/shard_map/all_to_all | solution.py:479
  82.0 4.7 %collective-permute-start.5 = (bf16[16,96,256]{2,1,0:T(8,128)(2,1)S(1)}, bf16[16,96,256]{2,1,0:T(8,128)(2,1)S(1)}, u32[]{:S(2)}, u32[]{:S(2)}) collective-permute-start(bf16[16,96,256]{2,1,0:T(8,128)(2,1)S(1)} %all_to_all.32.h_own.h_one), channel_id=1, source_target_pairs={{0,1},{1,0},{2,3},{3,2},{4,5},{5,4},{6,7},{7,6},{8,9},{9,8},{10,11... | collective-permute-start | bytes 2359304 | tf_op jit(solution)/shard_map/ppermute | solution.py:482
  86.7 1.9 %collective-permute-done.5.h_oth = bf16[16,96,256]{2,1,0:T(8,128)(2,1)S(1)} collective-permute-done((bf16[16,96,256]{2,1,0:T(8,128)(2,1)S(1)}, bf16[16,96,256]{2,1,0:T(8,128)(2,1)S(1)}, u32[]{:S(2)}, u32[]{:S(2)}) %collective-permute-start.5) | collective-permute-done | bytes 786464 | tf_op jit(solution)/shard_map/ppermute | solution.py:482
  88.6 5.4 %shard_map.113 = (bf16[16,96,256]{2,1,0:T(8,128)(2,1)S(1)}, bf16[16,96,256]{2,1,0:T(8,128)(2,1)S(1)}, f32[272,256]{1,0:T(8,128)S(1)}) custom-call(s32[16,8]{1,0:T(8,128)S(1)} %bitcast.8, bf16[2,4,256,256]{3,2,1,0:T(8,128)(2,1)S(1)} %copy-done.4, f32[2,2,256,256]{3,2,1,0:T(8,128)S(1)} %copy-done.1, f32[2,2,256,256]{3,2,1,0:T(8,128)S(1)} %collective-permute-done.p_oth, ...), custom_call_target="tpu_custom_call" | custom-call | flops 2147483648 | bytes 10485760 | tf_op jit(solution)/shard_map/pallas_call | solution.py:422
  94.5 1.1 shard_map.114.scale
  96.6 17.2 %all_to_all.33.parts = bf16[16,112,256]{2,1,0:T(8,128)(2,1)S(1)} all-to-all(bf16[16,112,256]{2,1,0:T(8,128)(2,1)S(1)} %get-tuple-element.48), channel_id=1, replica_groups=mesh['tile'=4,'tm'=16,'mode'=2] {'tm'}, dimensions={0} | all-to-all | bytes 1835008 | tf_op jit(solution)/shard_map/all_to_all | solution.py:479
  115.9 1.0 shard_map.117.objs
  116.9 1.9 %collective-permute-done.8.two = bf16[80,256]{1,0:T(8,128)(2,1)S(1)} collective-permute-done((bf16[80,256]{1,0:T(8,128)(2,1)S(1)}, bf16[80,256]{1,0:T(8,128)(2,1)S(1)}, u32[]{:S(2)}, u32[]{:S(2)}) %collective-permute-start.8) | collective-permute-done | bytes 40992 | tf_op jit(solution)/shard_map/ppermute | solution.py:486
  120.1 14.4 %all_to_all.34.h_own.h_two = bf16[16,96,256]{2,1,0:T(8,128)(2,1)S(1)} all-to-all(bf16[16,96,256]{2,1,0:T(8,128)(2,1)S(1)} %get-tuple-element.53), channel_id=1, replica_groups=mesh['tile'=4,'tm'=16,'mode'=2] {'tm'}, dimensions={0} | all-to-all | bytes 1572864 | tf_op jit(solution)/shard_map/all_to_all | solution.py:479
  134.4 4.7 %collective-permute-start.10 = (bf16[16,96,256]{2,1,0:T(8,128)(2,1)S(1)}, bf16[16,96,256]{2,1,0:T(8,128)(2,1)S(1)}, u32[]{:S(2)}, u32[]{:S(2)}) collective-permute-start(bf16[16,96,256]{2,1,0:T(8,128)(2,1)S(1)} %all_to_all.34.h_own.h_two), channel_id=1, source_target_pairs={{0,1},{1,0},{2,3},{3,2},{4,5},{5,4},{6,7},{7,6},{8,9},{9,8},{10,11... | collective-permute-start | bytes 2359304 | tf_op jit(solution)/shard_map/ppermute | solution.py:482
  139.1 1.2 shard_map.120
  (34 shorter events, 9.1 us)
Async XLA Ops:
  1.3 10.6 %copy-start.2 = (f32[2,256,256]{2,1,0:T(8,128)S(1)}, f32[2,256,256]{2,1,0:T(8,128)}, u32[]{:S(2)}) copy-start(f32[2,256,256]{2,1,0:T(8,128)} %amp.1) | copy-start | bytes 1572868
  1.3 10.6 %copy-start.3 = (bf16[256,256]{1,0:T(8,128)(2,1)S(1)}, bf16[256,256]{1,0:T(8,128)(2,1)}, u32[]{:S(2)}) copy-start(bf16[256,256]{1,0:T(8,128)(2,1)} %constant.7.clone.table) | copy-start | bytes 393220
  3.1 17.5 %copy-start.1 = (f32[2,2,256,256]{3,2,1,0:T(8,128)S(1)}, f32[2,2,256,256]{3,2,1,0:T(8,128)}, u32[]{:S(2)}) copy-start(f32[2,2,256,256]{3,2,1,0:T(8,128)} %p_own.5) | copy-start | bytes 3145732
  3.1 32.2 %copy-start.4 = (bf16[2,4,256,256]{3,2,1,0:T(8,128)(2,1)S(1)}, bf16[2,4,256,256]{3,2,1,0:T(8,128)(2,1)}, u32[]{:S(2)}) copy-start(bf16[2,4,256,256]{3,2,1,0:T(8,128)(2,1)} %constant.6.clone.tables) | copy-start | bytes 3145732
  3.1 16.2 %all-to-all-start = ((bf16[16,32,256]{2,1,0:T(8,128)(2,1)}), bf16[16,32,256]{2,1,0:T(8,128)(2,1)S(1)}, u32[]{:S(2)}, u32[]{:S(2)}) async-start(bf16[16,32,256]{2,1,0:T(8,128)(2,1)} %shard_map.104), calls=%async_computation | async-start | bytes 524288 | tf_op jit(solution)/shard_map/all_to_all | solution.py:479
  20.6 14.7 %collective-permute-start = (f32[2,2,256,256]{3,2,1,0:T(8,128)S(1)}, f32[2,2,256,256]{3,2,1,0:T(8,128)S(1)}, u32[]{:S(2)}, u32[]{:S(2)}) collective-permute-start(f32[2,2,256,256]{3,2,1,0:T(8,128)S(1)} %copy-done.1), channel_id=1, source_target_pairs={{0,1},{1,0},{2,3},{3,2},{4,5},{5,4},{6,7},{7,6},{8,9},{9,8},{10,11... | collective-permute-start | bytes 3145736 | tf_op jit(solution)/shard_map/ppermute | solution.py:482
  40.6 2.4 %collective-permute-start.1 = (bf16[16,96,256]{2,1,0:T(8,128)(2,1)S(1)}, bf16[16,96,256]{2,1,0:T(8,128)(2,1)S(1)}, u32[]{:S(2)}, u32[]{:S(2)}) collective-permute-start(bf16[16,96,256]{2,1,0:T(8,128)(2,1)S(1)} %get-tuple-element.35), channel_id=1, source_target_pairs={{0,1},{1,0},{2,3},{3,2},{4,5},{5,4},{6,7},{7,6},{8,9},{9,8},{10,11... | collective-permute-start | bytes 2359304 | tf_op jit(solution)/shard_map/ppermute | solution.py:482
  60.2 5.2 %collective-permute-start.4 = (bf16[80,256]{1,0:T(8,128)(2,1)S(1)}, bf16[80,256]{1,0:T(8,128)(2,1)S(1)}, u32[]{:S(2)}, u32[]{:S(2)}) collective-permute-start(bf16[80,256]{1,0:T(8,128)(2,1)S(1)} %shard_map.110.own), channel_id=1, source_target_pairs={{0,96},{32,0},{64,32},{96,64},{1,97},{33,1},{65,33},{97,65},{2,98}... | collective-permute-start | bytes 122888 | tf_op jit(solution)/shard_map/ppermute | solution.py:486
  62.7 4.4 %collective-permute-start.3 = (bf16[80,256]{1,0:T(8,128)(2,1)S(1)}, bf16[80,256]{1,0:T(8,128)(2,1)S(1)}, u32[]{:S(2)}, u32[]{:S(2)}) collective-permute-start(bf16[80,256]{1,0:T(8,128)(2,1)S(1)} %shard_map.110.own), channel_id=1, source_target_pairs={{0,64},{32,96},{64,0},{96,32},{1,65},{33,97},{65,1},{97,33},{2,66}... | collective-permute-start | bytes 122888 | tf_op jit(solution)/shard_map/ppermute | solution.py:486
  63.2 4.3 %collective-permute-start.2 = (bf16[80,256]{1,0:T(8,128)(2,1)S(1)}, bf16[80,256]{1,0:T(8,128)(2,1)S(1)}, u32[]{:S(2)}, u32[]{:S(2)}) collective-permute-start(bf16[80,256]{1,0:T(8,128)(2,1)S(1)} %shard_map.110.own), channel_id=1, source_target_pairs={{0,32},{32,64},{64,96},{96,0},{1,33},{33,65},{65,97},{97,1},{2,34}... | collective-permute-start | bytes 122888 | tf_op jit(solution)/shard_map/ppermute | solution.py:486
  82.0 6.6 %collective-permute-start.5 = (bf16[16,96,256]{2,1,0:T(8,128)(2,1)S(1)}, bf16[16,96,256]{2,1,0:T(8,128)(2,1)S(1)}, u32[]{:S(2)}, u32[]{:S(2)}) collective-permute-start(bf16[16,96,256]{2,1,0:T(8,128)(2,1)S(1)} %all_to_all.32.h_own.h_one), channel_id=1, source_target_pairs={{0,1},{1,0},{2,3},{3,2},{4,5},{5,4},{6,7},{7,6},{8,9},{9,8},{10,11... | collective-permute-start | bytes 2359304 | tf_op jit(solution)/shard_map/ppermute | solution.py:482
  94.0 2.4 %collective-permute-start.6 = (bf16[16,96,256]{2,1,0:T(8,128)(2,1)S(1)}, bf16[16,96,256]{2,1,0:T(8,128)(2,1)S(1)}, u32[]{:S(2)}, u32[]{:S(2)}) collective-permute-start(bf16[16,96,256]{2,1,0:T(8,128)(2,1)S(1)} %get-tuple-element.45), channel_id=1, source_target_pairs={{0,1},{1,0},{2,3},{3,2},{4,5},{5,4},{6,7},{7,6},{8,9},{9,8},{10,11... | collective-permute-start | bytes 2359304 | tf_op jit(solution)/shard_map/ppermute | solution.py:482
  113.9 2.9 %collective-permute-start.9 = (bf16[80,256]{1,0:T(8,128)(2,1)S(1)}, bf16[80,256]{1,0:T(8,128)(2,1)S(1)}, u32[]{:S(2)}, u32[]{:S(2)}) collective-permute-start(bf16[80,256]{1,0:T(8,128)(2,1)S(1)} %shard_map.116.own), channel_id=1, source_target_pairs={{0,96},{32,0},{64,32},{96,64},{1,97},{33,1},{65,33},{97,65},{2,98}... | collective-permute-start | bytes 122888 | tf_op jit(solution)/shard_map/ppermute | solution.py:486
  114.4 4.4 %collective-permute-start.8 = (bf16[80,256]{1,0:T(8,128)(2,1)S(1)}, bf16[80,256]{1,0:T(8,128)(2,1)S(1)}, u32[]{:S(2)}, u32[]{:S(2)}) collective-permute-start(bf16[80,256]{1,0:T(8,128)(2,1)S(1)} %shard_map.116.own), channel_id=1, source_target_pairs={{0,64},{32,96},{64,0},{96,32},{1,65},{33,97},{65,1},{97,33},{2,66}... | collective-permute-start | bytes 122888 | tf_op jit(solution)/shard_map/ppermute | solution.py:486
  115.3 4.1 %collective-permute-start.7 = (bf16[80,256]{1,0:T(8,128)(2,1)S(1)}, bf16[80,256]{1,0:T(8,128)(2,1)S(1)}, u32[]{:S(2)}, u32[]{:S(2)}) collective-permute-start(bf16[80,256]{1,0:T(8,128)(2,1)S(1)} %shard_map.116.own), channel_id=1, source_target_pairs={{0,32},{32,64},{64,96},{96,0},{1,33},{33,65},{65,97},{97,1},{2,34}... | collective-permute-start | bytes 122888 | tf_op jit(solution)/shard_map/ppermute | solution.py:486
  134.4 6.7 %copy-start = (f32[2,264,256]{2,1,0:T(8,128)S(1)}, f32[2,264,256]{2,1,0:T(8,128)}, u32[]{:S(2)}) copy-start(f32[2,264,256]{2,1,0:T(8,128)} %obj.3) | copy-start | bytes 1622020
  134.4 6.6 %collective-permute-start.10 = (bf16[16,96,256]{2,1,0:T(8,128)(2,1)S(1)}, bf16[16,96,256]{2,1,0:T(8,128)(2,1)S(1)}, u32[]{:S(2)}, u32[]{:S(2)}) collective-permute-start(bf16[16,96,256]{2,1,0:T(8,128)(2,1)S(1)} %all_to_all.34.h_own.h_two), channel_id=1, source_target_pairs={{0,1},{1,0},{2,3},{3,2},{4,5},{5,4},{6,7},{7,6},{8,9},{9,8},{10,11... | collective-permute-start | bytes 2359304 | tf_op jit(solution)/shard_map/ppermute | solution.py:482

commit v6 on v4

--- a/solution.py
+++ b/solution.py
@@ -123,7 +123,7 @@
             total = total + both * both * alive.astype(F32)
         return total
 
-    denom[...] = lax.fori_loop(0, N_TM, visit, jnp.zeros((CH, PS), F32), unroll=4)
+    denom[...] = lax.fori_loop(0, N_TM, visit, jnp.zeros((CH, PS), F32), unroll=UNROLL)
 
 
 def window_kernel(meta, high, out, denom):
@@ -262,7 +262,9 @@
     keep, send, power, obj, probe, x_even, x_odd, y_even, y_odd, half_even, half_odd, far_even, far_odd, shifted,
     left, right,
 ):
-    for k in range(4):
+    if PARTS == 1:
+        left = right = tables.at[0]
+    for k in range(4 if PARTS > 1 else 0):
         for part, which in enumerate((0, 0, 1)[:PARTS]):
             left[k, :, part * PS : (part + 1) * PS] = tables[which, k]
             right[k, part * PS : (part + 1) * PS, :] = tables[which, k]

time: 139 us -> 139 us (level)
  transfers between devices with their start and end apart: 12 -> 12, of which waited for: 9 -> 9; matrix products, arithmetic and copies ran while one was open for 0% -> 0% of each run, Pallas kernels for 5% -> 4%
where the time goes in v6:
time: 139 us
  blocking collectives  75.4 us (54%)
  starting transfers between devices  26.8 us (19%)
  Pallas kernels  18.8 us (14%)
  waiting for transfers between devices  16 us (12%)
  between operations  1.46 us (1%)
    all_to_all x4, blocking collectives, exchange(): return lax.all_to_all(x, 'tm', 0, 0)  62.8 us
    all_to_all x1, blocking collectives, body(): h_own = h_oth = lax.all_to_all(windows, ('tm', 'mode'), 0, 0)  12.6 us
    ppermute x5, starting transfers between devices, swap(): return lax.ppermute(x, 'mode', SWAP)  12.4 us
    all_to_all x1, starting transfers between devices, exchange(): return lax.all_to_all(x, 'tm', 0, 0)  8.74 us
    pallas_call x2, Pallas kernels, position(): call(functools.partial(position_kernel, with_update), (part, part, arr((2...  7.48 us
    all_to_all x1, waiting for transfers between devices, exchange(): return lax.all_to_all(x, 'tm', 0, 0)  6.94 us
    ppermute x6, starting transfers between devices, over_tiles(): lax.ppermute(x, 'tile', [(i, (i + k) % n) for i in range(n)])  5.64 us
    ppermute x6, waiting for transfers between devices, over_tiles(): lax.ppermute(x, 'tile', [(i, (i + k) % n) for i in range(n)])  4.68 us
  transfers between devices with their start and end apart: 12, of which 9 were waited for; matrix products, arithmetic and copies ran while one was open for 0% of the time, Pallas kernels for 4%

profile of v6, /device:TPU:1, one launch (start us, length us, event | category | flops | bytes accessed | tf_op | source)
XLA Modules:
  0.0 138.6 jit_solution(1292460161275380122)
XLA Ops:
  1.3 1.8 %shard_map.104 = bf16[16,32,256]{2,1,0:T(8,128)(2,1)} custom-call(s32[2]{0:T(128)} %bitcast.11, s32[2]{0:T(128)} %row_offset.1, s32[2]{0:T(128)} %col_offset.1, s32[1,1]{1,0:T(1,128)} %bitcast.3.live_counts, f32[2,264,256]{2,1,0:T(8,128)} %obj.3), custom_call_target="tpu_custom_call" | custom-call | bytes 1048576 | tf_op jit(solution)/shard_map/pallas_call | solution.py:493
  3.1 8.7 %all-to-all-start = ((bf16[16,32,256]{2,1,0:T(8,128)(2,1)}), bf16[16,32,256]{2,1,0:T(8,128)(2,1)S(1)}, u32[]{:S(2)}, u32[]{:S(2)}) async-start(bf16[16,32,256]{2,1,0:T(8,128)(2,1)} %shard_map.104), calls=%async_computation | async-start | bytes 524288 | tf_op jit(solution)/shard_map/all_to_all | solution.py:481
  12.4 6.9 %all-to-all-done.high = bf16[16,32,256]{2,1,0:T(8,128)(2,1)S(1)} async-done(((bf16[16,32,256]{2,1,0:T(8,128)(2,1)}), bf16[16,32,256]{2,1,0:T(8,128)(2,1)S(1)}, u32[]{:S(2)}, u32[]{:S(2)}) %all-to-all-start) | async-done | bytes 262176 | tf_op jit(solution)/shard_map/all_to_all | solution.py:481
  19.3 1.1 shard_map.106
  20.4 2.1 %collective-permute-start = (f32[2,2,256,256]{3,2,1,0:T(8,128)S(1)}, f32[2,2,256,256]{3,2,1,0:T(8,128)S(1)}, u32[]{:S(2)}, u32[]{:S(2)}) collective-permute-start(f32[2,2,256,256]{3,2,1,0:T(8,128)S(1)} %copy-done), channel_id=1, source_target_pairs={{0,1},{1,0},{2,3},{3,2},{4,5},{5,4},{6,7},{7,6},{8,9},{9,8},{10,11... | collective-permute-start | bytes 3145736 | tf_op jit(solution)/shard_map/ppermute | solution.py:484
  22.5 12.6 %all_to_all.30.h_own.h_oth = bf16[32,16,256]{2,1,0:T(8,128)(2,1)S(1)} all-to-all(bf16[32,16,256]{2,1,0:T(8,128)(2,1)S(1)} %get-tuple-element.31), channel_id=1, replica_groups=mesh['tile'=4,'tm'=16,'mode'=2] {'tm','mode'}, dimensions={0} | all-to-all | bytes 524288 | tf_op jit(solution)/shard_map/all_to_all | solution.py:511
  35.1 3.7 %shard_map.107 = (bf16[16,96,256]{2,1,0:T(8,128)(2,1)S(1)}, bf16[16,96,256]{2,1,0:T(8,128)(2,1)S(1)}, f32[272,256]{1,0:T(8,128)S(1)}) custom-call(s32[16,8]{1,0:T(8,128)S(1)} %bitcast.5, bf16[1,4,256,256]{3,2,1,0:T(8,128)(2,1)S(1)} %copy-done.2, f32[2,2,256,256]{3,2,1,0:T(8,128)S(1)} %copy-done, f32[2,2,256,256]{3,2,1,0:T(8,128)S(1)} %collective-permute-done.p_oth, ...), custom_call_target="tpu_custom_call" | custom-call | flops 1073741824 | bytes 10485760 | tf_op jit(solution)/shard_map/pallas_call | solution.py:424
  39.0 1.1 shard_map.108.scale
  40.2 1.0 collective-permute-done.1.recv
  41.3 16.8 %all_to_all.31.parts = bf16[16,112,256]{2,1,0:T(8,128)(2,1)S(1)} all-to-all(bf16[16,112,256]{2,1,0:T(8,128)(2,1)S(1)} %get-tuple-element.38), channel_id=1, replica_groups=mesh['tile'=4,'tm'=16,'mode'=2] {'tm'}, dimensions={0} | all-to-all | bytes 1835008 | tf_op jit(solution)/shard_map/all_to_all | solution.py:481
  58.3 2.5 %collective-permute-start.4 = (bf16[80,256]{1,0:T(8,128)(2,1)S(1)}, bf16[80,256]{1,0:T(8,128)(2,1)S(1)}, u32[]{:S(2)}, u32[]{:S(2)}) collective-permute-start(bf16[80,256]{1,0:T(8,128)(2,1)S(1)} %shard_map.110.own), channel_id=1, source_target_pairs={{0,96},{32,0},{64,32},{96,64},{1,97},{33,1},{65,33},{97,65},{2,98}... | collective-permute-start | bytes 122888 | tf_op jit(solution)/shard_map/ppermute | solution.py:488
  62.0 1.3 shard_map.111
  63.4 1.9 %collective-permute-done.3.two = bf16[80,256]{1,0:T(8,128)(2,1)S(1)} collective-permute-done((bf16[80,256]{1,0:T(8,128)(2,1)S(1)}, bf16[80,256]{1,0:T(8,128)(2,1)S(1)}, u32[]{:S(2)}, u32[]{:S(2)}) %collective-permute-start.3) | collective-permute-done | bytes 40992 | tf_op jit(solution)/shard_map/ppermute | solution.py:488
  65.7 14.4 %all_to_all.32.h_own.h_one = bf16[16,96,256]{2,1,0:T(8,128)(2,1)S(1)} all-to-all(bf16[16,96,256]{2,1,0:T(8,128)(2,1)S(1)} %get-tuple-element.42), channel_id=1, replica_groups=mesh['tile'=4,'tm'=16,'mode'=2] {'tm'}, dimensions={0} | all-to-all | bytes 1572864 | tf_op jit(solution)/shard_map/all_to_all | solution.py:481
  80.1 4.7 %collective-permute-start.5 = (bf16[16,96,256]{2,1,0:T(8,128)(2,1)S(1)}, bf16[16,96,256]{2,1,0:T(8,128)(2,1)S(1)}, u32[]{:S(2)}, u32[]{:S(2)}) collective-permute-start(bf16[16,96,256]{2,1,0:T(8,128)(2,1)S(1)} %all_to_all.32.h_own.h_one), channel_id=1, source_target_pairs={{0,1},{1,0},{2,3},{3,2},{4,5},{5,4},{6,7},{7,6},{8,9},{9,8},{10,11... | collective-permute-start | bytes 2359304 | tf_op jit(solution)/shard_map/ppermute | solution.py:484
  84.8 1.9 %collective-permute-done.5.h_oth = bf16[16,96,256]{2,1,0:T(8,128)(2,1)S(1)} collective-permute-done((bf16[16,96,256]{2,1,0:T(8,128)(2,1)S(1)}, bf16[16,96,256]{2,1,0:T(8,128)(2,1)S(1)}, u32[]{:S(2)}, u32[]{:S(2)}) %collective-permute-start.5) | collective-permute-done | bytes 786464 | tf_op jit(solution)/shard_map/ppermute | solution.py:484
  86.8 3.8 %shard_map.113 = (bf16[16,96,256]{2,1,0:T(8,128)(2,1)S(1)}, bf16[16,96,256]{2,1,0:T(8,128)(2,1)S(1)}, f32[272,256]{1,0:T(8,128)S(1)}) custom-call(s32[16,8]{1,0:T(8,128)S(1)} %bitcast.8, bf16[1,4,256,256]{3,2,1,0:T(8,128)(2,1)S(1)} %copy-done.2, f32[2,2,256,256]{3,2,1,0:T(8,128)S(1)} %copy-done, f32[2,2,256,256]{3,2,1,0:T(8,128)S(1)} %collective-permute-done.p_oth, ...), custom_call_target="tpu_custom_call" | custom-call | flops 1073741824 | bytes 10485760 | tf_op jit(solution)/shard_map/pallas_call | solution.py:424
  91.2 1.1 shard_map.114.scale
  93.3 17.2 %all_to_all.33.parts = bf16[16,112,256]{2,1,0:T(8,128)(2,1)S(1)} all-to-all(bf16[16,112,256]{2,1,0:T(8,128)(2,1)S(1)} %get-tuple-element.48), channel_id=1, replica_groups=mesh['tile'=4,'tm'=16,'mode'=2] {'tm'}, dimensions={0} | all-to-all | bytes 1835008 | tf_op jit(solution)/shard_map/all_to_all | solution.py:481
  112.6 1.0 shard_map.117.objs
  113.6 1.9 %collective-permute-done.8.two = bf16[80,256]{1,0:T(8,128)(2,1)S(1)} collective-permute-done((bf16[80,256]{1,0:T(8,128)(2,1)S(1)}, bf16[80,256]{1,0:T(8,128)(2,1)S(1)}, u32[]{:S(2)}, u32[]{:S(2)}) %collective-permute-start.8) | collective-permute-done | bytes 40992 | tf_op jit(solution)/shard_map/ppermute | solution.py:488
  116.7 14.4 %all_to_all.34.h_own.h_two = bf16[16,96,256]{2,1,0:T(8,128)(2,1)S(1)} all-to-all(bf16[16,96,256]{2,1,0:T(8,128)(2,1)S(1)} %get-tuple-element.53), channel_id=1, replica_groups=mesh['tile'=4,'tm'=16,'mode'=2] {'tm'}, dimensions={0} | all-to-all | bytes 1572864 | tf_op jit(solution)/shard_map/all_to_all | solution.py:481
  131.1 4.7 %collective-permute-start.10 = (bf16[16,96,256]{2,1,0:T(8,128)(2,1)S(1)}, bf16[16,96,256]{2,1,0:T(8,128)(2,1)S(1)}, u32[]{:S(2)}, u32[]{:S(2)}) collective-permute-start(bf16[16,96,256]{2,1,0:T(8,128)(2,1)S(1)} %all_to_all.34.h_own.h_two), channel_id=1, source_target_pairs={{0,1},{1,0},{2,3},{3,2},{4,5},{5,4},{6,7},{7,6},{8,9},{9,8},{10,11... | collective-permute-start | bytes 2359304 | tf_op jit(solution)/shard_map/ppermute | solution.py:484
  135.8 1.2 shard_map.120
  (34 shorter events, 9.2 us)
Async XLA Ops:
  1.3 10.6 %copy-start.3 = (f32[2,256,256]{2,1,0:T(8,128)S(1)}, f32[2,256,256]{2,1,0:T(8,128)}, u32[]{:S(2)}) copy-start(f32[2,256,256]{2,1,0:T(8,128)} %amp.1) | copy-start | bytes 1572868
  1.3 10.6 %copy-start.4 = (bf16[256,256]{1,0:T(8,128)(2,1)S(1)}, bf16[256,256]{1,0:T(8,128)(2,1)}, u32[]{:S(2)}) copy-start(bf16[256,256]{1,0:T(8,128)(2,1)} %constant.7.clone.table) | copy-start | bytes 393220
  3.1 17.3 %copy-start = (f32[2,2,256,256]{3,2,1,0:T(8,128)S(1)}, f32[2,2,256,256]{3,2,1,0:T(8,128)}, u32[]{:S(2)}) copy-start(f32[2,2,256,256]{3,2,1,0:T(8,128)} %p_own.5) | copy-start | bytes 3145732
  3.1 16.2 %all-to-all-start = ((bf16[16,32,256]{2,1,0:T(8,128)(2,1)}), bf16[16,32,256]{2,1,0:T(8,128)(2,1)S(1)}, u32[]{:S(2)}, u32[]{:S(2)}) async-start(bf16[16,32,256]{2,1,0:T(8,128)(2,1)} %shard_map.104), calls=%async_computation | async-start | bytes 524288 | tf_op jit(solution)/shard_map/all_to_all | solution.py:481
  12.4 22.7 %copy-start.2 = (bf16[1,4,256,256]{3,2,1,0:T(8,128)(2,1)S(1)}, bf16[1,4,256,256]{3,2,1,0:T(8,128)(2,1)}, u32[]{:S(2)}) copy-start(bf16[1,4,256,256]{3,2,1,0:T(8,128)(2,1)} %constant.6.clone.tables) | copy-start | bytes 1572868
  20.4 14.7 %collective-permute-start = (f32[2,2,256,256]{3,2,1,0:T(8,128)S(1)}, f32[2,2,256,256]{3,2,1,0:T(8,128)S(1)}, u32[]{:S(2)}, u32[]{:S(2)}) collective-permute-start(f32[2,2,256,256]{3,2,1,0:T(8,128)S(1)} %copy-done), channel_id=1, source_target_pairs={{0,1},{1,0},{2,3},{3,2},{4,5},{5,4},{6,7},{7,6},{8,9},{9,8},{10,11... | collective-permute-start | bytes 3145736 | tf_op jit(solution)/shard_map/ppermute | solution.py:484
  38.8 2.4 %collective-permute-start.1 = (bf16[16,96,256]{2,1,0:T(8,128)(2,1)S(1)}, bf16[16,96,256]{2,1,0:T(8,128)(2,1)S(1)}, u32[]{:S(2)}, u32[]{:S(2)}) collective-permute-start(bf16[16,96,256]{2,1,0:T(8,128)(2,1)S(1)} %get-tuple-element.35), channel_id=1, source_target_pairs={{0,1},{1,0},{2,3},{3,2},{4,5},{5,4},{6,7},{7,6},{8,9},{9,8},{10,11... | collective-permute-start | bytes 2359304 | tf_op jit(solution)/shard_map/ppermute | solution.py:484
  58.3 5.0 %collective-permute-start.4 = (bf16[80,256]{1,0:T(8,128)(2,1)S(1)}, bf16[80,256]{1,0:T(8,128)(2,1)S(1)}, u32[]{:S(2)}, u32[]{:S(2)}) collective-permute-start(bf16[80,256]{1,0:T(8,128)(2,1)S(1)} %shard_map.110.own), channel_id=1, source_target_pairs={{0,96},{32,0},{64,32},{96,64},{1,97},{33,1},{65,33},{97,65},{2,98}... | collective-permute-start | bytes 122888 | tf_op jit(solution)/shard_map/ppermute | solution.py:488
  60.9 4.4 %collective-permute-start.3 = (bf16[80,256]{1,0:T(8,128)(2,1)S(1)}, bf16[80,256]{1,0:T(8,128)(2,1)S(1)}, u32[]{:S(2)}, u32[]{:S(2)}) collective-permute-start(bf16[80,256]{1,0:T(8,128)(2,1)S(1)} %shard_map.110.own), channel_id=1, source_target_pairs={{0,64},{32,96},{64,0},{96,32},{1,65},{33,97},{65,1},{97,33},{2,66}... | collective-permute-start | bytes 122888 | tf_op jit(solution)/shard_map/ppermute | solution.py:488
  61.4 4.3 %collective-permute-start.2 = (bf16[80,256]{1,0:T(8,128)(2,1)S(1)}, bf16[80,256]{1,0:T(8,128)(2,1)S(1)}, u32[]{:S(2)}, u32[]{:S(2)}) collective-permute-start(bf16[80,256]{1,0:T(8,128)(2,1)S(1)} %shard_map.110.own), channel_id=1, source_target_pairs={{0,32},{32,64},{64,96},{96,0},{1,33},{33,65},{65,97},{97,1},{2,34}... | collective-permute-start | bytes 122888 | tf_op jit(solution)/shard_map/ppermute | solution.py:488
  80.1 6.6 %collective-permute-start.5 = (bf16[16,96,256]{2,1,0:T(8,128)(2,1)S(1)}, bf16[16,96,256]{2,1,0:T(8,128)(2,1)S(1)}, u32[]{:S(2)}, u32[]{:S(2)}) collective-permute-start(bf16[16,96,256]{2,1,0:T(8,128)(2,1)S(1)} %all_to_all.32.h_own.h_one), channel_id=1, source_target_pairs={{0,1},{1,0},{2,3},{3,2},{4,5},{5,4},{6,7},{7,6},{8,9},{9,8},{10,11... | collective-permute-start | bytes 2359304 | tf_op jit(solution)/shard_map/ppermute | solution.py:484
  90.6 2.5 %collective-permute-start.6 = (bf16[16,96,256]{2,1,0:T(8,128)(2,1)S(1)}, bf16[16,96,256]{2,1,0:T(8,128)(2,1)S(1)}, u32[]{:S(2)}, u32[]{:S(2)}) collective-permute-start(bf16[16,96,256]{2,1,0:T(8,128)(2,1)S(1)} %get-tuple-element.45), channel_id=1, source_target_pairs={{0,1},{1,0},{2,3},{3,2},{4,5},{5,4},{6,7},{7,6},{8,9},{9,8},{10,11... | collective-permute-start | bytes 2359304 | tf_op jit(solution)/shard_map/ppermute | solution.py:484
  110.7 2.9 %collective-permute-start.9 = (bf16[80,256]{1,0:T(8,128)(2,1)S(1)}, bf16[80,256]{1,0:T(8,128)(2,1)S(1)}, u32[]{:S(2)}, u32[]{:S(2)}) collective-permute-start(bf16[80,256]{1,0:T(8,128)(2,1)S(1)} %shard_map.116.own), channel_id=1, source_target_pairs={{0,96},{32,0},{64,32},{96,64},{1,97},{33,1},{65,33},{97,65},{2,98}... | collective-permute-start | bytes 122888 | tf_op jit(solution)/shard_map/ppermute | solution.py:488
  111.1 4.4 %collective-permute-start.8 = (bf16[80,256]{1,0:T(8,128)(2,1)S(1)}, bf16[80,256]{1,0:T(8,128)(2,1)S(1)}, u32[]{:S(2)}, u32[]{:S(2)}) collective-permute-start(bf16[80,256]{1,0:T(8,128)(2,1)S(1)} %shard_map.116.own), channel_id=1, source_target_pairs={{0,64},{32,96},{64,0},{96,32},{1,65},{33,97},{65,1},{97,33},{2,66}... | collective-permute-start | bytes 122888 | tf_op jit(solution)/shard_map/ppermute | solution.py:488
  111.9 4.1 %collective-permute-start.7 = (bf16[80,256]{1,0:T(8,128)(2,1)S(1)}, bf16[80,256]{1,0:T(8,128)(2,1)S(1)}, u32[]{:S(2)}, u32[]{:S(2)}) collective-permute-start(bf16[80,256]{1,0:T(8,128)(2,1)S(1)} %shard_map.116.own), channel_id=1, source_target_pairs={{0,32},{32,64},{64,96},{96,0},{1,33},{33,65},{65,97},{97,1},{2,34}... | collective-permute-start | bytes 122888 | tf_op jit(solution)/shard_map/ppermute | solution.py:488
  131.0 6.6 %copy-start.1 = (f32[2,264,256]{2,1,0:T(8,128)S(1)}, f32[2,264,256]{2,1,0:T(8,128)}, u32[]{:S(2)}) copy-start(f32[2,264,256]{2,1,0:T(8,128)} %obj.3) | copy-start | bytes 1622020
  131.1 6.6 %collective-permute-start.10 = (bf16[16,96,256]{2,1,0:T(8,128)(2,1)S(1)}, bf16[16,96,256]{2,1,0:T(8,128)(2,1)S(1)}, u32[]{:S(2)}, u32[]{:S(2)}) collective-permute-start(bf16[16,96,256]{2,1,0:T(8,128)(2,1)S(1)} %all_to_all.34.h_own.h_two), channel_id=1, source_target_pairs={{0,1},{1,0},{2,3},{3,2},{4,5},{5,4},{6,7},{7,6},{8,9},{9,8},{10,11... | collective-permute-start | bytes 2359304 | tf_op jit(solution)/shard_map/ppermute | solution.py:484

commit v7 on v6

--- a/solution.py
+++ b/solution.py
@@ -210,10 +210,13 @@
     out[64:80, :] = denom[...]
 
 
-def probe_update_kernel(own, one, two, three, objs, left_out, out, left_out_now):
+def probe_update_kernel(own, one, two, three, objs, *refs):
+    out, left_out_now = refs[-2:]
     total = (own[...].astype(F32) + two[...].astype(F32)) + (one[...].astype(F32) + three[...].astype(F32))
     scale = 1.0 / (total[64:80] + PROBE_REG)
-    exact = total[0:64] * jnp.concatenate([scale] * 4, axis=0) + left_out[...]
+    exact = total[0:64] * jnp.concatenate([scale] * 4, axis=0)
+    if len(refs) > 2:
+        exact = exact + refs[0][...]
     step = exact.astype(BF16)
     left_out_now[...] = exact - step.astype(F32)
 
@@ -510,7 +513,7 @@
     probe_other = swap(own)
     h_own = h_oth = lax.all_to_all(windows, ("tm", "mode"), 0, 0)
 
-    left_out = jnp.zeros((64, PS), F32)
+    left_out = ()
     for iteration in range(2):
         if iteration > 0:
             h_oth = swap(h_own)
@@ -538,9 +541,10 @@
                 meta, parts, scale, upd
             )
         h_first = h_own
-        updates, left_out = call(
-            probe_update_kernel, (arr((N_TM, 96, PS), BF16), arr((64, PS), F32)), [VM] * 6
-        )(probe_part, *others, objs, left_out)
+        updates, rest = call(
+            probe_update_kernel, (arr((N_TM, 96, PS), BF16), arr((64, PS), F32)), [VM] * (5 + iteration)
+        )(probe_part, *others, objs, *left_out)
+        left_out = (rest,)
         h_own = exchange(updates)
 
     h_oth = swap(h_own)

time: 139 us -> 139 us (level)
  no operation moved by 1% of the time
where the time goes in v7:
time: 139 us
  blocking collectives  75.4 us (54%)
  starting transfers between devices  26.8 us (19%)
  Pallas kernels  18.8 us (14%)
  waiting for transfers between devices  16 us (12%)
  between operations  1.46 us (1%)
    all_to_all x4, blocking collectives, exchange(): return lax.all_to_all(x, 'tm', 0, 0)  62.8 us
    all_to_all x1, blocking collectives, body(): h_own = h_oth = lax.all_to_all(windows, ('tm', 'mode'), 0, 0)  12.6 us
    ppermute x5, starting transfers between devices, swap(): return lax.ppermute(x, 'mode', SWAP)  12.4 us
    all_to_all x1, starting transfers between devices, exchange(): return lax.all_to_all(x, 'tm', 0, 0)  8.74 us
    pallas_call x2, Pallas kernels, position(): call(functools.partial(position_kernel, with_update), (part, part, arr((2...  7.48 us
    all_to_all x1, waiting for transfers between devices, exchange(): return lax.all_to_all(x, 'tm', 0, 0)  6.94 us
    ppermute x6, starting transfers between devices, over_tiles(): lax.ppermute(x, 'tile', [(i, (i + k) % n) for i in range(n)])  5.63 us
    ppermute x6, waiting for transfers between devices, over_tiles(): lax.ppermute(x, 'tile', [(i, (i + k) % n) for i in range(n)])  4.7 us
  transfers between devices with their start and end apart: 12, of which 9 were waited for; matrix products, arithmetic and copies ran while one was open for 0% of the time, Pallas kernels for 4%

profile of v7, /device:TPU:1, one launch (start us, length us, event | category | flops | bytes accessed | tf_op | source)
XLA Modules:
  0.0 138.5 jit_solution(4318973851697004890)
XLA Ops:
  1.3 1.8 %shard_map.104 = bf16[16,32,256]{2,1,0:T(8,128)(2,1)} custom-call(s32[2]{0:T(128)} %bitcast.11, s32[2]{0:T(128)} %row_offset.1, s32[2]{0:T(128)} %col_offset.1, s32[1,1]{1,0:T(1,128)} %bitcast.3.live_counts, f32[2,264,256]{2,1,0:T(8,128)} %obj.3), custom_call_target="tpu_custom_call" | custom-call | bytes 1048576 | tf_op jit(solution)/shard_map/pallas_call | solution.py:496
  3.1 8.7 %all-to-all-start = ((bf16[16,32,256]{2,1,0:T(8,128)(2,1)}), bf16[16,32,256]{2,1,0:T(8,128)(2,1)S(1)}, u32[]{:S(2)}, u32[]{:S(2)}) async-start(bf16[16,32,256]{2,1,0:T(8,128)(2,1)} %shard_map.104), calls=%async_computation | async-start | bytes 524288 | tf_op jit(solution)/shard_map/all_to_all | solution.py:484
  12.4 6.9 %all-to-all-done.high = bf16[16,32,256]{2,1,0:T(8,128)(2,1)S(1)} async-done(((bf16[16,32,256]{2,1,0:T(8,128)(2,1)}), bf16[16,32,256]{2,1,0:T(8,128)(2,1)S(1)}, u32[]{:S(2)}, u32[]{:S(2)}) %all-to-all-start) | async-done | bytes 262176 | tf_op jit(solution)/shard_map/all_to_all | solution.py:484
  19.3 1.1 shard_map.106
  20.4 2.1 %collective-permute-start = (f32[2,2,256,256]{3,2,1,0:T(8,128)S(1)}, f32[2,2,256,256]{3,2,1,0:T(8,128)S(1)}, u32[]{:S(2)}, u32[]{:S(2)}) collective-permute-start(f32[2,2,256,256]{3,2,1,0:T(8,128)S(1)} %copy-done), channel_id=1, source_target_pairs={{0,1},{1,0},{2,3},{3,2},{4,5},{5,4},{6,7},{7,6},{8,9},{9,8},{10,11... | collective-permute-start | bytes 3145736 | tf_op jit(solution)/shard_map/ppermute | solution.py:487
  22.5 12.6 %all_to_all.30.h_own.h_oth = bf16[32,16,256]{2,1,0:T(8,128)(2,1)S(1)} all-to-all(bf16[32,16,256]{2,1,0:T(8,128)(2,1)S(1)} %get-tuple-element.31), channel_id=1, replica_groups=mesh['tile'=4,'tm'=16,'mode'=2] {'tm','mode'}, dimensions={0} | all-to-all | bytes 524288 | tf_op jit(solution)/shard_map/all_to_all | solution.py:514
  35.1 3.7 %shard_map.107 = (bf16[16,96,256]{2,1,0:T(8,128)(2,1)S(1)}, bf16[16,96,256]{2,1,0:T(8,128)(2,1)S(1)}, f32[272,256]{1,0:T(8,128)S(1)}) custom-call(s32[16,8]{1,0:T(8,128)S(1)} %bitcast.5, bf16[1,4,256,256]{3,2,1,0:T(8,128)(2,1)S(1)} %copy-done.2, f32[2,2,256,256]{3,2,1,0:T(8,128)S(1)} %copy-done, f32[2,2,256,256]{3,2,1,0:T(8,128)S(1)} %collective-permute-done.p_oth, ...), custom_call_target="tpu_custom_call" | custom-call | flops 1073741824 | bytes 10485760 | tf_op jit(solution)/shard_map/pallas_call | solution.py:427
  39.0 1.1 shard_map.108.scale
  40.2 1.0 collective-permute-done.1.recv
  41.3 16.8 %all_to_all.31.parts = bf16[16,112,256]{2,1,0:T(8,128)(2,1)S(1)} all-to-all(bf16[16,112,256]{2,1,0:T(8,128)(2,1)S(1)} %get-tuple-element.38), channel_id=1, replica_groups=mesh['tile'=4,'tm'=16,'mode'=2] {'tm'}, dimensions={0} | all-to-all | bytes 1835008 | tf_op jit(solution)/shard_map/all_to_all | solution.py:484
  58.3 2.5 %collective-permute-start.4 = (bf16[80,256]{1,0:T(8,128)(2,1)S(1)}, bf16[80,256]{1,0:T(8,128)(2,1)S(1)}, u32[]{:S(2)}, u32[]{:S(2)}) collective-permute-start(bf16[80,256]{1,0:T(8,128)(2,1)S(1)} %shard_map.110.own), channel_id=1, source_target_pairs={{0,96},{32,0},{64,32},{96,64},{1,97},{33,1},{65,33},{97,65},{2,98}... | collective-permute-start | bytes 122888 | tf_op jit(solution)/shard_map/ppermute | solution.py:491
  62.0 1.3 shard_map.111
  63.4 1.9 %collective-permute-done.3.two = bf16[80,256]{1,0:T(8,128)(2,1)S(1)} collective-permute-done((bf16[80,256]{1,0:T(8,128)(2,1)S(1)}, bf16[80,256]{1,0:T(8,128)(2,1)S(1)}, u32[]{:S(2)}, u32[]{:S(2)}) %collective-permute-start.3) | collective-permute-done | bytes 40992 | tf_op jit(solution)/shard_map/ppermute | solution.py:491
  65.7 14.4 %all_to_all.32.h_own.h_one = bf16[16,96,256]{2,1,0:T(8,128)(2,1)S(1)} all-to-all(bf16[16,96,256]{2,1,0:T(8,128)(2,1)S(1)} %get-tuple-element.42), channel_id=1, replica_groups=mesh['tile'=4,'tm'=16,'mode'=2] {'tm'}, dimensions={0} | all-to-all | bytes 1572864 | tf_op jit(solution)/shard_map/all_to_all | solution.py:484
  80.1 4.7 %collective-permute-start.5 = (bf16[16,96,256]{2,1,0:T(8,128)(2,1)S(1)}, bf16[16,96,256]{2,1,0:T(8,128)(2,1)S(1)}, u32[]{:S(2)}, u32[]{:S(2)}) collective-permute-start(bf16[16,96,256]{2,1,0:T(8,128)(2,1)S(1)} %all_to_all.32.h_own.h_one), channel_id=1, source_target_pairs={{0,1},{1,0},{2,3},{3,2},{4,5},{5,4},{6,7},{7,6},{8,9},{9,8},{10,11... | collective-permute-start | bytes 2359304 | tf_op jit(solution)/shard_map/ppermute | solution.py:487
  84.8 1.9 %collective-permute-done.5.h_oth = bf16[16,96,256]{2,1,0:T(8,128)(2,1)S(1)} collective-permute-done((bf16[16,96,256]{2,1,0:T(8,128)(2,1)S(1)}, bf16[16,96,256]{2,1,0:T(8,128)(2,1)S(1)}, u32[]{:S(2)}, u32[]{:S(2)}) %collective-permute-start.5) | collective-permute-done | bytes 786464 | tf_op jit(solution)/shard_map/ppermute | solution.py:487
  86.8 3.8 %shard_map.113 = (bf16[16,96,256]{2,1,0:T(8,128)(2,1)S(1)}, bf16[16,96,256]{2,1,0:T(8,128)(2,1)S(1)}, f32[272,256]{1,0:T(8,128)S(1)}) custom-call(s32[16,8]{1,0:T(8,128)S(1)} %bitcast.8, bf16[1,4,256,256]{3,2,1,0:T(8,128)(2,1)S(1)} %copy-done.2, f32[2,2,256,256]{3,2,1,0:T(8,128)S(1)} %copy-done, f32[2,2,256,256]{3,2,1,0:T(8,128)S(1)} %collective-permute-done.p_oth, ...), custom_call_target="tpu_custom_call" | custom-call | flops 1073741824 | bytes 10485760 | tf_op jit(solution)/shard_map/pallas_call | solution.py:427
  91.2 1.1 shard_map.114.scale
  93.3 17.2 %all_to_all.33.parts = bf16[16,112,256]{2,1,0:T(8,128)(2,1)S(1)} all-to-all(bf16[16,112,256]{2,1,0:T(8,128)(2,1)S(1)} %get-tuple-element.48), channel_id=1, replica_groups=mesh['tile'=4,'tm'=16,'mode'=2] {'tm'}, dimensions={0} | all-to-all | bytes 1835008 | tf_op jit(solution)/shard_map/all_to_all | solution.py:484
  112.6 1.0 shard_map.117.objs
  113.6 1.9 %collective-permute-done.8.two = bf16[80,256]{1,0:T(8,128)(2,1)S(1)} collective-permute-done((bf16[80,256]{1,0:T(8,128)(2,1)S(1)}, bf16[80,256]{1,0:T(8,128)(2,1)S(1)}, u32[]{:S(2)}, u32[]{:S(2)}) %collective-permute-start.8) | collective-permute-done | bytes 40992 | tf_op jit(solution)/shard_map/ppermute | solution.py:491
  116.7 14.4 %all_to_all.34.h_own.h_two = bf16[16,96,256]{2,1,0:T(8,128)(2,1)S(1)} all-to-all(bf16[16,96,256]{2,1,0:T(8,128)(2,1)S(1)} %get-tuple-element.53), channel_id=1, replica_groups=mesh['tile'=4,'tm'=16,'mode'=2] {'tm'}, dimensions={0} | all-to-all | bytes 1572864 | tf_op jit(solution)/shard_map/all_to_all | solution.py:484
  131.0 4.7 %collective-permute-start.10 = (bf16[16,96,256]{2,1,0:T(8,128)(2,1)S(1)}, bf16[16,96,256]{2,1,0:T(8,128)(2,1)S(1)}, u32[]{:S(2)}, u32[]{:S(2)}) collective-permute-start(bf16[16,96,256]{2,1,0:T(8,128)(2,1)S(1)} %all_to_all.34.h_own.h_two), channel_id=1, source_target_pairs={{0,1},{1,0},{2,3},{3,2},{4,5},{5,4},{6,7},{7,6},{8,9},{9,8},{10,11... | collective-permute-start | bytes 2359304 | tf_op jit(solution)/shard_map/ppermute | solution.py:487
  135.8 1.2 shard_map.120
  (33 shorter events, 9.2 us)
Async XLA Ops:
  1.3 10.6 %copy-start.3 = (f32[2,256,256]{2,1,0:T(8,128)S(1)}, f32[2,256,256]{2,1,0:T(8,128)}, u32[]{:S(2)}) copy-start(f32[2,256,256]{2,1,0:T(8,128)} %amp.1) | copy-start | bytes 1572868
  1.3 10.6 %copy-start.4 = (bf16[256,256]{1,0:T(8,128)(2,1)S(1)}, bf16[256,256]{1,0:T(8,128)(2,1)}, u32[]{:S(2)}) copy-start(bf16[256,256]{1,0:T(8,128)(2,1)} %constant.5.clone.table) | copy-start | bytes 393220
  3.1 17.3 %copy-start = (f32[2,2,256,256]{3,2,1,0:T(8,128)S(1)}, f32[2,2,256,256]{3,2,1,0:T(8,128)}, u32[]{:S(2)}) copy-start(f32[2,2,256,256]{3,2,1,0:T(8,128)} %p_own.5) | copy-start | bytes 3145732
  3.1 16.2 %all-to-all-start = ((bf16[16,32,256]{2,1,0:T(8,128)(2,1)}), bf16[16,32,256]{2,1,0:T(8,128)(2,1)S(1)}, u32[]{:S(2)}, u32[]{:S(2)}) async-start(bf16[16,32,256]{2,1,0:T(8,128)(2,1)} %shard_map.104), calls=%async_computation | async-start | bytes 524288 | tf_op jit(solution)/shard_map/all_to_all | solution.py:484
  12.4 22.7 %copy-start.2 = (bf16[1,4,256,256]{3,2,1,0:T(8,128)(2,1)S(1)}, bf16[1,4,256,256]{3,2,1,0:T(8,128)(2,1)}, u32[]{:S(2)}) copy-start(bf16[1,4,256,256]{3,2,1,0:T(8,128)(2,1)} %constant.4.clone.tables) | copy-start | bytes 1572868
  20.4 14.7 %collective-permute-start = (f32[2,2,256,256]{3,2,1,0:T(8,128)S(1)}, f32[2,2,256,256]{3,2,1,0:T(8,128)S(1)}, u32[]{:S(2)}, u32[]{:S(2)}) collective-permute-start(f32[2,2,256,256]{3,2,1,0:T(8,128)S(1)} %copy-done), channel_id=1, source_target_pairs={{0,1},{1,0},{2,3},{3,2},{4,5},{5,4},{6,7},{7,6},{8,9},{9,8},{10,11... | collective-permute-start | bytes 3145736 | tf_op jit(solution)/shard_map/ppermute | solution.py:487
  38.8 2.4 %collective-permute-start.1 = (bf16[16,96,256]{2,1,0:T(8,128)(2,1)S(1)}, bf16[16,96,256]{2,1,0:T(8,128)(2,1)S(1)}, u32[]{:S(2)}, u32[]{:S(2)}) collective-permute-start(bf16[16,96,256]{2,1,0:T(8,128)(2,1)S(1)} %get-tuple-element.35), channel_id=1, source_target_pairs={{0,1},{1,0},{2,3},{3,2},{4,5},{5,4},{6,7},{7,6},{8,9},{9,8},{10,11... | collective-permute-start | bytes 2359304 | tf_op jit(solution)/shard_map/ppermute | solution.py:487
  58.3 5.0 %collective-permute-start.4 = (bf16[80,256]{1,0:T(8,128)(2,1)S(1)}, bf16[80,256]{1,0:T(8,128)(2,1)S(1)}, u32[]{:S(2)}, u32[]{:S(2)}) collective-permute-start(bf16[80,256]{1,0:T(8,128)(2,1)S(1)} %shard_map.110.own), channel_id=1, source_target_pairs={{0,96},{32,0},{64,32},{96,64},{1,97},{33,1},{65,33},{97,65},{2,98}... | collective-permute-start | bytes 122888 | tf_op jit(solution)/shard_map/ppermute | solution.py:491
  60.9 4.4 %collective-permute-start.3 = (bf16[80,256]{1,0:T(8,128)(2,1)S(1)}, bf16[80,256]{1,0:T(8,128)(2,1)S(1)}, u32[]{:S(2)}, u32[]{:S(2)}) collective-permute-start(bf16[80,256]{1,0:T(8,128)(2,1)S(1)} %shard_map.110.own), channel_id=1, source_target_pairs={{0,64},{32,96},{64,0},{96,32},{1,65},{33,97},{65,1},{97,33},{2,66}... | collective-permute-start | bytes 122888 | tf_op jit(solution)/shard_map/ppermute | solution.py:491
  61.4 4.3 %collective-permute-start.2 = (bf16[80,256]{1,0:T(8,128)(2,1)S(1)}, bf16[80,256]{1,0:T(8,128)(2,1)S(1)}, u32[]{:S(2)}, u32[]{:S(2)}) collective-permute-start(bf16[80,256]{1,0:T(8,128)(2,1)S(1)} %shard_map.110.own), channel_id=1, source_target_pairs={{0,32},{32,64},{64,96},{96,0},{1,33},{33,65},{65,97},{97,1},{2,34}... | collective-permute-start | bytes 122888 | tf_op jit(solution)/shard_map/ppermute | solution.py:491
  80.1 6.6 %collective-permute-start.5 = (bf16[16,96,256]{2,1,0:T(8,128)(2,1)S(1)}, bf16[16,96,256]{2,1,0:T(8,128)(2,1)S(1)}, u32[]{:S(2)}, u32[]{:S(2)}) collective-permute-start(bf16[16,96,256]{2,1,0:T(8,128)(2,1)S(1)} %all_to_all.32.h_own.h_one), channel_id=1, source_target_pairs={{0,1},{1,0},{2,3},{3,2},{4,5},{5,4},{6,7},{7,6},{8,9},{9,8},{10,11... | collective-permute-start | bytes 2359304 | tf_op jit(solution)/shard_map/ppermute | solution.py:487
  90.6 2.5 %collective-permute-start.6 = (bf16[16,96,256]{2,1,0:T(8,128)(2,1)S(1)}, bf16[16,96,256]{2,1,0:T(8,128)(2,1)S(1)}, u32[]{:S(2)}, u32[]{:S(2)}) collective-permute-start(bf16[16,96,256]{2,1,0:T(8,128)(2,1)S(1)} %get-tuple-element.45), channel_id=1, source_target_pairs={{0,1},{1,0},{2,3},{3,2},{4,5},{5,4},{6,7},{7,6},{8,9},{9,8},{10,11... | collective-permute-start | bytes 2359304 | tf_op jit(solution)/shard_map/ppermute | solution.py:487
  110.7 2.9 %collective-permute-start.9 = (bf16[80,256]{1,0:T(8,128)(2,1)S(1)}, bf16[80,256]{1,0:T(8,128)(2,1)S(1)}, u32[]{:S(2)}, u32[]{:S(2)}) collective-permute-start(bf16[80,256]{1,0:T(8,128)(2,1)S(1)} %shard_map.116.own), channel_id=1, source_target_pairs={{0,96},{32,0},{64,32},{96,64},{1,97},{33,1},{65,33},{97,65},{2,98}... | collective-permute-start | bytes 122888 | tf_op jit(solution)/shard_map/ppermute | solution.py:491
  111.1 4.4 %collective-permute-start.8 = (bf16[80,256]{1,0:T(8,128)(2,1)S(1)}, bf16[80,256]{1,0:T(8,128)(2,1)S(1)}, u32[]{:S(2)}, u32[]{:S(2)}) collective-permute-start(bf16[80,256]{1,0:T(8,128)(2,1)S(1)} %shard_map.116.own), channel_id=1, source_target_pairs={{0,64},{32,96},{64,0},{96,32},{1,65},{33,97},{65,1},{97,33},{2,66}... | collective-permute-start | bytes 122888 | tf_op jit(solution)/shard_map/ppermute | solution.py:491
  111.8 4.1 %collective-permute-start.7 = (bf16[80,256]{1,0:T(8,128)(2,1)S(1)}, bf16[80,256]{1,0:T(8,128)(2,1)S(1)}, u32[]{:S(2)}, u32[]{:S(2)}) collective-permute-start(bf16[80,256]{1,0:T(8,128)(2,1)S(1)} %shard_map.116.own), channel_id=1, source_target_pairs={{0,32},{32,64},{64,96},{96,0},{1,33},{33,65},{65,97},{97,1},{2,34}... | collective-permute-start | bytes 122888 | tf_op jit(solution)/shard_map/ppermute | solution.py:491
  131.0 6.6 %copy-start.1 = (f32[2,264,256]{2,1,0:T(8,128)S(1)}, f32[2,264,256]{2,1,0:T(8,128)}, u32[]{:S(2)}) copy-start(f32[2,264,256]{2,1,0:T(8,128)} %obj.3) | copy-start | bytes 1622020
  131.0 6.6 %collective-permute-start.10 = (bf16[16,96,256]{2,1,0:T(8,128)(2,1)S(1)}, bf16[16,96,256]{2,1,0:T(8,128)(2,1)S(1)}, u32[]{:S(2)}, u32[]{:S(2)}) collective-permute-start(bf16[16,96,256]{2,1,0:T(8,128)(2,1)S(1)} %all_to_all.34.h_own.h_two), channel_id=1, source_target_pairs={{0,1},{1,0},{2,3},{3,2},{4,5},{5,4},{6,7},{7,6},{8,9},{9,8},{10,11... | collective-permute-start | bytes 2359304 | tf_op jit(solution)/shard_map/ppermute | solution.py:487
